TPU v7x, 256 devices: a whole 4x4x8 slice. The times are simulated.
256 devices in a mesh: dp: 128 (over z, x, y), shard: 2 (over core).
Axes of the slice: x: 4, y: 4, z: 8, core: 2. Of those that a mesh axis runs over, the one named last changes fastest.
Arguments:
- features: bfloat16 [32768, 512], P(('dp', 'shard')), may hold values from -1.5 to 1.5
- norm_gain: float32 [512], replicated, may hold values from 0.25 to 1.75
- w_in: bfloat16 [512, 512], replicated, may hold values from -0.25 to 0.25
- w_out: bfloat16 [512, 512], replicated, may hold values from -1 to 1
- cotangent: bfloat16 [32768, 512], P(('dp', 'shard')), may hold values from -6 to 6
- positions: bfloat16 [3, 32768], P(None, ('dp', 'shard')), may hold values from 0 to 1
- crystal_of_atom: int32 [32768], P(('dp', 'shard')), may hold values from 0 to 7
- atom_owner: int32 [32768, 1], P(('dp', 'shard')), may hold values from 0 to 127; in each aligned block of 128 rows (0 to 127, 128 to 255, ...) at most 2 rows name the same one
- k_index: int32 [3, 131072], P(None, 'dp'), may hold values from -4 to 4
- k_crystal: int32 [131072], P('dp'), may hold values from 0 to 7
- damping: float32 [512], replicated, may hold values from 0.005 to 0.2
Outputs:
- updated: bfloat16 [32768, 512], P(('dp', 'shard'))
- grad_w_in: float32 [512, 512], replicated
- grad_w_out: float32 [512, 512], replicated
Inputs may be any that keep to these rules, and one draw needn't show every extreme that they name: `atom_owner`: among the rows of one device, at most 2 atoms name the same packing group, a bound that some block reaches.
All inputs are finite; a program needn't handle non-finite values.
Results may differ from a plain program's by a relative error of at most 0.015.
Values may be sent and summed in bfloat16 or wider, within the bound.
No kernel may reach another device: no remote copies, remote signals or barrier semaphores. Data moves between devices by JAX's collectives and lax.ppermute only.
A program may use at most 64 MiB of HBM per device.

v0:
```python
import math

import jax
import jax.numpy as jnp
from jax import lax
from jax.sharding import PartitionSpec as P

CRY_DEV = 8


def phase_matrix(k_float, k_group, coords, crystal_ids):
    theta = (
        2.0
        * math.pi
        * (
            k_float[0][:, None] * coords[0][None, :]
            + k_float[1][:, None] * coords[1][None, :]
            + k_float[2][:, None] * coords[2][None, :]
        )
    )
    matched = k_group[:, None] == crystal_ids[None, :]
    cosine = jnp.where(matched, jnp.cos(theta), 0.0).astype(jnp.bfloat16)
    sine = jnp.where(matched, jnp.sin(theta), 0.0).astype(jnp.bfloat16)
    return jnp.concatenate([cosine, sine], axis=0)


def project_back(phase, scaled, scale_m):
    return (
        scale_m
        * lax.dot_general(
            phase, scaled, (((0,), (0,)), ((), ())), preferred_element_type=jnp.float32
        )
    ).astype(jnp.bfloat16)


def filter_rows(k_float, damping):
    ksq = k_float[0] * k_float[0] + k_float[1] * k_float[1] + k_float[2] * k_float[2]
    filter_k = jnp.exp(-ksq[:, None] * damping[None, :]) / (1.0 + ksq[:, None])
    return jnp.concatenate([filter_k, filter_k], axis=0)


def local(
    features,
    norm_gain,
    w_in,
    w_out,
    cotangent,
    positions,
    crystal_of_atom,
    atom_owner,
    k_index,
    k_crystal,
    damping,
):
    rows = features.shape[0]
    width = features.shape[1]
    groups = lax.axis_size("dp")
    members = lax.axis_size("shard")
    capacity = 2 * rows // groups
    slot_total = groups * capacity
    kcount = k_index.shape[1]
    hidden = features.astype(jnp.float32)
    normed = (
        hidden
        * lax.rsqrt(jnp.mean(hidden * hidden, axis=-1, keepdims=True) + 1e-06)
        * norm_gain[None, :]
    ).astype(jnp.bfloat16)
    owner_group = atom_owner[:, 0]
    owner_hits = (owner_group[:, None] == jnp.arange(groups, dtype=jnp.int32)[None, :]).astype(
        jnp.int32
    )
    slot_rank = jnp.sum((jnp.cumsum(owner_hits, axis=0) - owner_hits) * owner_hits, axis=1)
    slot_index = owner_group * capacity + slot_rank

    def to_slots(values):
        placed = jnp.zeros((slot_total, width), jnp.bfloat16).at[slot_index].set(values)
        return placed.reshape(groups, capacity, width)

    meta_rows = jnp.concatenate([positions, crystal_of_atom.astype(jnp.bfloat16)[None, :]], axis=0)
    meta_send = jnp.zeros((4, slot_total), jnp.bfloat16).at[:, slot_index].set(meta_rows)
    meta_send = meta_send.reshape(4, groups, capacity).transpose(1, 0, 2)
    recv_x, recv_meta = (
        lax.all_to_all(to_slots(normed), "dp", split_axis=0, concat_axis=0, tiled=True),
        lax.all_to_all(meta_send, "dp", split_axis=0, concat_axis=0, tiled=True),
    )
    slot_x = recv_x.reshape(slot_total, width)
    slot_meta = recv_meta.transpose(1, 0, 2).reshape(4, slot_total)
    k_float = k_index.astype(jnp.float32)
    k_group = k_crystal.astype(jnp.float32)
    scale_s = (slot_total * 2 / CRY_DEV) ** (-0.5)
    scale_m = (kcount / CRY_DEV) ** (-0.5)
    down = jnp.dot(slot_x, w_in, preferred_element_type=jnp.float32).astype(jnp.bfloat16)
    filter_two = filter_rows(k_float, damping)
    phase = phase_matrix(
        k_float, k_group, slot_meta[:3].astype(jnp.float32), slot_meta[3].astype(jnp.float32)
    )
    structure = lax.psum(
        jnp.dot(phase, down, preferred_element_type=jnp.float32).astype(jnp.bfloat16), "shard"
    ).astype(jnp.float32)
    scaled = (structure * filter_two * scale_s).astype(jnp.bfloat16)
    message = project_back(phase, scaled, scale_m)
    change = jnp.dot(message, w_out, preferred_element_type=jnp.float32).astype(jnp.bfloat16)
    change_back = lax.all_to_all(
        change.reshape(groups, capacity, width), "dp", split_axis=0, concat_axis=0, tiled=True
    )
    change_rows = change_back.reshape(slot_total, width)[slot_index]
    updated = (hidden + change_rows.astype(jnp.float32)).astype(jnp.bfloat16)
    recv_g = lax.all_to_all(to_slots(cotangent), "dp", split_axis=0, concat_axis=0, tiled=True)
    slot_grad = recv_g.reshape(slot_total, width)
    grad_message = lax.dot_general(
        slot_grad, w_out, (((1,), (1,)), ((), ())), preferred_element_type=jnp.float32
    ).astype(jnp.bfloat16)
    back = lax.psum(
        jnp.dot(phase, grad_message, preferred_element_type=jnp.float32).astype(jnp.bfloat16),
        "shard",
    ).astype(jnp.float32)
    back_scaled = (back * filter_two * scale_s).astype(jnp.bfloat16)
    grad_down = project_back(phase, back_scaled, scale_m)
    norm_factor = (rows * groups * members) ** (-0.5)
    local_out = (
        lax.dot_general(
            message, slot_grad, (((0,), (0,)), ((), ())), preferred_element_type=jnp.float32
        )
        * norm_factor
    )
    grad_w_out = lax.psum(local_out, ("dp", "shard"))
    local_in = (
        lax.dot_general(
            slot_x, grad_down, (((0,), (0,)), ((), ())), preferred_element_type=jnp.float32
        )
        * norm_factor
    )
    grad_w_in = lax.psum(local_in, ("dp", "shard"))
    return (updated, grad_w_in, grad_w_out)


def solution(mesh):
    in_specs = (
        P(("dp", "shard"), None),
        P(),
        P(),
        P(),
        P(("dp", "shard"), None),
        P(None, ("dp", "shard")),
        P(("dp", "shard")),
        P(("dp", "shard"), None),
        P(None, "dp"),
        P("dp"),
        P(),
    )
    out_specs = (P(("dp", "shard"), None), P(), P())
    return jax.shard_map(local, mesh=mesh, in_specs=in_specs, out_specs=out_specs, check_vma=False)
```

profile of v0, /device:TPU:1, one launch (start us, length us, event | category | flops | bytes accessed | tf_op | source)
XLA Modules:
  0.0 400.7 jit_solution(9546135007991204523)
XLA Ops:
  7.2 0.8 fusion.38
  8.0 0.2 reduce_window_sum.11
  8.2 0.8 select_reduce_fusion
  9.0 0.7 fusion.41
  9.7 0.7 convert_bitcast_fusion
  10.3 0.7 maximum_bitcast_fusion
  11.0 0.1 copy.17
  11.2 1.5 scatter_custom_fusion
  12.6 16.3 %all-to-all-start = ((bf16[128,4,2]{1,2,0:T(2,128)(2,1)}), bf16[128,4,2]{1,2,0:T(2,128)(2,1)S(1)}, u32[]{:S(2)}, u32[]{:S(2)}) async-start(bf16[128,4,2]{1,2,0:T(2,128)(2,1)} %bitcast.6), calls=%async_computation | async-start | bytes 131072 | tf_op jit(solution)/shard_map/all_to_all | solution.py:84
  29.0 0.7 convert_element_type.83
  29.7 1.0 fusion.26
  30.7 1.5 scatter_custom_fusion.2
  32.3 0.8 reshape.95
  33.1 6.6 %all-to-all-done = bf16[128,4,2]{1,2,0:T(2,128)(2,1)S(1)} async-done(((bf16[128,4,2]{1,2,0:T(2,128)(2,1)}), bf16[128,4,2]{1,2,0:T(2,128)(2,1)S(1)}, u32[]{:S(2)}, u32[]{:S(2)}) %all-to-all-start) | async-done | bytes 2080 | tf_op jit(solution)/shard_map/all_to_all | solution.py:84
  39.7 6.6 %all-to-all-start.3 = ((bf16[128,2,512]{2,1,0:T(2,128)(2,1)}), bf16[128,2,512]{2,1,0:T(2,128)(2,1)S(1)}, u32[]{:S(2)}, u32[]{:S(2)}) async-start(bf16[128,2,512]{2,1,0:T(2,128)(2,1)} %reshape.95), calls=%async_computation.3 | async-start | bytes 524288 | tf_op jit(solution)/shard_map/all_to_all | solution.py:108
  46.3 0.7 convert_element_type.78
  47.0 1.3 scatter_custom_fusion.1
  48.3 0.8 reshape.91
  49.2 0.8 slice_reduce_fusion.2
  50.0 0.1 mul.158
  50.1 0.1 mul.163
  50.2 0.1 mul.168
  50.4 0.3 convert_reduce_fusion
  50.7 0.1 reshape.97
  50.8 7.8 %all-to-all-done.3 = bf16[128,2,512]{2,1,0:T(2,128)(2,1)S(1)} async-done(((bf16[128,2,512]{2,1,0:T(2,128)(2,1)}), bf16[128,2,512]{2,1,0:T(2,128)(2,1)S(1)}, u32[]{:S(2)}, u32[]{:S(2)}) %all-to-all-start.3) | async-done | bytes 262176 | tf_op jit(solution)/shard_map/all_to_all | solution.py:108
  58.6 7.1 %all-to-all-start.1 = ((bf16[128,2,512]{2,1,0:T(2,128)(2,1)}), bf16[128,2,512]{2,1,0:T(2,128)(2,1)S(1)}, u32[]{:S(2)}, u32[]{:S(2)}) async-start(bf16[128,2,512]{2,1,0:T(2,128)(2,1)} %reshape.91), calls=%async_computation.1 | async-start | bytes 524288 | tf_op jit(solution)/shard_map/all_to_all | solution.py:83
  65.7 0.2 all-reduce.7.cloned.1.call-start
  65.9 5.8 %fusion.24 = (bf16[1024,256]{1,0:T(8,128)(2,1)S(1)}, bf16[1024,256]{1,0:T(8,128)(2,1)S(1)}) fusion(f32[256]{0:T(256)S(1)} %mul.168, f32[1024]{0:T(1024)S(1)} %bitcast.31, f32[256]{0:T(256)S(1)} %mul.163, f32[1024]{0:T(1024)S(1)} %bitcast.33, f32[256]{0:T(256)S(1)} %mul.158, f32[1024]{0:T(1024)S(1)} %bitcast.29, f32[256]{0:T(256)S(1)} %reshape.97, ...), kind=kLoop, calls=%fused_computation.27 | loop fusion | flops 2883584 | bytes 1069056 | tf_op jit(solution)/shard_map/convert_element_type | solution.py:22
  71.8 0.1 reshape.96
  71.9 2.3 convolution_convert_fusion
  74.3 4.1 %all-to-all-done.1 = bf16[128,2,512]{2,1,0:T(2,128)(2,1)S(1)} async-done(((bf16[128,2,512]{2,1,0:T(2,128)(2,1)}), bf16[128,2,512]{2,1,0:T(2,128)(2,1)S(1)}, u32[]{:S(2)}, u32[]{:S(2)}) %all-to-all-start.1) | async-done | bytes 262176 | tf_op jit(solution)/shard_map/all_to_all | solution.py:83
  78.5 2.3 convolution_convert_fusion.1
  80.8 0.6 copy-done.5
  81.4 0.4 exponential_divide_fusion
  81.9 38.2 %all-reduce.7.cloned.1.call-done = (bf16[2048,512]{1,0:T(8,128)(2,1)}, bf16[2048,512]{1,0:T(8,128)(2,1)}) async-done(((bf16[2048,512]{1,0:T(8,128)(2,1)}, bf16[2048,512]{1,0:T(8,128)(2,1)}), (bf16[2048,512]{1,0:T(8,128)(2,1)}, bf16[2048,512]{1,0:T(8,128)(2,1)})) %all-reduce.7.cloned.1.call-update) | async-done | bytes 4194320 | tf_op jit(solution)/shard_map/psum | solution.py:97
  120.1 4.0 %convolution_multiply_fusion.1 = f32[512,512]{1,0:T(8,128)} fusion(bf16[256,512]{1,0:T(8,128)(2,1)S(1)} %reshape.92, f32[1024,512]{1,0:T(8,128)S(1)} %exponential_divide_fusion, bf16[2048,512]{1,0:T(8,128)(2,1)} %get-tuple-element.9, bf16[1024,256]{1,0:T(8,128)(2,1)} %copy-done.4, bf16[1024,256]{1,0:T(8,128)(2,1)} %copy-done.3), kind=kOutput, calls=%fused_computation.17 | convolution fusion | flops 678952960 | bytes 6553600 | tf_op jit(solution)/shard_map/dot_general | solution.py:128
  124.1 2.8 fusion.21
  126.9 1.3 convolution_multiply_fusion
  128.2 0.3 convolution_convert_fusion.3
  128.5 0.8 reshape.93
  129.3 13.6 %all-to-all-start.2 = ((bf16[128,2,512]{2,1,0:T(2,128)(2,1)}), bf16[128,2,512]{2,1,0:T(2,128)(2,1)S(1)}, u32[]{:S(2)}, u32[]{:S(2)}) async-start(bf16[128,2,512]{2,1,0:T(2,128)(2,1)} %reshape.93), calls=%async_computation.2 | async-start | bytes 524288 | tf_op jit(solution)/shard_map/all_to_all | solution.py:103
  142.9 14.9 %all-to-all-done.2 = bf16[128,2,512]{2,1,0:T(2,128)(2,1)S(1)} async-done(((bf16[128,2,512]{2,1,0:T(2,128)(2,1)}), bf16[128,2,512]{2,1,0:T(2,128)(2,1)S(1)}, u32[]{:S(2)}, u32[]{:S(2)}) %all-to-all-start.2) | async-done | bytes 262176 | tf_op jit(solution)/shard_map/all_to_all | solution.py:103
  157.8 0.1 reshape.94
  157.9 0.8 gather_fusion
  158.8 0.7 fusion.29
  159.5 231.1 %all-reduce.5.cloned.1.call-done = (f32[512,512]{1,0:T(8,128)}, f32[512,512]{1,0:T(8,128)}) async-done(((f32[512,512]{1,0:T(8,128)}, f32[512,512]{1,0:T(8,128)}), (f32[512,512]{1,0:T(8,128)}, f32[512,512]{1,0:T(8,128)})) %all-reduce.5.cloned.1.call-update) | async-done | bytes 2097168 | tf_op jit(solution)/shard_map/psum | solution.py:133
  390.6 2.4 copy.22
  392.9 1.0 copy.23
  (22 shorter events, 0.3 us)
Async XLA Ops:
  7.2 64.7 %copy-start = (bf16[512,512]{1,0:T(8,128)(2,1)S(1)}, bf16[512,512]{1,0:T(8,128)(2,1)}, u32[]{:S(2)}) copy-start(bf16[512,512]{1,0:T(8,128)(2,1)} %param.14) | copy-start | bytes 1572868
  7.2 39.8 %copy-start.1 = (bf16[128,512]{1,0:T(8,128)(2,1)S(1)}, bf16[128,512]{1,0:T(8,128)(2,1)}, u32[]{:S(2)}) copy-start(bf16[128,512]{1,0:T(8,128)(2,1)} %param.11) | copy-start | bytes 393220
  12.6 27.0 %all-to-all-start = ((bf16[128,4,2]{1,2,0:T(2,128)(2,1)}), bf16[128,4,2]{1,2,0:T(2,128)(2,1)S(1)}, u32[]{:S(2)}, u32[]{:S(2)}) async-start(bf16[128,4,2]{1,2,0:T(2,128)(2,1)} %bitcast.6), calls=%async_computation | async-start | bytes 131072 | tf_op jit(solution)/shard_map/all_to_all | solution.py:84
  39.7 19.0 %all-to-all-start.3 = ((bf16[128,2,512]{2,1,0:T(2,128)(2,1)}), bf16[128,2,512]{2,1,0:T(2,128)(2,1)S(1)}, u32[]{:S(2)}, u32[]{:S(2)}) async-start(bf16[128,2,512]{2,1,0:T(2,128)(2,1)} %reshape.95), calls=%async_computation.3 | async-start | bytes 524288 | tf_op jit(solution)/shard_map/all_to_all | solution.py:108
  58.6 19.7 %all-to-all-start.1 = ((bf16[128,2,512]{2,1,0:T(2,128)(2,1)}), bf16[128,2,512]{2,1,0:T(2,128)(2,1)S(1)}, u32[]{:S(2)}, u32[]{:S(2)}) async-start(bf16[128,2,512]{2,1,0:T(2,128)(2,1)} %reshape.91), calls=%async_computation.1 | async-start | bytes 524288 | tf_op jit(solution)/shard_map/all_to_all | solution.py:83
  65.7 54.4 %all-reduce.7.cloned.1.call-start = ((), (), s32[]{:S(2)}) async-start(), calls=%async_computation.5 | async-start | bytes 8388608 | tf_op jit(solution)/shard_map/psum | solution.py:97
  71.8 6.7 %copy-start.3 = (bf16[1024,256]{1,0:T(8,128)(2,1)}, bf16[1024,256]{1,0:T(8,128)(2,1)S(1)}, u32[]{:S(2)}) copy-start(bf16[1024,256]{1,0:T(8,128)(2,1)S(1)} %get-tuple-element.10) | copy-start | bytes 1572868
  71.8 6.7 %copy-start.4 = (bf16[1024,256]{1,0:T(8,128)(2,1)}, bf16[1024,256]{1,0:T(8,128)(2,1)S(1)}, u32[]{:S(2)}) copy-start(bf16[1024,256]{1,0:T(8,128)(2,1)S(1)} %get-tuple-element.11) | copy-start | bytes 1572868
  71.9 6.5 %copy-start.6 = (bf16[512,512]{1,0:T(8,128)(2,1)S(1)}, bf16[512,512]{1,0:T(8,128)(2,1)}, u32[]{:S(2)}) copy-start(bf16[512,512]{1,0:T(8,128)(2,1)} %param.13) | copy-start | bytes 1572868
  80.8 0.7 copy-start.5
  80.8 309.8 %all-reduce.5.cloned.1.call-start = ((), (), s32[]{:S(2)}) async-start(), calls=%async_computation.4 | async-start | bytes 4194304 | tf_op jit(solution)/shard_map/psum | solution.py:133
  129.3 28.5 %all-to-all-start.2 = ((bf16[128,2,512]{2,1,0:T(2,128)(2,1)}), bf16[128,2,512]{2,1,0:T(2,128)(2,1)S(1)}, u32[]{:S(2)}, u32[]{:S(2)}) async-start(bf16[128,2,512]{2,1,0:T(2,128)(2,1)} %reshape.93), calls=%async_computation.2 | async-start | bytes 524288 | tf_op jit(solution)/shard_map/all_to_all | solution.py:103
  390.6 2.4 copy-start.2
Sparse Core Ops, SparseCore 0:
  80.9 39.1 all-reduce.6
  128.3 262.2 all-reduce.4
where the time goes:
time: 402 us; the launch traced here: 401 us
  waiting for transfers between devices  303 us (75%)
  starting transfers between devices  43.8 us (11%)
  other arithmetic  14.9 us (4%)
  between operations  14.3 us (4%)
  matrix products  13 us (3%)
  local copies, waits for them, and re-layouts  12 us (3%)
    psum x1, waiting for transfers between devices, local(): grad_w_in = lax.psum(local_in, ('dp', 'shard'))  231 us
    psum x1, waiting for transfers between devices, local(): lax.psum(jnp.dot(phase, down, preferred_element_type=jnp.float32).astype(...  38.2 us
    all_to_all x1, starting transfers between devices, local(): lax.all_to_all(meta_send, 'dp', split_axis=0, concat_axis=0, tiled=True)  16.3 us
    all_to_all x1, waiting for transfers between devices, local(): lax.all_to_all(change.reshape(groups, capacity, width), 'dp', split_axis=...  14.9 us
    all_to_all x1, starting transfers between devices, local(): lax.all_to_all(change.reshape(groups, capacity, width), 'dp', split_axis=...  13.6 us
  transfers between devices with their start and end apart: 6, of which 6 were waited for; matrix products, arithmetic and copies ran while one was open for 5% of the time, Pallas kernels for 0%

commit v1 on v0

v1 whole, which is shorter than its diff:
```python
import functools
import math

import jax
import jax.numpy as jnp
from jax import lax
from jax.experimental import pallas as pl
from jax.experimental.pallas import tpu as pltpu
from jax.sharding import PartitionSpec as P

CRY_DEV = 8
BF = jnp.bfloat16
F32 = jnp.float32
VMEM_LIMIT = 48 * 1024 * 1024
META = 128

COS_POLY = (
    1.0,
    -19.73920440673828,
    64.93911743164062,
    -85.45014190673828,
    60.16762924194336,
    -25.967599868774414,
    6.528658390045166,
)
SIN_POLY = (
    6.283185005187988,
    -41.341590881347656,
    81.59994506835938,
    -76.61447143554688,
    41.3428840637207,
    -12.471243858337402,
)

VM = pl.BlockSpec(memory_space=pltpu.VMEM)
SM = pl.BlockSpec(memory_space=pltpu.SMEM)


def call(body, out_shape, inputs, scratch=(), specs=None):
    return pl.pallas_call(
        body,
        out_shape=out_shape,
        in_specs=specs if specs is not None else [VM] * len(inputs),
        out_specs=jax.tree.map(lambda _: VM, out_shape),
        scratch_shapes=list(scratch),
        compiler_params=pltpu.CompilerParams(vmem_limit_bytes=VMEM_LIMIT),
    )(*inputs)


def dot(a, b, ca, cb):
    return lax.dot_general(a, b, (((ca,), (cb,)), ((), ())), preferred_element_type=F32)


def prep_kernel(feat_ref, gain_ref, cot_ref, meta_ref, col_ref, row_ref, out_ref):
    rows = feat_ref.shape[0]
    peers = out_ref.shape[1]
    width = feat_ref.shape[1]
    hidden = feat_ref[...].astype(F32)
    normed = (
        hidden
        * lax.rsqrt(jnp.mean(hidden * hidden, axis=-1, keepdims=True) + 1e-06)
        * gain_ref[...]
    ).astype(BF)
    owner = row_ref[...]
    first = lax.broadcasted_iota(jnp.int32, (rows, rows), 0)
    second = lax.broadcasted_iota(jnp.int32, (rows, rows), 1)
    earlier = (col_ref[...] == owner) & (first < second)
    rank = jnp.sum(jnp.where(earlier, 1.0, 0.0), axis=0, keepdims=True)
    peer = lax.broadcasted_iota(jnp.int32, (peers, rows), 0)
    for r in range(2):
        place = jnp.where((owner == peer) & (rank == float(r)), 1.0, 0.0).astype(BF)
        out_ref[r, :, 0:width] = dot(place, normed, 1, 0).astype(BF)
        out_ref[r, :, width : 2 * width] = dot(place, cot_ref[...], 1, 0).astype(BF)
        out_ref[r, :, 2 * width : 2 * width + META] = dot(place, meta_ref[...], 1, 1).astype(BF)


def static_kernel(shard_ref, k_ref, damp_ref, w_in_ref, kmat_ref, filt_ref, w_in_t_ref, scale_s):
    half = filt_ref.shape[0]
    start = pl.multiple_of(shard_ref[0] * half, half)
    kf = k_ref[...].astype(F32)
    kmat_ref[...] = jnp.zeros(kmat_ref.shape, BF)
    kmat_ref[0:16, :] = jnp.concatenate([kf, jnp.zeros((13, kf.shape[1]), F32)], axis=0).astype(BF)
    ksq = kf[0:1] * kf[0:1] + kf[1:2] * kf[1:2] + kf[2:3] * kf[2:3]
    damp = damp_ref[pl.ds(start, half), :]
    scale = scale_s / (1.0 + ksq)
    step = 32

    def rows(i, carry):
        at = pl.multiple_of(i * step, step)
        d = damp_ref[pl.ds(pl.multiple_of(start + at, step), step), :]
        filt_ref[pl.ds(at, step), :] = jnp.exp(-(d * ksq)) * scale
        return carry

    lax.fori_loop(0, half // step, rows, 0)
    w_in_t_ref[...] = w_in_ref[:, pl.ds(start, half)].T


def main_kernel(
    shard_ref, own_ref, oth_ref, kmat_ref, kc_ref, filt_ref, w_in_t_ref, w_out_ref,
    msg_ref, grad_ref,
    turn_ref, phase_ref, stack_ref, scaled_ref, scale_m,
):
    slots = own_ref.shape[0]
    width = w_out_ref.shape[1]
    half = w_in_t_ref.shape[0]
    kcount = kc_ref.shape[1]
    start = pl.multiple_of(shard_ref[0] * half, half)
    w_out_half = w_out_ref[pl.ds(start, half), :]
    tile_rows, tile_cols = 16, 512
    for m, ref in enumerate((own_ref, oth_ref)):
        cols = slice(m * slots, (m + 1) * slots)
        turn_ref[cols, :] = dot(ref[:, 2 * width :], kmat_ref[...], 1, 0)
        stack_ref[0:half, cols] = dot(w_in_t_ref[...], ref[:, 0:width], 1, 1).astype(BF)
        stack_ref[half:, cols] = dot(w_out_half, ref[:, width : 2 * width], 1, 1).astype(BF)

        def tile(i, carry):
            at = pl.multiple_of(i * tile_rows, tile_rows)
            dst = pl.ds(pl.multiple_of(m * slots + at, tile_rows), tile_rows)
            crystal = ref[pl.ds(at, tile_rows), 2 * width :].astype(F32)[:, 3:4]
            for j in range(kcount // tile_cols):
                span = slice(j * tile_cols, (j + 1) * tile_cols)
                turn = turn_ref[dst, span]
                rest = turn - jnp.floor(turn + 0.5)
                square = rest * rest
                cosine = jnp.full(square.shape, COS_POLY[-1], F32)
                for c in COS_POLY[-2::-1]:
                    cosine = cosine * square + c
                sine = jnp.full(square.shape, SIN_POLY[-1], F32)
                for c in SIN_POLY[-2::-1]:
                    sine = sine * square + c
                matched = crystal == kc_ref[:, span]
                phase_ref[dst, span] = jnp.where(matched, cosine, 0.0).astype(BF)
                phase_ref[dst, kcount + j * tile_cols : kcount + (j + 1) * tile_cols] = jnp.where(
                    matched, sine * rest, 0.0
                ).astype(BF)
            return carry

        lax.fori_loop(0, slots // tile_rows, tile, 0)
    block = 512
    for j in range(2 * kcount // block):
        span = slice(j * block, (j + 1) * block)
        lo = (j * block) % kcount
        filt = filt_ref[:, lo : lo + block]
        for part in range(2):
            rows = slice(part * half, (part + 1) * half)
            structure = dot(stack_ref[rows, :], phase_ref[:, span], 1, 0)
            scaled_ref[rows, span] = (structure * filt).astype(BF)
    for part, first in ((0, width), (1, 0)):
        rows = slice(part * half, (part + 1) * half)
        back = (scale_m * dot(scaled_ref[rows, :], phase_ref[...], 1, 1)).astype(BF)
        if part == 0:
            msg_ref[...] = back
        total = dot(back[:, 0:slots], own_ref[:, first : first + width], 1, 0)
        total += dot(back[:, slots:], oth_ref[:, first : first + width], 1, 0)
        grad_ref[rows, :] = total.astype(BF)


def change_kernel(shard_ref, msg_ref, got_ref, w_out_ref, grad_ref, out_ref):
    half = msg_ref.shape[0]
    slots = msg_ref.shape[1]
    rows = out_ref.shape[1]
    mine = pl.multiple_of(shard_ref[0] * half, half)
    other = pl.multiple_of((1 - shard_ref[0]) * half, half)
    change = dot(msg_ref[...], w_out_ref[pl.ds(mine, half), :], 0, 0)
    change += dot(got_ref[...], w_out_ref[pl.ds(other, half), :], 0, 0)
    change = change.astype(BF)
    for r in range(slots // rows):
        out_ref[r] = change[r * rows : (r + 1) * rows]
    for r in range(grad_ref.shape[0] // rows):
        out_ref[slots // rows + r] = grad_ref[r * rows : (r + 1) * rows]


def sum_kernel(recv_ref, out_ref, norm_factor):
    for j in range(out_ref.shape[0]):
        total = jnp.sum(recv_ref[2 + j].astype(F32), axis=0, keepdims=True) * norm_factor
        out_ref[j] = jnp.broadcast_to(total.astype(BF), out_ref.shape[1:])


def update_kernel(feat_ref, recv_ref, col_ref, row_ref, out_ref):
    rows = feat_ref.shape[0]
    peers = recv_ref.shape[1]
    owner = col_ref[...]
    first = lax.broadcasted_iota(jnp.int32, (rows, rows), 0)
    second = lax.broadcasted_iota(jnp.int32, (rows, rows), 1)
    earlier = (owner == row_ref[...]) & (second < first)
    rank = jnp.sum(jnp.where(earlier, 1.0, 0.0), axis=1, keepdims=True)
    peer = lax.broadcasted_iota(jnp.int32, (rows, peers), 1)
    total = feat_ref[...].astype(F32)
    for r in range(2):
        pick = jnp.where((owner == peer) & (rank == float(r)), 1.0, 0.0).astype(BF)
        total += dot(pick, recv_ref[r], 1, 0)
    out_ref[...] = total.astype(BF)


def final_kernel(shard_ref, own_ref, oth_ref, grad_in_ref, grad_out_ref):
    half = own_ref.shape[1] * 2
    for ref, member in ((own_ref, shard_ref[0]), (oth_ref, 1 - shard_ref[0])):
        start = pl.multiple_of(member * half, half)
        out = jnp.concatenate([ref[0], ref[1]], axis=0).astype(F32)
        grad_out_ref[pl.ds(start, half), :] = out
        into = jnp.concatenate([ref[2], ref[3]], axis=0).astype(F32)
        grad_in_ref[:, pl.ds(start, half)] = into.T


def local(
    features,
    norm_gain,
    w_in,
    w_out,
    cotangent,
    positions,
    crystal_of_atom,
    atom_owner,
    k_index,
    k_crystal,
    damping,
):
    rows, width = features.shape
    groups = lax.axis_size("dp")
    members = lax.axis_size("shard")
    capacity = 2 * rows // groups
    slots = groups * capacity
    half = width // members
    kcount = k_index.shape[1]
    scale_s = (slots * members / CRY_DEV) ** (-0.5)
    scale_m = (kcount / CRY_DEV) ** (-0.5)
    norm_factor = (rows * groups * members) ** (-0.5)
    shard = lax.axis_index("shard").astype(jnp.int32).reshape(1)
    swap = [(0, 1), (1, 0)]

    meta = jnp.concatenate(
        [
            positions,
            crystal_of_atom.astype(BF)[None, :],
            jnp.zeros((META - 4, rows), BF),
        ],
        axis=0,
    )
    owner_row = atom_owner.reshape(1, rows)
    send = call(
        prep_kernel,
        jax.ShapeDtypeStruct((2, groups, 2 * width + META), BF),
        [features, norm_gain.reshape(1, width), cotangent, meta, atom_owner, owner_row],
    )
    recv = lax.all_to_all(send, "dp", split_axis=1, concat_axis=1, tiled=True)
    own = recv.reshape(slots, 2 * width + META)
    kmat, filt, w_in_t = call(
        functools.partial(static_kernel, scale_s=scale_s),
        (
            jax.ShapeDtypeStruct((META, kcount), BF),
            jax.ShapeDtypeStruct((half, kcount), F32),
            jax.ShapeDtypeStruct((half, width), BF),
        ),
        [shard, k_index, damping.reshape(width, 1), w_in],
        specs=[SM, VM, VM, VM],
    )
    other = lax.ppermute(own, "shard", swap)
    message, grads = call(
        functools.partial(main_kernel, scale_m=scale_m),
        (
            jax.ShapeDtypeStruct((half, 2 * slots), BF),
            jax.ShapeDtypeStruct((2 * half, width), BF),
        ),
        [shard, own, other, kmat, k_crystal.astype(F32).reshape(1, kcount), filt, w_in_t, w_out],
        scratch=[
            pltpu.VMEM((2 * slots, kcount), F32),
            pltpu.VMEM((2 * slots, 2 * kcount), BF),
            pltpu.VMEM((2 * half, 2 * slots), BF),
            pltpu.VMEM((2 * half, 2 * kcount), BF),
        ],
        specs=[SM] + [VM] * 7,
    )
    got = lax.ppermute(message[:, slots:], "shard", swap)
    back = call(
        change_kernel,
        jax.ShapeDtypeStruct((6, groups, width), BF),
        [shard, message[:, :slots], got, w_out, grads],
        specs=[SM] + [VM] * 4,
    )
    recv_back = lax.all_to_all(back, "dp", split_axis=1, concat_axis=1, tiled=True)
    share = call(
        functools.partial(sum_kernel, norm_factor=norm_factor),
        jax.ShapeDtypeStruct((4, groups, width), BF),
        [recv_back],
    )
    mine = lax.all_to_all(share, "dp", split_axis=1, concat_axis=1, tiled=True)
    updated = call(
        update_kernel,
        jax.ShapeDtypeStruct((rows, width), BF),
        [features, recv_back, atom_owner, owner_row],
    )
    theirs = lax.ppermute(mine, "shard", swap)
    grad_w_in, grad_w_out = call(
        final_kernel,
        (jax.ShapeDtypeStruct((width, width), F32), jax.ShapeDtypeStruct((width, width), F32)),
        [shard, mine, theirs],
        specs=[SM, VM, VM],
    )
    return (updated, grad_w_in, grad_w_out)


def solution(mesh):
    in_specs = (
        P(("dp", "shard"), None),
        P(),
        P(),
        P(),
        P(("dp", "shard"), None),
        P(None, ("dp", "shard")),
        P(("dp", "shard")),
        P(("dp", "shard"), None),
        P(None, "dp"),
        P("dp"),
        P(),
    )
    out_specs = (P(("dp", "shard"), None), P(), P())
    return jax.shard_map(local, mesh=mesh, in_specs=in_specs, out_specs=out_specs, check_vma=False)
```

time: 402 us -> 123 us (0.31)
  waiting for transfers between devices: 303 us -> 2.04 us
  blocking collectives: 0 us -> 95.8 us
  starting transfers between devices: 43.8 us -> 7.71 us
  other arithmetic: 14.9 us -> 0.75 us
  between operations: 14.3 us -> 0.79 us
  matrix products: 13 us -> 0 us
  Pallas kernels: 0 us -> 10.7 us
  local copies, waits for them, and re-layouts: 12 us -> 5.31 us
    psum x2 -> x0, waiting for transfers between devices: 269 us -> none  [the longest x1 231 us: local(): grad_w_in = lax.psum(local_in, ('dp', 'shard'))]
    all_to_all x0 -> x3, blocking collectives: none -> 95.8 us  [the longest x1 35.9 us: local(): recv = lax.all_to_all(send, 'dp', split_axis=1, concat_axis=1, tiled=True)]
    all_to_all x4 -> x0, starting transfers between devices: 43.6 us -> none  [the longest x1 16.3 us: local(): lax.all_to_all(meta_send, 'dp', split_axis=0, concat_axis=0, tiled=True)]
    all_to_all x4 -> x0, waiting for transfers between devices: 33.4 us -> none  [the longest x1 14.9 us: local(): lax.all_to_all(change.reshape(groups, capacity, width), 'dp', split_axis=...]
    dot_general x6 -> x0, matrix products: 13 us -> none  [the longest x1 4.02 us: local(): lax.dot_general(slot_x, grad_down, (((0,), (0,)), ((), ())), preferred_el...]
    pallas_call x0 -> x7, Pallas kernels: none -> 10.7 us  [call(): pl.pallas_call(body, out_shape=out_shape, in_specs=specs if specs is not...]
    convert_element_type x7 -> x1, other arithmetic: 9.08 us -> 0.01 us  [local(): k_crystal.astype(F32).reshape(1, kcount)]
    ppermute x0 -> x3, starting transfers between devices: none -> 7.71 us  [the longest x1 3.89 us: local(): theirs = lax.ppermute(mine, 'shard', swap)]
  transfers between devices with their start and end apart: 6 -> 3, of which waited for: 6 -> 3; matrix products, arithmetic and copies ran while one was open for 5% -> 0% of each run, Pallas kernels for 0% -> 2%
where the time goes in v1:
time: 123 us
  blocking collectives  95.8 us (78%)
  Pallas kernels  10.7 us (9%)
  starting transfers between devices  7.71 us (6%)
  local copies, waits for them, and re-layouts  5.31 us (4%)
  waiting for transfers between devices  2.04 us (2%)
    all_to_all x1, blocking collectives, local(): recv = lax.all_to_all(send, 'dp', split_axis=1, concat_axis=1, tiled=True)  35.9 us
    all_to_all x1, blocking collectives, local(): lax.all_to_all(back, 'dp', split_axis=1, concat_axis=1, tiled=True)  35.1 us
    all_to_all x1, blocking collectives, local(): mine = lax.all_to_all(share, 'dp', split_axis=1, concat_axis=1, tiled=True)  24.8 us
    pallas_call x7, Pallas kernels, call(): pl.pallas_call(body, out_shape=out_shape, in_specs=specs if specs is not...  10.7 us
    ppermute x1, starting transfers between devices, local(): theirs = lax.ppermute(mine, 'shard', swap)  3.89 us
    ppermute x1, starting transfers between devices, local(): other = lax.ppermute(own, 'shard', swap)  3.36 us
    unnamed x23, local copies, waits for them, and re-layouts  3.22 us
  transfers between devices with their start and end apart: 3, of which 3 were waited for; matrix products, arithmetic and copies ran while one was open for 0% of the time, Pallas kernels for 2%

profile of v1, /device:TPU:1, one launch (start us, length us, event | category | flops | bytes accessed | tf_op | source)
XLA Modules:
  0.0 123.1 jit_solution(1880062186453922621)
XLA Ops:
  0.6 0.0 copy-start.6
  0.6 0.7 convert_bitcast_fusion
  1.3 0.0 copy-done.6
  1.3 0.1 copy.19.col_ref
  1.4 0.0 copy-start.10
  1.4 0.1 pad.2.clone
  1.5 0.6 copy-done.10
  2.1 0.1 maximum_maximum_fusion.meta_ref
  2.2 0.0 copy-start.7
  2.2 0.7 copy-done.7
  2.9 0.0 copy-start.2
  2.9 0.9 copy-done.2
  3.8 0.0 copy-start.4
  3.8 0.9 copy-done.4
  4.7 0.4 shard_map.130
  5.1 0.6 copy.20
  5.8 35.9 %all_to_all.15 = bf16[2,128,1152]{2,0,1:T(2,128)(2,1)S(1)} all-to-all(bf16[2,128,1152]{2,0,1:T(2,128)(2,1)S(1)} %copy.20), channel_id=1, replica_groups=mesh['dp'=128,'shard'=2] {'dp'}, dimensions={1} | all-to-all | bytes 1179648 | tf_op jit(solution)/shard_map/all_to_all | solution.py:245
  41.7 0.0 copy-start.9
  41.7 0.0 copy-start.1
  41.7 0.0 copy-start.5
  41.7 0.1 copy.21
  41.7 0.0 copy-start.8
  41.7 3.4 %collective-permute-start = (bf16[256,1152]{1,0:T(8,128)(2,1)S(1)}, bf16[256,1152]{1,0:T(8,128)(2,1)S(1)}, u32[]{:S(2)}, u32[]{:S(2)}) collective-permute-start(bf16[256,1152]{1,0:T(8,128)(2,1)S(1)} %bitcast.8), channel_id=1, source_target_pairs={{0,1},{1,0},{2,3},{3,2},{4,5},{5,4},{6,7},{7,6},{8,9},{9,8},{10,11... | collective-permute-start | bytes 1769480 | tf_op jit(solution)/shard_map/ppermute | solution.py:257
  45.1 0.0 copy-done.8
  45.1 0.0 copy-done.9
  45.1 0.1 copy.22.damp_ref
  45.3 0.0 copy-done.1
  45.3 0.0 copy-done.5
  45.3 0.9 shard_map.131
  46.2 0.5 collective-permute-done.oth_ref
  46.7 0.0 copy-done
  46.7 6.3 %shard_map.132 = (bf16[256,512]{1,0:T(8,128)(2,1)S(1)}, bf16[512,512]{1,0:T(8,128)(2,1)S(1)}) custom-call(s32[1]{0:T(128)} %bitcast.shard_ref, bf16[256,1152]{1,0:T(8,128)(2,1)S(1)} %bitcast.9, bf16[256,1152]{1,0:T(8,128)(2,1)S(1)} %collective-permute-done.oth_ref, bf16[128,1024]{1,0:T(8,128)(2,1)S(1)} %get-tuple-element.10.kmat_ref, ...), custom_call_target="tpu_custom_call" | custom-call | tf_op jit(solution)/shard_map/pallas_call | solution.py:40
  53.1 0.5 collective-permute-start.1
  53.5 1.0 collective-permute-done.1.got_ref
  54.5 0.3 shard_map.133
  54.9 0.4 copy.23
  55.3 35.1 %all_to_all.16 = bf16[6,128,512]{2,0,1:T(8,128)(2,1)S(1)} all-to-all(bf16[6,128,512]{2,0,1:T(8,128)(2,1)S(1)} %copy.23), channel_id=1, replica_groups=mesh['dp'=128,'shard'=2] {'dp'}, dimensions={1} | all-to-all | bytes 1572864 | tf_op jit(solution)/shard_map/all_to_all | solution.py:280
  90.4 0.2 copy.24.recv_ref
  90.7 0.1 shard_map.135
  90.8 0.4 copy.27
  91.2 24.8 %all_to_all.17 = bf16[4,128,512]{2,0,1:T(4,128)(2,1)S(1)} all-to-all(bf16[4,128,512]{2,0,1:T(4,128)(2,1)S(1)} %copy.27), channel_id=1, replica_groups=mesh['dp'=128,'shard'=2] {'dp'}, dimensions={1} | all-to-all | bytes 1048576 | tf_op jit(solution)/shard_map/all_to_all | solution.py:286
  116.0 0.0 copy-start.3
  116.0 0.1 copy.29.own_ref
  116.1 3.9 %collective-permute-start.2 = (bf16[4,128,512]{2,1,0:T(8,128)(2,1)S(1)}, bf16[4,128,512]{2,1,0:T(8,128)(2,1)S(1)}, u32[]{:S(2)}, u32[]{:S(2)}) collective-permute-start(bf16[4,128,512]{2,1,0:T(8,128)(2,1)S(1)} %copy.29.own_ref), channel_id=1, source_target_pairs={{0,1},{1,0},{2,3},{3,2},{4,5},{5,4},{6,7},{7,6},{8,9},{9,8},{10,11... | collective-permute-start | bytes 1572872 | tf_op jit(solution)/shard_map/ppermute | solution.py:292
  119.9 0.0 copy-done.3
  119.9 1.0 shard_map.134
  120.9 0.5 collective-permute-done.2.oth_ref
  121.5 1.6 %shard_map.136 = (f32[512,512]{1,0:T(8,128)}, f32[512,512]{1,0:T(8,128)}) custom-call(s32[1]{0:T(128)} %bitcast.shard_ref, bf16[4,128,512]{2,1,0:T(8,128)(2,1)S(1)} %copy.29.own_ref, bf16[4,128,512]{2,1,0:T(8,128)(2,1)S(1)} %collective-permute-done.2.oth_ref), custom_call_target="tpu_custom_call" | custom-call | tf_op jit(solution)/shard_map/pallas_call | solution.py:40
  (4 shorter events, 0.0 us)
Async XLA Ops:
  0.6 0.7 copy-start.6
  1.4 0.7 copy-start.10
  2.2 0.7 copy-start.7
  2.9 0.9 copy-start.2
  3.8 0.9 copy-start.4
  41.7 3.5 %copy-start.9 = (f32[512]{0:T(512)S(1)}, f32[512]{0:T(512)}, u32[]{:S(2)}) copy-start(f32[512]{0:T(512)} %param.21) | copy-start | bytes 6148
  41.7 3.6 %copy-start.1 = (bf16[512,512]{1,0:T(8,128)(2,1)S(1)}, bf16[512,512]{1,0:T(8,128)(2,1)}, u32[]{:S(2)}) copy-start(bf16[512,512]{1,0:T(8,128)(2,1)} %w_in_ref.1) | copy-start | bytes 1572868
  41.7 3.6 %copy-start.5 = (s32[3,1024]{1,0:T(4,128)S(1)}, s32[3,1024]{1,0:T(4,128)}, u32[]{:S(2)}) copy-start(s32[3,1024]{1,0:T(4,128)} %k_ref.1) | copy-start | bytes 36868
  41.7 3.4 %copy-start.8 = (s32[1024]{0:T(1024)S(1)}, s32[1024]{0:T(1024)}, u32[]{:S(2)}) copy-start(s32[1024]{0:T(1024)} %param.20) | copy-start | bytes 12292
  41.7 5.0 %collective-permute-start = (bf16[256,1152]{1,0:T(8,128)(2,1)S(1)}, bf16[256,1152]{1,0:T(8,128)(2,1)S(1)}, u32[]{:S(2)}, u32[]{:S(2)}) collective-permute-start(bf16[256,1152]{1,0:T(8,128)(2,1)S(1)} %bitcast.8), channel_id=1, source_target_pairs={{0,1},{1,0},{2,3},{3,2},{4,5},{5,4},{6,7},{7,6},{8,9},{9,8},{10,11... | collective-permute-start | bytes 1769480 | tf_op jit(solution)/shard_map/ppermute | solution.py:257
  45.1 1.6 %copy-start = (bf16[512,512]{1,0:T(8,128)(2,1)S(1)}, bf16[512,512]{1,0:T(8,128)(2,1)}, u32[]{:S(2)}) copy-start(bf16[512,512]{1,0:T(8,128)(2,1)} %w_out_ref.3) | copy-start | bytes 1572868
  53.1 1.5 %collective-permute-start.1 = (bf16[256,256]{1,0:T(8,128)(2,1)S(1)}, bf16[256,256]{1,0:T(8,128)(2,1)S(1)}, u32[]{:S(2)}, u32[]{:S(2)}) collective-permute-start(bf16[256,256]{1,0:T(8,128)(2,1)S(1)} %get-tuple-element.17), channel_id=1, source_target_pairs={{0,1},{1,0},{2,3},{3,2},{4,5},{5,4},{6,7},{7,6},{8,9},{9,8},{10,11... | collective-permute-start | bytes 393224 | tf_op jit(solution)/shard_map/ppermute | solution.py:273
  116.0 4.0 %copy-start.3 = (bf16[128,512]{1,0:T(8,128)(2,1)S(1)}, bf16[128,512]{1,0:T(8,128)(2,1)}, u32[]{:S(2)}) copy-start(bf16[128,512]{1,0:T(8,128)(2,1)} %feat_ref.3) | copy-start | bytes 393220
  116.1 5.4 %collective-permute-start.2 = (bf16[4,128,512]{2,1,0:T(8,128)(2,1)S(1)}, bf16[4,128,512]{2,1,0:T(8,128)(2,1)S(1)}, u32[]{:S(2)}, u32[]{:S(2)}) collective-permute-start(bf16[4,128,512]{2,1,0:T(8,128)(2,1)S(1)} %copy.29.own_ref), channel_id=1, source_target_pairs={{0,1},{1,0},{2,3},{3,2},{4,5},{5,4},{6,7},{7,6},{8,9},{9,8},{10,11... | collective-permute-start | bytes 1572872 | tf_op jit(solution)/shard_map/ppermute | solution.py:292

commit v2 on v1

--- a/solution.py
+++ b/solution.py
@@ -6,6 +6,7 @@
 from jax import lax
 from jax.experimental import pallas as pl
 from jax.experimental.pallas import tpu as pltpu
+from jax.sharding import Mesh
 from jax.sharding import PartitionSpec as P
 
 CRY_DEV = 8
@@ -34,9 +35,11 @@
 
 VM = pl.BlockSpec(memory_space=pltpu.VMEM)
 SM = pl.BlockSpec(memory_space=pltpu.SMEM)
-
-
-def call(body, out_shape, inputs, scratch=(), specs=None):
+HB = pl.BlockSpec(memory_space=pl.ANY)
+PLANE = 16
+
+
+def call(body, out_shape, inputs, scratch=(), specs=None, flops=1_000_000):
     return pl.pallas_call(
         body,
         out_shape=out_shape,
@@ -44,6 +47,7 @@
         out_specs=jax.tree.map(lambda _: VM, out_shape),
         scratch_shapes=list(scratch),
         compiler_params=pltpu.CompilerParams(vmem_limit_bytes=VMEM_LIMIT),
+        cost_estimate=pl.CostEstimate(flops=flops, bytes_accessed=1_000_000, transcendentals=0),
     )(*inputs)
 
 
@@ -51,27 +55,69 @@
     return lax.dot_general(a, b, (((ca,), (cb,)), ((), ())), preferred_element_type=F32)
 
 
-def prep_kernel(feat_ref, gain_ref, cot_ref, meta_ref, col_ref, row_ref, out_ref):
-    rows = feat_ref.shape[0]
-    peers = out_ref.shape[1]
-    width = feat_ref.shape[1]
+def plane_major(owner):
+    return (owner & 15) * 8 + (owner >> 4)
+
+
+def as_column(row):
+    n = row.shape[1]
+    diagonal = lax.broadcasted_iota(jnp.int32, (n, n), 0) == lax.broadcasted_iota(
+        jnp.int32, (n, n), 1
+    )
+    return jnp.sum(jnp.where(diagonal, row, 0.0), axis=1, keepdims=True)
+
+
+def fetch(pairs, sems):
+    copies = [pltpu.make_async_copy(src, dst, sems.at[i]) for i, (src, dst) in enumerate(pairs)]
+    for copy in copies:
+        copy.start()
+    for copy in copies:
+        copy.wait()
+
+
+def prep_kernel(
+    feat_hbm, gain_hbm, cot_hbm, pos_hbm, cry_hbm, own_hbm, out_ref,
+    feat_ref, gain_ref, cot_ref, pos_ref, cry_ref, own_ref, sems,
+):
+    fetch(
+        (
+            (own_hbm, own_ref),
+            (feat_hbm, feat_ref),
+            (cot_hbm, cot_ref),
+            (gain_hbm, gain_ref),
+            (pos_hbm, pos_ref),
+            (cry_hbm, cry_ref),
+        ),
+        sems,
+    )
+    rows, width = feat_ref.shape
+    slots = out_ref.shape[0]
     hidden = feat_ref[...].astype(F32)
     normed = (
         hidden
         * lax.rsqrt(jnp.mean(hidden * hidden, axis=-1, keepdims=True) + 1e-06)
         * gain_ref[...]
     ).astype(BF)
-    owner = row_ref[...]
+    owner = plane_major(own_ref[...]).astype(F32)
     first = lax.broadcasted_iota(jnp.int32, (rows, rows), 0)
     second = lax.broadcasted_iota(jnp.int32, (rows, rows), 1)
-    earlier = (col_ref[...] == owner) & (first < second)
+    earlier = (as_column(owner) == owner) & (first < second)
     rank = jnp.sum(jnp.where(earlier, 1.0, 0.0), axis=0, keepdims=True)
-    peer = lax.broadcasted_iota(jnp.int32, (peers, rows), 0)
-    for r in range(2):
-        place = jnp.where((owner == peer) & (rank == float(r)), 1.0, 0.0).astype(BF)
-        out_ref[r, :, 0:width] = dot(place, normed, 1, 0).astype(BF)
-        out_ref[r, :, width : 2 * width] = dot(place, cot_ref[...], 1, 0).astype(BF)
-        out_ref[r, :, 2 * width : 2 * width + META] = dot(place, meta_ref[...], 1, 1).astype(BF)
+    slot = (owner * 2.0 + rank).astype(jnp.int32)
+    place = jnp.where(
+        slot == lax.broadcasted_iota(jnp.int32, (slots, rows), 0), 1.0, 0.0
+    ).astype(BF)
+    meta = jnp.concatenate(
+        [
+            pos_ref[...].astype(F32),
+            cry_ref[...].astype(F32),
+            jnp.zeros((META - 4, rows), F32),
+        ],
+        axis=0,
+    ).astype(BF)
+    out_ref[:, 0:width] = dot(place, normed, 1, 0).astype(BF)
+    out_ref[:, width : 2 * width] = dot(place, cot_ref[...], 1, 0).astype(BF)
+    out_ref[:, 2 * width : 2 * width + META] = dot(place, meta, 1, 1).astype(BF)
 
 
 def static_kernel(shard_ref, k_ref, damp_ref, w_in_ref, kmat_ref, filt_ref, w_in_t_ref, scale_s):
@@ -157,48 +203,74 @@
 
 def change_kernel(shard_ref, msg_ref, got_ref, w_out_ref, grad_ref, out_ref):
     half = msg_ref.shape[0]
-    slots = msg_ref.shape[1]
-    rows = out_ref.shape[1]
     mine = pl.multiple_of(shard_ref[0] * half, half)
     other = pl.multiple_of((1 - shard_ref[0]) * half, half)
     change = dot(msg_ref[...], w_out_ref[pl.ds(mine, half), :], 0, 0)
     change += dot(got_ref[...], w_out_ref[pl.ds(other, half), :], 0, 0)
     change = change.astype(BF)
-    for r in range(slots // rows):
-        out_ref[r] = change[r * rows : (r + 1) * rows]
-    for r in range(grad_ref.shape[0] // rows):
-        out_ref[slots // rows + r] = grad_ref[r * rows : (r + 1) * rows]
-
-
-def sum_kernel(recv_ref, out_ref, norm_factor):
-    for j in range(out_ref.shape[0]):
-        total = jnp.sum(recv_ref[2 + j].astype(F32), axis=0, keepdims=True) * norm_factor
-        out_ref[j] = jnp.broadcast_to(total.astype(BF), out_ref.shape[1:])
-
-
-def update_kernel(feat_ref, recv_ref, col_ref, row_ref, out_ref):
+    step = half // PLANE
+    for q in range(PLANE):
+        out_ref[q, 0:step] = change[q * step : (q + 1) * step]
+        out_ref[q, step : 2 * step] = grad_ref[q * step : (q + 1) * step]
+        out_ref[q, 2 * step :] = grad_ref[half + q * step : half + (q + 1) * step]
+
+
+def plane_sum_kernel(recv_ref, out_ref):
+    planes, block = out_ref.shape[0], recv_ref.shape[1] // 3
+    slots = PLANE * block
+    change = jnp.concatenate([recv_ref[q, 0:block] for q in range(PLANE)], axis=0)
+    to = lax.broadcasted_iota(jnp.int32, (slots, slots), 0)
+    of = lax.broadcasted_iota(jnp.int32, (slots, slots), 1)
+    width = 2 * PLANE
+    source = ((to & 31) >> 1) * block + (to >> 5) * 2 + (to & 1)
+    move = jnp.where(source == of, 1.0, 0.0).astype(BF)
+    change = dot(move, change, 1, 0).astype(BF)
+    total = recv_ref[0, block:].astype(F32)
+    for q in range(1, PLANE):
+        total += recv_ref[q, block:].astype(F32)
+    total = total.astype(BF)
+    for z in range(planes):
+        out_ref[z, 0:width] = change[z * width : (z + 1) * width]
+        out_ref[z, width:] = total
+
+
+def column_sum_kernel(recv_ref, out_ref, norm_factor):
+    first = recv_ref.shape[1] - out_ref.shape[1]
+    total = recv_ref[0, first:].astype(F32)
+    for z in range(1, recv_ref.shape[0]):
+        total += recv_ref[z, first:].astype(F32)
+    total = (total * norm_factor).astype(BF)
+    for q in range(out_ref.shape[0]):
+        out_ref[q] = total
+
+
+def update_kernel(feat_ref, recv_ref, own_ref, out_ref):
     rows = feat_ref.shape[0]
-    peers = recv_ref.shape[1]
-    owner = col_ref[...]
+    planes = recv_ref.shape[0]
+    width = 2 * PLANE
+    owner_row = own_ref[...].astype(F32)
+    owner = as_column(owner_row)
     first = lax.broadcasted_iota(jnp.int32, (rows, rows), 0)
     second = lax.broadcasted_iota(jnp.int32, (rows, rows), 1)
-    earlier = (owner == row_ref[...]) & (second < first)
+    earlier = (owner == owner_row) & (second < first)
     rank = jnp.sum(jnp.where(earlier, 1.0, 0.0), axis=1, keepdims=True)
-    peer = lax.broadcasted_iota(jnp.int32, (rows, peers), 1)
-    total = feat_ref[...].astype(F32)
-    for r in range(2):
-        pick = jnp.where((owner == peer) & (rank == float(r)), 1.0, 0.0).astype(BF)
-        total += dot(pick, recv_ref[r], 1, 0)
-    out_ref[...] = total.astype(BF)
+    slot = (owner * 2.0 + rank).astype(jnp.int32)
+    pick = jnp.where(
+        slot == lax.broadcasted_iota(jnp.int32, (rows, planes * width), 1), 1.0, 0.0
+    ).astype(BF)
+    change = jnp.concatenate([recv_ref[z, 0:width] for z in range(planes)], axis=0)
+    out_ref[...] = (feat_ref[...].astype(F32) + dot(pick, change, 1, 0)).astype(BF)
 
 
 def final_kernel(shard_ref, own_ref, oth_ref, grad_in_ref, grad_out_ref):
-    half = own_ref.shape[1] * 2
+    block = own_ref.shape[1] // 2
+    half = PLANE * block
     for ref, member in ((own_ref, shard_ref[0]), (oth_ref, 1 - shard_ref[0])):
         start = pl.multiple_of(member * half, half)
-        out = jnp.concatenate([ref[0], ref[1]], axis=0).astype(F32)
-        grad_out_ref[pl.ds(start, half), :] = out
-        into = jnp.concatenate([ref[2], ref[3]], axis=0).astype(F32)
+        for q in range(PLANE):
+            at = pl.ds(pl.multiple_of(start + q * block, block), block)
+            grad_out_ref[at, :] = ref[q, 0:block].astype(F32)
+        into = jnp.concatenate([ref[q, block:] for q in range(PLANE)], axis=0).astype(F32)
         grad_in_ref[:, pl.ds(start, half)] = into.T
 
 
@@ -216,7 +288,10 @@
     damping,
 ):
     rows, width = features.shape
-    groups = lax.axis_size("dp")
+    around = ("x", "y", "z")
+    plane = ("x", "y")
+    groups = lax.axis_size(around)
+    planes = lax.axis_size("z")
     members = lax.axis_size("shard")
     capacity = 2 * rows // groups
     slots = groups * capacity
@@ -228,22 +303,28 @@
     shard = lax.axis_index("shard").astype(jnp.int32).reshape(1)
     swap = [(0, 1), (1, 0)]
 
-    meta = jnp.concatenate(
-        [
-            positions,
-            crystal_of_atom.astype(BF)[None, :],
-            jnp.zeros((META - 4, rows), BF),
-        ],
-        axis=0,
-    )
     owner_row = atom_owner.reshape(1, rows)
+    packed = 2 * width + META
+    operands = [
+        features,
+        norm_gain.reshape(1, width),
+        cotangent,
+        positions,
+        crystal_of_atom.reshape(1, rows),
+        owner_row,
+    ]
     send = call(
         prep_kernel,
-        jax.ShapeDtypeStruct((2, groups, 2 * width + META), BF),
-        [features, norm_gain.reshape(1, width), cotangent, meta, atom_owner, owner_row],
-    )
-    recv = lax.all_to_all(send, "dp", split_axis=1, concat_axis=1, tiled=True)
-    own = recv.reshape(slots, 2 * width + META)
+        jax.ShapeDtypeStruct((slots, packed), BF),
+        operands,
+        scratch=[pltpu.VMEM(a.shape, a.dtype) for a in operands]
+        + [pltpu.SemaphoreType.DMA((len(operands),))],
+        specs=[HB] * len(operands),
+    )
+    recv = lax.all_to_all(
+        send.reshape(groups, capacity, packed), around, split_axis=0, concat_axis=0, tiled=True
+    )
+    own = recv.reshape(slots, packed)
     kmat, filt, w_in_t = call(
         functools.partial(static_kernel, scale_s=scale_s),
         (
@@ -253,6 +334,7 @@
         ),
         [shard, k_index, damping.reshape(width, 1), w_in],
         specs=[SM, VM, VM, VM],
+        flops=4_000_000_000,
     )
     other = lax.ppermute(own, "shard", swap)
     message, grads = call(
@@ -271,23 +353,31 @@
         specs=[SM] + [VM] * 7,
     )
     got = lax.ppermute(message[:, slots:], "shard", swap)
+    block = slots // PLANE
     back = call(
         change_kernel,
-        jax.ShapeDtypeStruct((6, groups, width), BF),
+        jax.ShapeDtypeStruct((PLANE, 3 * block, width), BF),
         [shard, message[:, :slots], got, w_out, grads],
         specs=[SM] + [VM] * 4,
     )
-    recv_back = lax.all_to_all(back, "dp", split_axis=1, concat_axis=1, tiled=True)
+    recv_plane = lax.all_to_all(back, plane, split_axis=0, concat_axis=0, tiled=True)
+    column = call(
+        plane_sum_kernel,
+        jax.ShapeDtypeStruct((planes, slots // planes + 2 * block, width), BF),
+        [recv_plane],
+    )
+    recv_column = lax.all_to_all(column, "z", split_axis=0, concat_axis=0, tiled=True)
     share = call(
-        functools.partial(sum_kernel, norm_factor=norm_factor),
-        jax.ShapeDtypeStruct((4, groups, width), BF),
-        [recv_back],
-    )
-    mine = lax.all_to_all(share, "dp", split_axis=1, concat_axis=1, tiled=True)
+        functools.partial(column_sum_kernel, norm_factor=norm_factor),
+        jax.ShapeDtypeStruct((PLANE, 2 * block, width), BF),
+        [recv_column],
+    )
+    mine = lax.all_to_all(share, plane, split_axis=0, concat_axis=0, tiled=True)
     updated = call(
         update_kernel,
         jax.ShapeDtypeStruct((rows, width), BF),
-        [features, recv_back, atom_owner, owner_row],
+        [features, recv_column, owner_row],
+        flops=4_000_000_000,
     )
     theirs = lax.ppermute(mine, "shard", swap)
     grad_w_in, grad_w_out = call(
@@ -300,18 +390,24 @@
 
 
 def solution(mesh):
+    axes = Mesh(
+        mesh.devices.reshape(mesh.shape["dp"] // PLANE, 4, PLANE // 4, mesh.shape["shard"]),
+        ("z", "x", "y", "shard"),
+    )
+    dp = ("z", "x", "y")
+    every = (*dp, "shard")
     in_specs = (
-        P(("dp", "shard"), None),
+        P(every, None),
         P(),
         P(),
         P(),
-        P(("dp", "shard"), None),
-        P(None, ("dp", "shard")),
-        P(("dp", "shard")),
-        P(("dp", "shard"), None),
-        P(None, "dp"),
-        P("dp"),
+        P(every, None),
+        P(None, every),
+        P(every),
+        P(every, None),
+        P(None, dp),
+        P(dp),
         P(),
     )
-    out_specs = (P(("dp", "shard"), None), P(), P())
-    return jax.shard_map(local, mesh=mesh, in_specs=in_specs, out_specs=out_specs, check_vma=False)
+    out_specs = (P(every, None), P(), P())
+    return jax.shard_map(local, mesh=axes, in_specs=in_specs, out_specs=out_specs, check_vma=False)

time: 123 us -> 109 us (0.89)
  blocking collectives: 95.8 us -> 83.4 us
  local copies, waits for them, and re-layouts: 5.31 us -> 3.78 us
    all_to_all x3 -> x4, blocking collectives: 95.8 us -> 83.4 us  [the longest x1 36.7 us: local(): lax.all_to_all(send.reshape(groups, capacity, packed), around, split_axis...]
    pallas_call x3 -> x0, local copies, waits for them, and re-layouts: 1.46 us -> none  [call(): pl.pallas_call(body, out_shape=out_shape, in_specs=specs if specs is not...]
    pallas_call x7 -> x8, Pallas kernels: 10.7 us -> 11.2 us  [call(): pl.pallas_call(body, out_shape=out_shape, in_specs=specs if specs is not...]
    unnamed x23 -> x24, local copies, waits for them, and re-layouts: 3.22 us -> 3.17 us
  transfers between devices with their start and end apart: 3 -> 3, of which waited for: 3 -> 2; matrix products, arithmetic and copies ran while one was open for 0% -> 0% of each run, Pallas kernels for 2% -> 2%
where the time goes in v2:
time: 109 us; the launch traced here: 108 us
  blocking collectives  83.4 us (77%)
  Pallas kernels  11.2 us (10%)
  starting transfers between devices  7.52 us (7%)
  local copies, waits for them, and re-layouts  3.78 us (3%)
  waiting for transfers between devices  1.55 us (1%)
    all_to_all x1, blocking collectives, local(): lax.all_to_all(send.reshape(groups, capacity, packed), around, split_axis...  36.7 us
    all_to_all x1, blocking collectives, local(): lax.all_to_all(column, 'z', split_axis=0, concat_axis=0, tiled=True)  17.6 us
    all_to_all x1, blocking collectives, local(): lax.all_to_all(back, plane, split_axis=0, concat_axis=0, tiled=True)  16 us
    all_to_all x1, blocking collectives, local(): mine = lax.all_to_all(share, plane, split_axis=0, concat_axis=0, tiled=True)  13.1 us
    pallas_call x8, Pallas kernels, call(): pl.pallas_call(body, out_shape=out_shape, in_specs=specs if specs is not...  11.2 us
    ppermute x1, starting transfers between devices, local(): theirs = lax.ppermute(mine, 'shard', swap)  4.24 us
    unnamed x24, local copies, waits for them, and re-layouts  3.17 us
    ppermute x1, starting transfers between devices, local(): other = lax.ppermute(own, 'shard', swap)  2.58 us
  transfers between devices with their start and end apart: 3, of which 2 were waited for; matrix products, arithmetic and copies ran while one was open for 0% of the time, Pallas kernels for 2%

profile of v2, /device:TPU:1, one launch (start us, length us, event | category | flops | bytes accessed | tf_op | source)
XLA Modules:
  0.0 108.2 jit_solution(8831194408942268164)
XLA Ops:
  0.6 0.0 copy-start.7
  0.6 0.0 copy-start.4
  0.7 0.0 copy-start.5
  0.7 0.0 copy-start.6
  0.7 0.6 copy-done.7
  1.3 0.0 copy-done.4
  1.3 0.0 copy-done.5
  1.3 0.0 copy-done.6
  1.3 0.0 copy-start.1
  1.3 0.9 copy-done.1
  2.3 0.0 copy-start.2
  2.3 0.9 copy-done.2
  3.2 0.8 shard_map.130
  4.0 0.2 reshape.34
  4.2 36.7 %all_to_all.20 = bf16[128,2,1152]{2,1,0:T(2,128)(2,1)S(1)} all-to-all(bf16[128,2,1152]{2,1,0:T(2,128)(2,1)S(1)} %reshape.34), channel_id=1, replica_groups=mesh['z'=8,'x'=4,'y'=4,'shard'=2] {'x','y','z'}, dimensions={0} | all-to-all | bytes 1179648 | tf_op jit(solution)/shard_map/all_to_all | solution.py:324
  40.9 0.0 copy-start.11
  40.9 0.0 copy-start.8
  40.9 0.2 reshape.35.own_ref
  41.1 0.0 copy-start.10
  41.1 2.6 %collective-permute-start = (bf16[256,1152]{1,0:T(8,128)(2,1)S(1)}, bf16[256,1152]{1,0:T(8,128)(2,1)S(1)}, u32[]{:S(2)}, u32[]{:S(2)}) collective-permute-start(bf16[256,1152]{1,0:T(8,128)(2,1)S(1)} %reshape.35.own_ref), channel_id=1, source_target_pairs={{0,1},{1,0},{2,3},{3,2},{4,5},{5,4},{6,7},{7,6},{8,9},{9,8},{10,11... | collective-permute-start | bytes 1769480 | tf_op jit(solution)/shard_map/ppermute | solution.py:339
  43.7 0.0 copy-done.10
  43.7 0.0 copy-done.11
  43.7 0.0 copy-start.9
  43.7 0.1 copy.14.damp_ref
  43.9 0.0 copy-done.8
  43.9 0.5 copy-done.9
  44.4 0.0 copy-start
  44.4 0.9 shard_map.131
  45.3 0.0 collective-permute-done.oth_ref
  45.4 0.1 copy-done
  45.5 6.3 %shard_map.132 = (bf16[256,512]{1,0:T(8,128)(2,1)S(1)}, bf16[512,512]{1,0:T(8,128)(2,1)S(1)}) custom-call(s32[1]{0:T(128)} %bitcast.shard_ref, bf16[256,1152]{1,0:T(8,128)(2,1)S(1)} %reshape.35.own_ref, bf16[256,1152]{1,0:T(8,128)(2,1)S(1)} %collective-permute-done.oth_ref, bf16[128,1024]{1,0:T(8,128)(2,1)S(1)} %get-tuple-element.10.kmat_ref, ...), custom_call_target="tpu_custom_call" | custom-call | flops 1000000 | bytes 1000000 | tf_op jit(solution)/shard_map/pallas_call | solution.py:43
  51.8 0.7 collective-permute-start.1
  52.5 1.0 collective-permute-done.1.got_ref
  53.5 0.3 shard_map.133
  53.8 16.0 %all_to_all.21.recv_ref = bf16[16,48,512]{2,1,0:T(8,128)(2,1)S(1)} all-to-all(bf16[16,48,512]{2,1,0:T(8,128)(2,1)S(1)} %shard_map.133), channel_id=1, replica_groups=mesh['z'=8,'x'=4,'y'=4,'shard'=2] {'x','y'}, dimensions={0} | all-to-all | bytes 1572864 | tf_op jit(solution)/shard_map/all_to_all | solution.py:363
  69.9 0.2 shard_map.134
  70.1 17.6 %all_to_all.22.recv_ref = bf16[8,64,512]{2,1,0:T(8,128)(2,1)S(1)} all-to-all(bf16[8,64,512]{2,1,0:T(8,128)(2,1)S(1)} %shard_map.134), channel_id=1, replica_groups=mesh['z'=8,'x'=4,'y'=4,'shard'=2] {'z'}, dimensions={0} | all-to-all | bytes 1048576 | tf_op jit(solution)/shard_map/all_to_all | solution.py:369
  87.7 0.1 shard_map.136
  87.8 0.0 copy-start.3
  87.8 13.1 %all_to_all.23.own_ref = bf16[16,32,512]{2,1,0:T(8,128)(2,1)S(1)} all-to-all(bf16[16,32,512]{2,1,0:T(8,128)(2,1)S(1)} %shard_map.136), channel_id=1, replica_groups=mesh['z'=8,'x'=4,'y'=4,'shard'=2] {'x','y'}, dimensions={0} | all-to-all | bytes 1048576 | tf_op jit(solution)/shard_map/all_to_all | solution.py:375
  100.9 4.2 %collective-permute-start.2 = (bf16[16,32,512]{2,1,0:T(8,128)(2,1)S(1)}, bf16[16,32,512]{2,1,0:T(8,128)(2,1)S(1)}, u32[]{:S(2)}, u32[]{:S(2)}) collective-permute-start(bf16[16,32,512]{2,1,0:T(8,128)(2,1)S(1)} %all_to_all.23.own_ref), channel_id=1, source_target_pairs={{0,1},{1,0},{2,3},{3,2},{4,5},{5,4},{6,7},{7,6},{8,9},{9,8},{10,11... | collective-permute-start | bytes 1572872 | tf_op jit(solution)/shard_map/ppermute | solution.py:382
  105.1 0.0 copy-done.3
  105.1 1.0 shard_map.135
  106.1 0.6 collective-permute-done.2.oth_ref
  106.7 1.6 %shard_map.137 = (f32[512,512]{1,0:T(8,128)}, f32[512,512]{1,0:T(8,128)}) custom-call(s32[1]{0:T(128)} %bitcast.shard_ref, bf16[16,32,512]{2,1,0:T(8,128)(2,1)S(1)} %all_to_all.23.own_ref, bf16[16,32,512]{2,1,0:T(8,128)(2,1)S(1)} %collective-permute-done.2.oth_ref), custom_call_target="tpu_custom_call" | custom-call | flops 1000000 | bytes 1000000 | tf_op jit(solution)/shard_map/pallas_call | solution.py:43
  (2 shorter events, 0.0 us)
Async XLA Ops:
  0.6 0.7 copy-start.7
  0.6 0.7 copy-start.4
  0.7 0.7 copy-start.5
  0.7 0.7 copy-start.6
  1.3 0.9 copy-start.1
  2.3 0.9 copy-start.2
  40.9 2.8 %copy-start.11 = (f32[512]{0:T(512)S(1)}, f32[512]{0:T(512)}, u32[]{:S(2)}) copy-start(f32[512]{0:T(512)} %param.21) | copy-start | bytes 6148
  40.9 3.0 %copy-start.8 = (bf16[512,512]{1,0:T(8,128)(2,1)S(1)}, bf16[512,512]{1,0:T(8,128)(2,1)}, u32[]{:S(2)}) copy-start(bf16[512,512]{1,0:T(8,128)(2,1)} %w_in_ref.1) | copy-start | bytes 1572868
  41.1 2.6 %copy-start.10 = (s32[1024]{0:T(1024)S(1)}, s32[1024]{0:T(1024)}, u32[]{:S(2)}) copy-start(s32[1024]{0:T(1024)} %param.20) | copy-start | bytes 12292
  41.1 4.2 %collective-permute-start = (bf16[256,1152]{1,0:T(8,128)(2,1)S(1)}, bf16[256,1152]{1,0:T(8,128)(2,1)S(1)}, u32[]{:S(2)}, u32[]{:S(2)}) collective-permute-start(bf16[256,1152]{1,0:T(8,128)(2,1)S(1)} %reshape.35.own_ref), channel_id=1, source_target_pairs={{0,1},{1,0},{2,3},{3,2},{4,5},{5,4},{6,7},{7,6},{8,9},{9,8},{10,11... | collective-permute-start | bytes 1769480 | tf_op jit(solution)/shard_map/ppermute | solution.py:339
  43.7 0.7 copy-start.9
  44.4 1.0 copy-start
  51.8 1.7 %collective-permute-start.1 = (bf16[256,256]{1,0:T(8,128)(2,1)S(1)}, bf16[256,256]{1,0:T(8,128)(2,1)S(1)}, u32[]{:S(2)}, u32[]{:S(2)}) collective-permute-start(bf16[256,256]{1,0:T(8,128)(2,1)S(1)} %get-tuple-element.17), channel_id=1, source_target_pairs={{0,1},{1,0},{2,3},{3,2},{4,5},{5,4},{6,7},{7,6},{8,9},{9,8},{10,11... | collective-permute-start | bytes 393224 | tf_op jit(solution)/shard_map/ppermute | solution.py:355
  87.8 17.4 %copy-start.3 = (bf16[128,512]{1,0:T(8,128)(2,1)S(1)}, bf16[128,512]{1,0:T(8,128)(2,1)}, u32[]{:S(2)}) copy-start(bf16[128,512]{1,0:T(8,128)(2,1)} %feat_ref.1) | copy-start | bytes 393220
  100.9 5.8 %collective-permute-start.2 = (bf16[16,32,512]{2,1,0:T(8,128)(2,1)S(1)}, bf16[16,32,512]{2,1,0:T(8,128)(2,1)S(1)}, u32[]{:S(2)}, u32[]{:S(2)}) collective-permute-start(bf16[16,32,512]{2,1,0:T(8,128)(2,1)S(1)} %all_to_all.23.own_ref), channel_id=1, source_target_pairs={{0,1},{1,0},{2,3},{3,2},{4,5},{5,4},{6,7},{7,6},{8,9},{9,8},{10,11... | collective-permute-start | bytes 1572872 | tf_op jit(solution)/shard_map/ppermute | solution.py:382

commit v3 on v2

--- a/solution.py
+++ b/solution.py
@@ -12,17 +12,17 @@
 CRY_DEV = 8
 BF = jnp.bfloat16
 F32 = jnp.float32
-VMEM_LIMIT = 48 * 1024 * 1024
+VMEM_LIMIT = 24 * 1024 * 1024
+FULL_VMEM = 63 * 1024 * 1024
 META = 128
 
 COS_POLY = (
-    1.0,
-    -19.73920440673828,
-    64.93911743164062,
-    -85.45014190673828,
-    60.16762924194336,
-    -25.967599868774414,
-    6.528658390045166,
+    0.9999992251396179,
+    -19.738981246948242,
+    64.92865753173828,
+    -85.27162170410156,
+    58.79049301147461,
+    -21.07110595703125,
 )
 SIN_POLY = (
     6.283185005187988,
@@ -35,18 +35,20 @@
 
 VM = pl.BlockSpec(memory_space=pltpu.VMEM)
 SM = pl.BlockSpec(memory_space=pltpu.SMEM)
-HB = pl.BlockSpec(memory_space=pl.ANY)
+HB = pl.BlockSpec(memory_space=pltpu.MemorySpace.HBM)
 PLANE = 16
 
 
-def call(body, out_shape, inputs, scratch=(), specs=None, flops=1_000_000):
+def call(body, out_shape, inputs, scratch=(), specs=None, outs=None, flops=1_000_000, aliases=None,
+         limit=VMEM_LIMIT):
     return pl.pallas_call(
         body,
         out_shape=out_shape,
         in_specs=specs if specs is not None else [VM] * len(inputs),
-        out_specs=jax.tree.map(lambda _: VM, out_shape),
+        out_specs=outs if outs is not None else jax.tree.map(lambda _: VM, out_shape),
         scratch_shapes=list(scratch),
-        compiler_params=pltpu.CompilerParams(vmem_limit_bytes=VMEM_LIMIT),
+        input_output_aliases=aliases or {},
+        compiler_params=pltpu.CompilerParams(vmem_limit_bytes=limit),
         cost_estimate=pl.CostEstimate(flops=flops, bytes_accessed=1_000_000, transcendentals=0),
     )(*inputs)
 
@@ -91,7 +93,7 @@
         sems,
     )
     rows, width = feat_ref.shape
-    slots = out_ref.shape[0]
+    slots = out_ref.shape[0] * out_ref.shape[1]
     hidden = feat_ref[...].astype(F32)
     normed = (
         hidden
@@ -115,19 +117,23 @@
         ],
         axis=0,
     ).astype(BF)
-    out_ref[:, 0:width] = dot(place, normed, 1, 0).astype(BF)
-    out_ref[:, width : 2 * width] = dot(place, cot_ref[...], 1, 0).astype(BF)
-    out_ref[:, 2 * width : 2 * width + META] = dot(place, meta, 1, 1).astype(BF)
-
-
-def static_kernel(shard_ref, k_ref, damp_ref, w_in_ref, kmat_ref, filt_ref, w_in_t_ref, scale_s):
+    first = 0
+    for part in (dot(place, normed, 1, 0), dot(place, cot_ref[...], 1, 0), dot(place, meta, 1, 1)):
+        last = first + part.shape[1]
+        out_ref[:, :, first:last] = part.reshape(slots // 2, 2, part.shape[1]).astype(BF)
+        first = last
+
+
+def static_kernel(
+    shard_ref, k_ref, kc_ref, damp_ref, w_in_ref, kmat_ref, kcf_ref, filt_ref, w_in_t_ref, scale_s
+):
     half = filt_ref.shape[0]
     start = pl.multiple_of(shard_ref[0] * half, half)
     kf = k_ref[...].astype(F32)
     kmat_ref[...] = jnp.zeros(kmat_ref.shape, BF)
     kmat_ref[0:16, :] = jnp.concatenate([kf, jnp.zeros((13, kf.shape[1]), F32)], axis=0).astype(BF)
+    kcf_ref[...] = kc_ref[...].astype(F32)
     ksq = kf[0:1] * kf[0:1] + kf[1:2] * kf[1:2] + kf[2:3] * kf[2:3]
-    damp = damp_ref[pl.ds(start, half), :]
     scale = scale_s / (1.0 + ksq)
     step = 32
 
@@ -141,64 +147,100 @@
     w_in_t_ref[...] = w_in_ref[:, pl.ds(start, half)].T
 
 
-def main_kernel(
-    shard_ref, own_ref, oth_ref, kmat_ref, kc_ref, filt_ref, w_in_t_ref, w_out_ref,
-    msg_ref, grad_ref,
-    turn_ref, phase_ref, stack_ref, scaled_ref, scale_m,
-):
-    slots = own_ref.shape[0]
-    width = w_out_ref.shape[1]
+def fill_phase(rows_ref, kmat_ref, kc_ref, turn_ref, phase_ref):
+    slots = rows_ref.shape[0]
+    kcount = kc_ref.shape[1]
+    first = rows_ref.shape[1] - META
+    turn_ref[...] = dot(rows_ref[:, first:], kmat_ref[...], 1, 0)
+    tile_rows, tile_cols = 16, 512
+
+    def tile(i, carry):
+        at = pl.ds(pl.multiple_of(i * tile_rows, tile_rows), tile_rows)
+        crystal = rows_ref[at, first:].astype(F32)[:, 3:4]
+        for j in range(kcount // tile_cols):
+            span = slice(j * tile_cols, (j + 1) * tile_cols)
+            turn = turn_ref[at, span]
+            rest = turn - jnp.floor(turn + 0.5)
+            square = rest * rest
+            cosine = jnp.full(square.shape, COS_POLY[-1], F32)
+            for c in COS_POLY[-2::-1]:
+                cosine = cosine * square + c
+            sine = jnp.full(square.shape, SIN_POLY[-1], F32)
+            for c in SIN_POLY[-2::-1]:
+                sine = sine * square + c
+            matched = crystal == kc_ref[:, span]
+            phase_ref[at, span] = jnp.where(matched, cosine, 0.0).astype(BF)
+            phase_ref[at, kcount + j * tile_cols : kcount + (j + 1) * tile_cols] = jnp.where(
+                matched, sine * rest, 0.0
+            ).astype(BF)
+        return carry
+
+    lax.fori_loop(0, slots // tile_rows, tile, 0)
+
+
+def fill_stack(rows_ref, w_in_t_ref, w_out_half, stack_ref):
     half = w_in_t_ref.shape[0]
-    kcount = kc_ref.shape[1]
-    start = pl.multiple_of(shard_ref[0] * half, half)
-    w_out_half = w_out_ref[pl.ds(start, half), :]
-    tile_rows, tile_cols = 16, 512
-    for m, ref in enumerate((own_ref, oth_ref)):
-        cols = slice(m * slots, (m + 1) * slots)
-        turn_ref[cols, :] = dot(ref[:, 2 * width :], kmat_ref[...], 1, 0)
-        stack_ref[0:half, cols] = dot(w_in_t_ref[...], ref[:, 0:width], 1, 1).astype(BF)
-        stack_ref[half:, cols] = dot(w_out_half, ref[:, width : 2 * width], 1, 1).astype(BF)
-
-        def tile(i, carry):
-            at = pl.multiple_of(i * tile_rows, tile_rows)
-            dst = pl.ds(pl.multiple_of(m * slots + at, tile_rows), tile_rows)
-            crystal = ref[pl.ds(at, tile_rows), 2 * width :].astype(F32)[:, 3:4]
-            for j in range(kcount // tile_cols):
-                span = slice(j * tile_cols, (j + 1) * tile_cols)
-                turn = turn_ref[dst, span]
-                rest = turn - jnp.floor(turn + 0.5)
-                square = rest * rest
-                cosine = jnp.full(square.shape, COS_POLY[-1], F32)
-                for c in COS_POLY[-2::-1]:
-                    cosine = cosine * square + c
-                sine = jnp.full(square.shape, SIN_POLY[-1], F32)
-                for c in SIN_POLY[-2::-1]:
-                    sine = sine * square + c
-                matched = crystal == kc_ref[:, span]
-                phase_ref[dst, span] = jnp.where(matched, cosine, 0.0).astype(BF)
-                phase_ref[dst, kcount + j * tile_cols : kcount + (j + 1) * tile_cols] = jnp.where(
-                    matched, sine * rest, 0.0
-                ).astype(BF)
-            return carry
-
-        lax.fori_loop(0, slots // tile_rows, tile, 0)
+    width = w_in_t_ref.shape[1]
+    stack_ref[0:half, :] = dot(w_in_t_ref[...], rows_ref[:, 0:width], 1, 1).astype(BF)
+    stack_ref[half:, :] = dot(w_out_half, rows_ref[:, width : 2 * width], 1, 1).astype(BF)
+
+
+def half_of(ref, shard_ref, half):
+    return ref[pl.ds(pl.multiple_of(shard_ref[0] * half, half), half), :]
+
+
+def own_kernel(
+    shard_ref, own_ref, kmat_ref, kc_ref, w_in_t_ref, w_out_ref, phase_ref, stack_ref, turn_ref
+):
+    fill_stack(own_ref, w_in_t_ref, half_of(w_out_ref, shard_ref, w_in_t_ref.shape[0]), stack_ref)
+    fill_phase(own_ref, kmat_ref, kc_ref, turn_ref, phase_ref)
+
+
+def there_and_back(stacks, phases, rows, filt_ref, scaled_ref, scale_m):
+    kcount = filt_ref.shape[1]
     block = 512
     for j in range(2 * kcount // block):
         span = slice(j * block, (j + 1) * block)
         lo = (j * block) % kcount
-        filt = filt_ref[:, lo : lo + block]
-        for part in range(2):
-            rows = slice(part * half, (part + 1) * half)
-            structure = dot(stack_ref[rows, :], phase_ref[:, span], 1, 0)
-            scaled_ref[rows, span] = (structure * filt).astype(BF)
-    for part, first in ((0, width), (1, 0)):
-        rows = slice(part * half, (part + 1) * half)
-        back = (scale_m * dot(scaled_ref[rows, :], phase_ref[...], 1, 1)).astype(BF)
-        if part == 0:
-            msg_ref[...] = back
-        total = dot(back[:, 0:slots], own_ref[:, first : first + width], 1, 0)
-        total += dot(back[:, slots:], oth_ref[:, first : first + width], 1, 0)
-        grad_ref[rows, :] = total.astype(BF)
+        structure = dot(stacks[0][rows, :], phases[0][:, span], 1, 0)
+        structure += dot(stacks[1][rows, :], phases[1][:, span], 1, 0)
+        scaled_ref[:, span] = (structure * filt_ref[:, lo : lo + block]).astype(BF)
+    return [
+        (scale_m * dot(scaled_ref[...], phase[...], 1, 1)).astype(BF) for phase in phases
+    ]
+
+
+def forward_kernel(
+    shard_ref, oth_ref, phase_own_ref, stack_own_ref, kmat_ref, kc_ref, filt_ref, w_in_t_ref,
+    w_out_ref,
+    phase_ref, stack_ref, msg_own_ref, msg_oth_ref,
+    turn_ref, scaled_ref, scale_m,
+):
+    half = w_in_t_ref.shape[0]
+    fill_stack(oth_ref, w_in_t_ref, half_of(w_out_ref, shard_ref, half), stack_ref)
+    fill_phase(oth_ref, kmat_ref, kc_ref, turn_ref, phase_ref)
+    msg_own_ref[...], msg_oth_ref[...] = there_and_back(
+        (stack_own_ref, stack_ref), (phase_own_ref, phase_ref), slice(0, half), filt_ref,
+        scaled_ref, scale_m,
+    )
+
+
+def backward_kernel(
+    own_ref, oth_ref, phase_own_ref, phase_oth_ref, stack_own_ref, stack_oth_ref, msg_own_ref,
+    msg_oth_ref, filt_ref, grad_ref, scaled_ref, scale_m,
+):
+    half = msg_own_ref.shape[0]
+    width = grad_ref.shape[1]
+    total = dot(msg_own_ref[...], own_ref[:, width : 2 * width], 1, 0)
+    total += dot(msg_oth_ref[...], oth_ref[:, width : 2 * width], 1, 0)
+    grad_ref[0:half, :] = total.astype(BF)
+    back_own, back_oth = there_and_back(
+        (stack_own_ref, stack_oth_ref), (phase_own_ref, phase_oth_ref), slice(half, 2 * half),
+        filt_ref, scaled_ref, scale_m,
+    )
+    total = dot(back_own, own_ref[:, 0:width], 1, 0)
+    total += dot(back_oth, oth_ref[:, 0:width], 1, 0)
+    grad_ref[half:, :] = total.astype(BF)
 
 
 def change_kernel(shard_ref, msg_ref, got_ref, w_out_ref, grad_ref, out_ref):
@@ -262,16 +304,23 @@
     out_ref[...] = (feat_ref[...].astype(F32) + dot(pick, change, 1, 0)).astype(BF)
 
 
-def final_kernel(shard_ref, own_ref, oth_ref, grad_in_ref, grad_out_ref):
-    block = own_ref.shape[1] // 2
+def final_kernel(*refs, member):
+    shard_ref, ref = refs[:2]
+    grad_in_hbm, grad_out_hbm, in_ref, out_ref, sems = refs[-5:]
+    block = ref.shape[1] // 2
     half = PLANE * block
-    for ref, member in ((own_ref, shard_ref[0]), (oth_ref, 1 - shard_ref[0])):
-        start = pl.multiple_of(member * half, half)
-        for q in range(PLANE):
-            at = pl.ds(pl.multiple_of(start + q * block, block), block)
-            grad_out_ref[at, :] = ref[q, 0:block].astype(F32)
-        into = jnp.concatenate([ref[q, block:] for q in range(PLANE)], axis=0).astype(F32)
-        grad_in_ref[:, pl.ds(start, half)] = into.T
+    which = shard_ref[0] if member == 0 else 1 - shard_ref[0]
+    start = pl.multiple_of(which * half, half)
+    for q in range(PLANE):
+        out_ref[q * block : (q + 1) * block, :] = ref[q, 0:block].astype(F32)
+    rows = pltpu.make_async_copy(out_ref, grad_out_hbm.at[pl.ds(start, half), :], sems.at[0])
+    rows.start()
+    into = jnp.concatenate([ref[q, block:] for q in range(PLANE)], axis=0).astype(F32)
+    in_ref[...] = into.T
+    cols = pltpu.make_async_copy(in_ref, grad_in_hbm.at[:, pl.ds(start, half)], sems.at[1])
+    cols.start()
+    rows.wait()
+    cols.wait()
 
 
 def local(
@@ -315,49 +364,62 @@
     ]
     send = call(
         prep_kernel,
-        jax.ShapeDtypeStruct((slots, packed), BF),
+        jax.ShapeDtypeStruct((groups, capacity, packed), BF),
         operands,
         scratch=[pltpu.VMEM(a.shape, a.dtype) for a in operands]
         + [pltpu.SemaphoreType.DMA((len(operands),))],
         specs=[HB] * len(operands),
-    )
-    recv = lax.all_to_all(
-        send.reshape(groups, capacity, packed), around, split_axis=0, concat_axis=0, tiled=True
-    )
+        limit=FULL_VMEM,
+    )
+    recv = lax.all_to_all(send, around, split_axis=0, concat_axis=0, tiled=True)
     own = recv.reshape(slots, packed)
-    kmat, filt, w_in_t = call(
+    kmat, kc, filt, w_in_t = call(
         functools.partial(static_kernel, scale_s=scale_s),
         (
             jax.ShapeDtypeStruct((META, kcount), BF),
+            jax.ShapeDtypeStruct((1, kcount), F32),
             jax.ShapeDtypeStruct((half, kcount), F32),
             jax.ShapeDtypeStruct((half, width), BF),
         ),
-        [shard, k_index, damping.reshape(width, 1), w_in],
-        specs=[SM, VM, VM, VM],
+        [shard, k_index, k_crystal.reshape(1, kcount), damping.reshape(width, 1), w_in],
+        specs=[SM, VM, VM, VM, VM],
         flops=4_000_000_000,
     )
+    own, kmat, kc, filt, w_in_t = lax.optimization_barrier((own, kmat, kc, filt, w_in_t))
     other = lax.ppermute(own, "shard", swap)
-    message, grads = call(
-        functools.partial(main_kernel, scale_m=scale_m),
-        (
-            jax.ShapeDtypeStruct((half, 2 * slots), BF),
-            jax.ShapeDtypeStruct((2 * half, width), BF),
-        ),
-        [shard, own, other, kmat, k_crystal.astype(F32).reshape(1, kcount), filt, w_in_t, w_out],
-        scratch=[
-            pltpu.VMEM((2 * slots, kcount), F32),
-            pltpu.VMEM((2 * slots, 2 * kcount), BF),
-            pltpu.VMEM((2 * half, 2 * slots), BF),
-            pltpu.VMEM((2 * half, 2 * kcount), BF),
-        ],
-        specs=[SM] + [VM] * 7,
-    )
-    got = lax.ppermute(message[:, slots:], "shard", swap)
+    phase_shape = jax.ShapeDtypeStruct((slots, 2 * kcount), BF)
+    stack_shape = jax.ShapeDtypeStruct((2 * half, slots), BF)
+    message_shape = jax.ShapeDtypeStruct((half, slots), BF)
+    turn = pltpu.VMEM((slots, kcount), F32)
+    scaled = pltpu.VMEM((half, 2 * kcount), BF)
+    phase_own, stack_own = call(
+        own_kernel,
+        (phase_shape, stack_shape),
+        [shard, own, kmat, kc, w_in_t, w_out],
+        scratch=[turn],
+        specs=[SM] + [VM] * 5,
+        flops=4_000_000_000,
+    )
+    phase_oth, stack_oth, message, message_oth = call(
+        functools.partial(forward_kernel, scale_m=scale_m),
+        (phase_shape, stack_shape, message_shape, message_shape),
+        [shard, other, phase_own, stack_own, kmat, kc, filt, w_in_t, w_out],
+        scratch=[turn, scaled],
+        specs=[SM] + [VM] * 8,
+    )
+    got = lax.ppermute(message_oth, "shard", swap)
+    grads = call(
+        functools.partial(backward_kernel, scale_m=scale_m),
+        jax.ShapeDtypeStruct((2 * half, width), BF),
+        [own, other, phase_own, phase_oth, stack_own, stack_oth, message, message_oth, filt],
+        scratch=[scaled],
+        flops=4_000_000_000,
+    )
     block = slots // PLANE
     back = call(
         change_kernel,
         jax.ShapeDtypeStruct((PLANE, 3 * block, width), BF),
-        [shard, message[:, :slots], got, w_out, grads],
+        [shard, message, got, w_out, grads],
         specs=[SM] + [VM] * 4,
     )
     recv_plane = lax.all_to_all(back, plane, split_axis=0, concat_axis=0, tiled=True)
@@ -380,11 +442,30 @@
         flops=4_000_000_000,
     )
     theirs = lax.ppermute(mine, "shard", swap)
+    grads = (jax.ShapeDtypeStruct((width, width), F32),) * 2
+    placing = dict(
+        outs=(HB, HB),
+        scratch=[
+            pltpu.VMEM((width, half), F32),
+            pltpu.VMEM((half, width), F32),
+            pltpu.SemaphoreType.DMA((2,)),
+        ],
+    )
+    first = call(
+        functools.partial(final_kernel, member=0),
+        grads,
+        [shard, mine],
+        specs=[SM, VM],
+        flops=4_000_000_000,
+        **placing,
+    )
     grad_w_in, grad_w_out = call(
-        final_kernel,
-        (jax.ShapeDtypeStruct((width, width), F32), jax.ShapeDtypeStruct((width, width), F32)),
-        [shard, mine, theirs],
-        specs=[SM, VM, VM],
+        functools.partial(final_kernel, member=1),
+        grads,
+        [shard, theirs, *first],
+        specs=[SM, VM, HB, HB],
+        aliases={2: 0, 3: 1},
+        **placing,
     )
     return (updated, grad_w_in, grad_w_out)
 

time: 109 us -> 105 us (0.963)
  blocking collectives: 83.4 us -> 46.9 us
  waiting for transfers between devices: 1.55 us -> 18.2 us
  starting transfers between devices: 7.52 us -> 23.5 us
  Pallas kernels: 11.2 us -> 13.8 us
  local copies, waits for them, and re-layouts: 3.78 us -> 1.62 us
    all_to_all x1 -> x0, blocking collectives: 36.7 us -> none  [local(): lax.all_to_all(send.reshape(groups, capacity, packed), around, split_axis...]
    all_to_all x0 -> x1, waiting for transfers between devices: none -> 18.2 us  [local(): recv = lax.all_to_all(send, around, split_axis=0, concat_axis=0, tiled=True)]
    all_to_all x0 -> x1, starting transfers between devices: none -> 16.5 us  [local(): recv = lax.all_to_all(send, around, split_axis=0, concat_axis=0, tiled=True)]
    pallas_call x8 -> x11, Pallas kernels: 11.2 us -> 13.8 us  [call(): pl.pallas_call(body, out_shape=out_shape, in_specs=specs if specs is not...]
    unnamed x24 -> x14, local copies, waits for them, and re-layouts: 3.17 us -> 1.26 us
  transfers between devices with their start and end apart: 3 -> 4, of which waited for: 2 -> 1; matrix products, arithmetic and copies ran while one was open for 0% -> 0% of each run, Pallas kernels for 2% -> 6%
where the time goes in v3:
time: 105 us
  blocking collectives  46.9 us (45%)
  starting transfers between devices  23.5 us (22%)
  waiting for transfers between devices  18.2 us (17%)
  Pallas kernels  13.8 us (13%)
  local copies, waits for them, and re-layouts  1.62 us (2%)
    all_to_all x1, waiting for transfers between devices, local(): recv = lax.all_to_all(send, around, split_axis=0, concat_axis=0, tiled=True)  18.2 us
    all_to_all x1, blocking collectives, local(): lax.all_to_all(column, 'z', split_axis=0, concat_axis=0, tiled=True)  17.5 us
    all_to_all x1, starting transfers between devices, local(): recv = lax.all_to_all(send, around, split_axis=0, concat_axis=0, tiled=True)  16.5 us
    all_to_all x1, blocking collectives, local(): lax.all_to_all(back, plane, split_axis=0, concat_axis=0, tiled=True)  16 us
    pallas_call x11, Pallas kernels, call(): pl.pallas_call(body, out_shape=out_shape, in_specs=specs if specs is not...  13.8 us
    all_to_all x1, blocking collectives, local(): mine = lax.all_to_all(share, plane, split_axis=0, concat_axis=0, tiled=True)  13.4 us
    ppermute x1, starting transfers between devices, local(): theirs = lax.ppermute(mine, 'shard', swap)  4.12 us
    ppermute x1, starting transfers between devices, local(): other = lax.ppermute(own, 'shard', swap)  2.58 us
  transfers between devices with their start and end apart: 4, of which 1 were waited for; matrix products, arithmetic and copies ran while one was open for 0% of the time, Pallas kernels for 6%

profile of v3, /device:TPU:1, one launch (start us, length us, event | category | flops | bytes accessed | tf_op | source)
XLA Modules:
  0.0 104.8 jit_solution(6666400847191562517)
XLA Ops:
  0.6 2.6 %shard_map.130 = bf16[128,2,1152]{2,1,0:T(2,128)(2,1)} custom-call(bf16[128,512]{1,0:T(8,128)(2,1)} %feat_ref.1, f32[1,512]{1,0:T(1,128)} %bitcast.9, bf16[128,512]{1,0:T(8,128)(2,1)} %cot_hbm.1, bf16[3,128]{1,0:T(4,128)(2,1)} %pos_hbm.1, s32[1,128]{1,0:T(1,128)} %bitcast.11, s32[1,128]{1,0:T(1,128)} %bitcast.6), custom_call_target="tpu_custom_call" | custom-call | flops 1000000 | bytes 1000000 | tf_op jit(solution)/shard_map/pallas_call | solution.py:44
  3.3 0.0 copy-start.3
  3.3 16.5 %all-to-all-start = ((bf16[128,2,1152]{2,1,0:T(2,128)(2,1)}), bf16[128,2,1152]{2,1,0:T(2,128)(2,1)S(1)}, u32[]{:S(2)}, u32[]{:S(2)}) async-start(bf16[128,2,1152]{2,1,0:T(2,128)(2,1)} %shard_map.130), calls=%async_computation | async-start | bytes 1179648 | tf_op jit(solution)/shard_map/all_to_all | solution.py:374
  19.8 0.0 copy-start.6
  19.8 0.7 copy-done.6
  20.5 0.0 copy-start.4
  20.5 0.0 copy-start.5
  20.5 0.1 copy.16.damp_ref
  20.6 0.0 copy-done.3
  20.6 0.6 copy-done.4
  21.2 0.0 copy-done.5
  21.2 0.9 shard_map.131
  22.1 0.0 copy-start
  22.1 18.2 %all-to-all-done = bf16[128,2,1152]{2,1,0:T(2,128)(2,1)S(1)} async-done(((bf16[128,2,1152]{2,1,0:T(2,128)(2,1)}), bf16[128,2,1152]{2,1,0:T(2,128)(2,1)S(1)}, u32[]{:S(2)}, u32[]{:S(2)}) %all-to-all-start) | async-done | bytes 589856 | tf_op jit(solution)/shard_map/all_to_all | solution.py:374
  40.3 0.2 reshape.31.own_ref
  40.5 2.6 %collective-permute-start = (bf16[256,1152]{1,0:T(8,128)(2,1)S(1)}, bf16[256,1152]{1,0:T(8,128)(2,1)S(1)}, u32[]{:S(2)}, u32[]{:S(2)}) collective-permute-start(bf16[256,1152]{1,0:T(8,128)(2,1)S(1)} %reshape.31.own_ref), channel_id=1, source_target_pairs={{0,1},{1,0},{2,3},{3,2},{4,5},{5,4},{6,7},{7,6},{8,9},{9,8},{10,11... | collective-permute-start | bytes 1769480 | tf_op jit(solution)/shard_map/ppermute | solution.py:389
  43.1 0.0 copy-done
  43.1 1.8 %shard_map.132 = (bf16[256,2048]{1,0:T(8,128)(2,1)S(1)}, bf16[512,256]{1,0:T(8,128)(2,1)S(1)}) custom-call(s32[1]{0:T(128)} %bitcast.shard_ref.refs_0_, bf16[256,1152]{1,0:T(8,128)(2,1)S(1)} %reshape.31.own_ref, bf16[128,1024]{1,0:T(8,128)(2,1)S(1)} %get-tuple-element.27.kmat_ref, f32[1,1024]{1,0:T(1,128)S(1)} %get-tuple-element.28.kc_ref, ...), custom_call_target="tpu_custom_call" | custom-call | flops 4000000000 | bytes 1000000 | tf_op jit(solution)/shard_map/pallas_call | solution.py:44
  44.9 0.0 collective-permute-done.oth_ref
  44.9 3.1 %shard_map.133 = (bf16[256,2048]{1,0:T(8,128)(2,1)S(1)}, bf16[512,256]{1,0:T(8,128)(2,1)S(1)}, bf16[256,256]{1,0:T(8,128)(2,1)S(1)}, bf16[256,256]{1,0:T(8,128)(2,1)S(1)}) custom-call(s32[1]{0:T(128)} %bitcast.shard_ref.refs_0_, bf16[256,1152]{1,0:T(8,128)(2,1)S(1)} %collective-permute-done.oth_ref, bf16[256,2048]{1,0:T(8,128)(2,1)S(1)} %get-tuple-element.30.phase_own_ref, ...), custom_call_target="tpu_custom_call" | custom-call | flops 1000000 | bytes 1000000 | tf_op jit(solution)/shard_map/pallas_call | solution.py:44
  48.0 0.3 collective-permute-start.1
  48.3 1.6 %shard_map.134.grad_ref = bf16[512,512]{1,0:T(8,128)(2,1)S(1)} custom-call(bf16[256,1152]{1,0:T(8,128)(2,1)S(1)} %reshape.31.own_ref, bf16[256,1152]{1,0:T(8,128)(2,1)S(1)} %collective-permute-done.oth_ref, bf16[256,2048]{1,0:T(8,128)(2,1)S(1)} %get-tuple-element.30.phase_own_ref, bf16[256,2048]{1,0:T(8,128)(2,1)S(1)} %get-tuple-element.35.phase_oth_ref, ...), custom_call_target="tpu_custom_call" | custom-call | flops 4000000000 | bytes 1000000 | tf_op jit(solution)/shard_map/pallas_call | solution.py:44
  49.9 0.0 collective-permute-done.1.got_ref
  49.9 0.3 shard_map.135
  50.2 16.0 %all_to_all.20.recv_ref = bf16[16,48,512]{2,1,0:T(8,128)(2,1)S(1)} all-to-all(bf16[16,48,512]{2,1,0:T(8,128)(2,1)S(1)} %shard_map.135), channel_id=1, replica_groups=mesh['z'=8,'x'=4,'y'=4,'shard'=2] {'x','y'}, dimensions={0} | all-to-all | bytes 1572864 | tf_op jit(solution)/shard_map/all_to_all | solution.py:425
  66.2 0.2 shard_map.136
  66.5 17.5 %all_to_all.21.recv_ref = bf16[8,64,512]{2,1,0:T(8,128)(2,1)S(1)} all-to-all(bf16[8,64,512]{2,1,0:T(8,128)(2,1)S(1)} %shard_map.136), channel_id=1, replica_groups=mesh['z'=8,'x'=4,'y'=4,'shard'=2] {'z'}, dimensions={0} | all-to-all | bytes 1048576 | tf_op jit(solution)/shard_map/all_to_all | solution.py:431
  84.0 0.1 shard_map.138
  84.1 0.0 copy-start.1
  84.1 0.0 copy-start.2
  84.1 13.4 %all_to_all.22.refs_1_ = bf16[16,32,512]{2,1,0:T(8,128)(2,1)S(1)} all-to-all(bf16[16,32,512]{2,1,0:T(8,128)(2,1)S(1)} %shard_map.138), channel_id=1, replica_groups=mesh['z'=8,'x'=4,'y'=4,'shard'=2] {'x','y'}, dimensions={0} | all-to-all | bytes 1048576 | tf_op jit(solution)/shard_map/all_to_all | solution.py:437
  97.5 4.1 %collective-permute-start.2 = (bf16[16,32,512]{2,1,0:T(8,128)(2,1)S(1)}, bf16[16,32,512]{2,1,0:T(8,128)(2,1)S(1)}, u32[]{:S(2)}, u32[]{:S(2)}) collective-permute-start(bf16[16,32,512]{2,1,0:T(8,128)(2,1)S(1)} %all_to_all.22.refs_1_), channel_id=1, source_target_pairs={{0,1},{1,0},{2,3},{3,2},{4,5},{5,4},{6,7},{7,6},{8,9},{9,8},{10,11... | collective-permute-start | bytes 1572872 | tf_op jit(solution)/shard_map/ppermute | solution.py:444
  101.6 0.0 copy-done.1
  101.6 0.0 copy-done.2
  101.6 1.0 shard_map.137
  102.6 1.1 %shard_map.139 = (f32[512,512]{1,0:T(8,128)}, f32[512,512]{1,0:T(8,128)}) custom-call(s32[1]{0:T(128)} %bitcast.shard_ref.refs_0_, bf16[16,32,512]{2,1,0:T(8,128)(2,1)S(1)} %all_to_all.22.refs_1_), custom_call_target="tpu_custom_call" | custom-call | flops 4000000000 | bytes 1000000 | tf_op jit(solution)/shard_map/pallas_call | solution.py:44
  103.7 0.0 collective-permute-done.2.refs_1_
  103.7 1.1 %shard_map.140 = (f32[512,512]{1,0:T(8,128)}, f32[512,512]{1,0:T(8,128)}) custom-call(s32[1]{0:T(128)} %bitcast.shard_ref.refs_0_, bf16[16,32,512]{2,1,0:T(8,128)(2,1)S(1)} %collective-permute-done.2.refs_1_, f32[512,512]{1,0:T(8,128)} %get-tuple-element.37.refs_2_, f32[512,512]{1,0:T(8,128)} %get-tuple-element.38.refs_3_), custom_call_target="tpu_custom_call", output_to_operand_aliasing={{0}: (2, {}), {1}: (3, {})} | custom-call | flops 1000000 | bytes 1000000 | tf_op jit(solution)/shard_map/pallas_call | solution.py:44
Async XLA Ops:
  3.3 17.3 %copy-start.3 = (bf16[512,512]{1,0:T(8,128)(2,1)S(1)}, bf16[512,512]{1,0:T(8,128)(2,1)}, u32[]{:S(2)}) copy-start(bf16[512,512]{1,0:T(8,128)(2,1)} %w_in_ref.1) | copy-start | bytes 1572868
  3.3 37.0 %all-to-all-start = ((bf16[128,2,1152]{2,1,0:T(2,128)(2,1)}), bf16[128,2,1152]{2,1,0:T(2,128)(2,1)S(1)}, u32[]{:S(2)}, u32[]{:S(2)}) async-start(bf16[128,2,1152]{2,1,0:T(2,128)(2,1)} %shard_map.130), calls=%async_computation | async-start | bytes 1179648 | tf_op jit(solution)/shard_map/all_to_all | solution.py:374
  19.8 0.7 copy-start.6
  20.5 0.7 copy-start.4
  20.5 0.7 copy-start.5
  22.1 21.0 %copy-start = (bf16[512,512]{1,0:T(8,128)(2,1)S(1)}, bf16[512,512]{1,0:T(8,128)(2,1)}, u32[]{:S(2)}) copy-start(bf16[512,512]{1,0:T(8,128)(2,1)} %w_out_ref.5) | copy-start | bytes 1572868
  40.5 4.4 %collective-permute-start = (bf16[256,1152]{1,0:T(8,128)(2,1)S(1)}, bf16[256,1152]{1,0:T(8,128)(2,1)S(1)}, u32[]{:S(2)}, u32[]{:S(2)}) collective-permute-start(bf16[256,1152]{1,0:T(8,128)(2,1)S(1)} %reshape.31.own_ref), channel_id=1, source_target_pairs={{0,1},{1,0},{2,3},{3,2},{4,5},{5,4},{6,7},{7,6},{8,9},{9,8},{10,11... | collective-permute-start | bytes 1769480 | tf_op jit(solution)/shard_map/ppermute | solution.py:389
  48.0 1.9 %collective-permute-start.1 = (bf16[256,256]{1,0:T(8,128)(2,1)S(1)}, bf16[256,256]{1,0:T(8,128)(2,1)S(1)}, u32[]{:S(2)}, u32[]{:S(2)}) collective-permute-start(bf16[256,256]{1,0:T(8,128)(2,1)S(1)} %get-tuple-element.34.msg_oth_ref), channel_id=1, source_target_pairs={{0,1},{1,0},{2,3},{3,2},{4,5},{5,4},{6,7},{7,6},{8,9},{9,8},{10,11... | collective-permute-start | bytes 393224 | tf_op jit(solution)/shard_map/ppermute | solution.py:410
  84.1 17.5 %copy-start.1 = (bf16[128,512]{1,0:T(8,128)(2,1)S(1)}, bf16[128,512]{1,0:T(8,128)(2,1)}, u32[]{:S(2)}) copy-start(bf16[128,512]{1,0:T(8,128)(2,1)} %feat_ref.1) | copy-start | bytes 393220
  84.1 17.5 %copy-start.2 = (s32[128,1]{0,1:T(1,128)S(1)}, s32[128,1]{0,1:T(1,128)}, u32[]{:S(2)}) copy-start(s32[128,1]{0,1:T(1,128)} %param.18) | copy-start | bytes 1540
  97.5 6.2 %collective-permute-start.2 = (bf16[16,32,512]{2,1,0:T(8,128)(2,1)S(1)}, bf16[16,32,512]{2,1,0:T(8,128)(2,1)S(1)}, u32[]{:S(2)}, u32[]{:S(2)}) collective-permute-start(bf16[16,32,512]{2,1,0:T(8,128)(2,1)S(1)} %all_to_all.22.refs_1_), channel_id=1, source_target_pairs={{0,1},{1,0},{2,3},{3,2},{4,5},{5,4},{6,7},{7,6},{8,9},{9,8},{10,11... | collective-permute-start | bytes 1572872 | tf_op jit(solution)/shard_map/ppermute | solution.py:444

commit v4 on v3

--- a/solution.py
+++ b/solution.py
@@ -6,7 +6,6 @@
 from jax import lax
 from jax.experimental import pallas as pl
 from jax.experimental.pallas import tpu as pltpu
-from jax.sharding import Mesh
 from jax.sharding import PartitionSpec as P
 
 CRY_DEV = 8
@@ -39,6 +38,40 @@
 PLANE = 16
 
 
+def place_of(owner, shard):
+    first = jnp.where(shard == 0, owner & 15, (owner >> 4) * 2 + (owner & 1))
+    second = jnp.where(shard == 0, owner >> 4, (owner >> 1) & 7)
+    return first, second
+
+
+def hop_sets():
+    every = [(z, x, y) for z in range(8) for x in range(4) for y in range(4)]
+
+    def split(shard):
+        if shard == 0:
+            return {(x * 4 + y, z): (z, x, y) for z, x, y in every}
+        return {(z * 2 + y % 2, x * 2 + y // 2): (z, x, y) for z, x, y in every}
+
+    around, first, second = [], [], []
+    for shard in range(2):
+        at = {key: ((z * 4 + x) * 4 + y) * 2 + shard for key, (z, x, y) in split(shard).items()}
+        around.append([at[i, j] for i in range(PLANE) for j in range(8)])
+        first += [[at[i, j] for i in range(PLANE)] for j in range(8)]
+        second += [[at[i, j] for j in range(8)] for i in range(PLANE)]
+    return around, first, second
+
+
+def exchange(array, sets):
+    return lax.all_to_all(
+        array,
+        ("dp", "shard"),
+        split_axis=0,
+        concat_axis=0,
+        axis_index_groups=sets,
+        tiled=True,
+    )
+
+
 def call(body, out_shape, inputs, scratch=(), specs=None, outs=None, flops=1_000_000, aliases=None,
          limit=VMEM_LIMIT):
     return pl.pallas_call(
@@ -57,10 +90,6 @@
     return lax.dot_general(a, b, (((ca,), (cb,)), ((), ())), preferred_element_type=F32)
 
 
-def plane_major(owner):
-    return (owner & 15) * 8 + (owner >> 4)
-
-
 def as_column(row):
     n = row.shape[1]
     diagonal = lax.broadcasted_iota(jnp.int32, (n, n), 0) == lax.broadcasted_iota(
@@ -78,7 +107,7 @@
 
 
 def prep_kernel(
-    feat_hbm, gain_hbm, cot_hbm, pos_hbm, cry_hbm, own_hbm, out_ref,
+    shard_ref, feat_hbm, gain_hbm, cot_hbm, pos_hbm, cry_hbm, own_hbm, out_ref,
     feat_ref, gain_ref, cot_ref, pos_ref, cry_ref, own_ref, sems,
 ):
     fetch(
@@ -100,12 +129,13 @@
         * lax.rsqrt(jnp.mean(hidden * hidden, axis=-1, keepdims=True) + 1e-06)
         * gain_ref[...]
     ).astype(BF)
-    owner = plane_major(own_ref[...]).astype(F32)
+    owner = own_ref[...].astype(F32)
     first = lax.broadcasted_iota(jnp.int32, (rows, rows), 0)
     second = lax.broadcasted_iota(jnp.int32, (rows, rows), 1)
     earlier = (as_column(owner) == owner) & (first < second)
     rank = jnp.sum(jnp.where(earlier, 1.0, 0.0), axis=0, keepdims=True)
-    slot = (owner * 2.0 + rank).astype(jnp.int32)
+    first, second = place_of(own_ref[...], shard_ref[0])
+    slot = (first * 8 + second) * 2 + rank.astype(jnp.int32)
     place = jnp.where(
         slot == lax.broadcasted_iota(jnp.int32, (slots, rows), 0), 1.0, 0.0
     ).astype(BF)
@@ -286,7 +316,7 @@
         out_ref[q] = total
 
 
-def update_kernel(feat_ref, recv_ref, own_ref, out_ref):
+def update_kernel(shard_ref, feat_ref, recv_ref, own_ref, out_ref):
     rows = feat_ref.shape[0]
     planes = recv_ref.shape[0]
     width = 2 * PLANE
@@ -296,7 +326,8 @@
     second = lax.broadcasted_iota(jnp.int32, (rows, rows), 1)
     earlier = (owner == owner_row) & (second < first)
     rank = jnp.sum(jnp.where(earlier, 1.0, 0.0), axis=1, keepdims=True)
-    slot = (owner * 2.0 + rank).astype(jnp.int32)
+    first, second = place_of(owner.astype(jnp.int32), shard_ref[0])
+    slot = (second * PLANE + first) * 2 + rank.astype(jnp.int32)
     pick = jnp.where(
         slot == lax.broadcasted_iota(jnp.int32, (rows, planes * width), 1), 1.0, 0.0
     ).astype(BF)
@@ -337,10 +368,9 @@
     damping,
 ):
     rows, width = features.shape
-    around = ("x", "y", "z")
-    plane = ("x", "y")
-    groups = lax.axis_size(around)
-    planes = lax.axis_size("z")
+    around, plane, column_set = hop_sets()
+    groups = lax.axis_size("dp")
+    planes = groups // PLANE
     members = lax.axis_size("shard")
     capacity = 2 * rows // groups
     slots = groups * capacity
@@ -355,6 +385,7 @@
     owner_row = atom_owner.reshape(1, rows)
     packed = 2 * width + META
     operands = [
+        shard,
         features,
         norm_gain.reshape(1, width),
         cotangent,
@@ -366,12 +397,12 @@
         prep_kernel,
         jax.ShapeDtypeStruct((groups, capacity, packed), BF),
         operands,
-        scratch=[pltpu.VMEM(a.shape, a.dtype) for a in operands]
-        + [pltpu.SemaphoreType.DMA((len(operands),))],
-        specs=[HB] * len(operands),
+        scratch=[pltpu.VMEM(a.shape, a.dtype) for a in operands[1:]]
+        + [pltpu.SemaphoreType.DMA((len(operands) - 1,))],
+        specs=[SM] + [HB] * (len(operands) - 1),
         limit=FULL_VMEM,
     )
-    recv = lax.all_to_all(send, around, split_axis=0, concat_axis=0, tiled=True)
+    recv = exchange(send, around)
     own = recv.reshape(slots, packed)
     kmat, kc, filt, w_in_t = call(
         functools.partial(static_kernel, scale_s=scale_s),
@@ -422,23 +453,24 @@
         [shard, message, got, w_out, grads],
         specs=[SM] + [VM] * 4,
     )
-    recv_plane = lax.all_to_all(back, plane, split_axis=0, concat_axis=0, tiled=True)
+    recv_plane = exchange(back, plane)
     column = call(
         plane_sum_kernel,
         jax.ShapeDtypeStruct((planes, slots // planes + 2 * block, width), BF),
         [recv_plane],
     )
-    recv_column = lax.all_to_all(column, "z", split_axis=0, concat_axis=0, tiled=True)
+    recv_column = exchange(column, column_set)
     share = call(
         functools.partial(column_sum_kernel, norm_factor=norm_factor),
         jax.ShapeDtypeStruct((PLANE, 2 * block, width), BF),
         [recv_column],
     )
-    mine = lax.all_to_all(share, plane, split_axis=0, concat_axis=0, tiled=True)
+    mine = exchange(share, plane)
     updated = call(
         update_kernel,
         jax.ShapeDtypeStruct((rows, width), BF),
-        [features, recv_column, owner_row],
+        [shard, features, recv_column, owner_row],
+        specs=[SM, VM, VM, VM],
         flops=4_000_000_000,
     )
     theirs = lax.ppermute(mine, "shard", swap)
@@ -471,12 +503,7 @@
 
 
 def solution(mesh):
-    axes = Mesh(
-        mesh.devices.reshape(mesh.shape["dp"] // PLANE, 4, PLANE // 4, mesh.shape["shard"]),
-        ("z", "x", "y", "shard"),
-    )
-    dp = ("z", "x", "y")
-    every = (*dp, "shard")
+    every = ("dp", "shard")
     in_specs = (
         P(every, None),
         P(),
@@ -486,9 +513,9 @@
         P(None, every),
         P(every),
         P(every, None),
-        P(None, dp),
-        P(dp),
+        P(None, "dp"),
+        P("dp"),
         P(),
     )
     out_specs = (P(every, None), P(), P())
-    return jax.shard_map(local, mesh=axes, in_specs=in_specs, out_specs=out_specs, check_vma=False)
+    return jax.shard_map(local, mesh=mesh, in_specs=in_specs, out_specs=out_specs, check_vma=False)

time: 105 us -> 100 us (0.952)
  blocking collectives: 46.9 us -> 44.1 us
  waiting for transfers between devices: 18.2 us -> 15.8 us
    all_to_all x3, blocking collectives: 46.9 us -> 44.1 us  [exchange(): lax.all_to_all(array, ('dp', 'shard'), split_axis=0, concat_axis=0, axis_...]
    ppermute x1, starting transfers between devices: 2.58 us -> 5.21 us  [local(): other = lax.ppermute(own, 'shard', swap)]
    all_to_all x1, waiting for transfers between devices: 18.2 us -> 15.8 us  [exchange(): lax.all_to_all(array, ('dp', 'shard'), split_axis=0, concat_axis=0, axis_...]
    ppermute x1, starting transfers between devices: 4.12 us -> 2.45 us  [local(): theirs = lax.ppermute(mine, 'shard', swap)]
where the time goes in v4:
time: 100 us
  blocking collectives  44.1 us (44%)
  starting transfers between devices  24.4 us (24%)
  waiting for transfers between devices  15.8 us (16%)
  Pallas kernels  13.8 us (14%)
    all_to_all x3, blocking collectives, exchange(): lax.all_to_all(array, ('dp', 'shard'), split_axis=0, concat_axis=0, axis_...  44.1 us
    all_to_all x1, starting transfers between devices, exchange(): lax.all_to_all(array, ('dp', 'shard'), split_axis=0, concat_axis=0, axis_...  16.5 us
    all_to_all x1, waiting for transfers between devices, exchange(): lax.all_to_all(array, ('dp', 'shard'), split_axis=0, concat_axis=0, axis_...  15.8 us
    pallas_call x11, Pallas kernels, call(): pl.pallas_call(body, out_shape=out_shape, in_specs=specs if specs is not...  13.8 us
    ppermute x1, starting transfers between devices, local(): other = lax.ppermute(own, 'shard', swap)  5.21 us
    ppermute x1, starting transfers between devices, local(): theirs = lax.ppermute(mine, 'shard', swap)  2.45 us
  transfers between devices with their start and end apart: 4, of which 1 were waited for; matrix products, arithmetic and copies ran while one was open for 0% of the time, Pallas kernels for 6%

profile of v4, /device:TPU:1, one launch (start us, length us, event | category | flops | bytes accessed | tf_op | source)
XLA Modules:
  0.0 100.0 jit_solution(1508504701406200007)
XLA Ops:
  0.6 2.6 %shard_map.130 = bf16[128,2,1152]{2,1,0:T(2,128)(2,1)} custom-call(s32[1]{0:T(128)} %bitcast.shard_ref.refs_0_, bf16[128,512]{1,0:T(8,128)(2,1)} %feat_ref.1, f32[1,512]{1,0:T(1,128)} %bitcast.9, bf16[128,512]{1,0:T(8,128)(2,1)} %cot_hbm.1, bf16[3,128]{1,0:T(4,128)(2,1)} %pos_hbm.1, s32[1,128]{1,0:T(1,128)} %bitcast.11, s32[1,128]{1,0:T(1,128)} %bitcast.6), custom_call_target="tpu_custom_call" | custom-call | flops 1000000 | bytes 1000000 | tf_op jit(solution)/shard_map/pallas_call | solution.py:77
  3.3 0.0 copy-start.6
  3.3 0.0 copy-start.3
  3.3 16.5 %all-to-all-start = ((bf16[128,2,1152]{2,1,0:T(2,128)(2,1)}), bf16[128,2,1152]{2,1,0:T(2,128)(2,1)S(1)}, u32[]{:S(2)}, u32[]{:S(2)}) async-start(bf16[128,2,1152]{2,1,0:T(2,128)(2,1)} %shard_map.130), calls=%async_computation | async-start | bytes 1179648 | tf_op jit(solution)/shard_map/all_to_all | solution.py:65
  19.8 0.0 copy-done.6
  19.8 0.0 copy-start.4
  19.8 0.0 copy-start.5
  19.8 0.1 copy.16.damp_ref
  20.0 0.0 copy-done.3
  20.0 0.5 copy-done.4
  20.5 0.0 copy-done.5
  20.5 0.9 shard_map.131
  21.4 0.0 copy-start
  21.4 15.8 %all-to-all-done = bf16[128,2,1152]{2,1,0:T(2,128)(2,1)S(1)} async-done(((bf16[128,2,1152]{2,1,0:T(2,128)(2,1)}), bf16[128,2,1152]{2,1,0:T(2,128)(2,1)S(1)}, u32[]{:S(2)}, u32[]{:S(2)}) %all-to-all-start) | async-done | bytes 589856 | tf_op jit(solution)/shard_map/all_to_all | solution.py:65
  37.3 0.2 reshape.31.own_ref
  37.5 5.2 %collective-permute-start = (bf16[256,1152]{1,0:T(8,128)(2,1)S(1)}, bf16[256,1152]{1,0:T(8,128)(2,1)S(1)}, u32[]{:S(2)}, u32[]{:S(2)}) collective-permute-start(bf16[256,1152]{1,0:T(8,128)(2,1)S(1)} %reshape.31.own_ref), channel_id=1, source_target_pairs={{0,1},{1,0},{2,3},{3,2},{4,5},{5,4},{6,7},{7,6},{8,9},{9,8},{10,11... | collective-permute-start | bytes 1769480 | tf_op jit(solution)/shard_map/ppermute | solution.py:420
  42.7 0.0 copy-done
  42.7 1.8 %shard_map.132 = (bf16[256,2048]{1,0:T(8,128)(2,1)S(1)}, bf16[512,256]{1,0:T(8,128)(2,1)S(1)}) custom-call(s32[1]{0:T(128)} %bitcast.shard_ref.refs_0_, bf16[256,1152]{1,0:T(8,128)(2,1)S(1)} %reshape.31.own_ref, bf16[128,1024]{1,0:T(8,128)(2,1)S(1)} %get-tuple-element.27.kmat_ref, f32[1,1024]{1,0:T(1,128)S(1)} %get-tuple-element.28.kc_ref, ...), custom_call_target="tpu_custom_call" | custom-call | flops 4000000000 | bytes 1000000 | tf_op jit(solution)/shard_map/pallas_call | solution.py:77
  44.5 0.0 collective-permute-done.oth_ref
  44.5 3.1 %shard_map.133 = (bf16[256,2048]{1,0:T(8,128)(2,1)S(1)}, bf16[512,256]{1,0:T(8,128)(2,1)S(1)}, bf16[256,256]{1,0:T(8,128)(2,1)S(1)}, bf16[256,256]{1,0:T(8,128)(2,1)S(1)}) custom-call(s32[1]{0:T(128)} %bitcast.shard_ref.refs_0_, bf16[256,1152]{1,0:T(8,128)(2,1)S(1)} %collective-permute-done.oth_ref, bf16[256,2048]{1,0:T(8,128)(2,1)S(1)} %get-tuple-element.30.phase_own_ref, ...), custom_call_target="tpu_custom_call" | custom-call | flops 1000000 | bytes 1000000 | tf_op jit(solution)/shard_map/pallas_call | solution.py:77
  47.6 0.3 collective-permute-start.1
  47.9 1.6 %shard_map.134.grad_ref = bf16[512,512]{1,0:T(8,128)(2,1)S(1)} custom-call(bf16[256,1152]{1,0:T(8,128)(2,1)S(1)} %reshape.31.own_ref, bf16[256,1152]{1,0:T(8,128)(2,1)S(1)} %collective-permute-done.oth_ref, bf16[256,2048]{1,0:T(8,128)(2,1)S(1)} %get-tuple-element.30.phase_own_ref, bf16[256,2048]{1,0:T(8,128)(2,1)S(1)} %get-tuple-element.35.phase_oth_ref, ...), custom_call_target="tpu_custom_call" | custom-call | flops 4000000000 | bytes 1000000 | tf_op jit(solution)/shard_map/pallas_call | solution.py:77
  49.5 0.0 collective-permute-done.1.got_ref
  49.5 0.3 shard_map.135
  49.9 17.8 %all_to_all.20.recv_ref = bf16[16,48,512]{2,1,0:T(8,128)(2,1)S(1)} all-to-all(bf16[16,48,512]{2,1,0:T(8,128)(2,1)S(1)} %shard_map.135), channel_id=1, replica_groups={{0,2,4,6,8,10,12,14,16,18,20,22,24,26,28,30},{32,34,36,38,40,42,44,46,4..., dimensions={0} | all-to-all | bytes 1572864 | tf_op jit(solution)/shard_map/all_to_all | solution.py:65
  67.7 0.2 shard_map.136
  67.9 11.4 %all_to_all.21.recv_ref = bf16[8,64,512]{2,1,0:T(8,128)(2,1)S(1)} all-to-all(bf16[8,64,512]{2,1,0:T(8,128)(2,1)S(1)} %shard_map.136), channel_id=1, replica_groups={{0,32,64,96,128,160,192,224},{2,34,66,98,130,162,194,226},{4,36,68,100,..., dimensions={0} | all-to-all | bytes 1048576 | tf_op jit(solution)/shard_map/all_to_all | solution.py:65
  79.4 0.1 shard_map.138
  79.4 0.0 copy-start.1
  79.4 0.0 copy-start.2
  79.4 14.9 %all_to_all.22.refs_1_ = bf16[16,32,512]{2,1,0:T(8,128)(2,1)S(1)} all-to-all(bf16[16,32,512]{2,1,0:T(8,128)(2,1)S(1)} %shard_map.138), channel_id=1, replica_groups={{0,2,4,6,8,10,12,14,16,18,20,22,24,26,28,30},{32,34,36,38,40,42,44,46,4..., dimensions={0} | all-to-all | bytes 1048576 | tf_op jit(solution)/shard_map/all_to_all | solution.py:65
  94.3 2.4 %collective-permute-start.2 = (bf16[16,32,512]{2,1,0:T(8,128)(2,1)S(1)}, bf16[16,32,512]{2,1,0:T(8,128)(2,1)S(1)}, u32[]{:S(2)}, u32[]{:S(2)}) collective-permute-start(bf16[16,32,512]{2,1,0:T(8,128)(2,1)S(1)} %all_to_all.22.refs_1_), channel_id=1, source_target_pairs={{0,1},{1,0},{2,3},{3,2},{4,5},{5,4},{6,7},{7,6},{8,9},{9,8},{10,11... | collective-permute-start | bytes 1572872 | tf_op jit(solution)/shard_map/ppermute | solution.py:476
  96.8 0.0 copy-done.1
  96.8 0.0 copy-done.2
  96.8 1.0 shard_map.137
  97.8 1.1 %shard_map.139 = (f32[512,512]{1,0:T(8,128)}, f32[512,512]{1,0:T(8,128)}) custom-call(s32[1]{0:T(128)} %bitcast.shard_ref.refs_0_, bf16[16,32,512]{2,1,0:T(8,128)(2,1)S(1)} %all_to_all.22.refs_1_), custom_call_target="tpu_custom_call" | custom-call | flops 4000000000 | bytes 1000000 | tf_op jit(solution)/shard_map/pallas_call | solution.py:77
  98.9 0.0 collective-permute-done.2.refs_1_
  98.9 1.1 %shard_map.140 = (f32[512,512]{1,0:T(8,128)}, f32[512,512]{1,0:T(8,128)}) custom-call(s32[1]{0:T(128)} %bitcast.shard_ref.refs_0_, bf16[16,32,512]{2,1,0:T(8,128)(2,1)S(1)} %collective-permute-done.2.refs_1_, f32[512,512]{1,0:T(8,128)} %get-tuple-element.37.refs_2_, f32[512,512]{1,0:T(8,128)} %get-tuple-element.38.refs_3_), custom_call_target="tpu_custom_call", output_to_operand_aliasing={{0}: (2, {}), {1}: (3, {})} | custom-call | flops 1000000 | bytes 1000000 | tf_op jit(solution)/shard_map/pallas_call | solution.py:77
Async XLA Ops:
  3.3 16.5 %copy-start.6 = (f32[512]{0:T(512)S(1)}, f32[512]{0:T(512)}, u32[]{:S(2)}) copy-start(f32[512]{0:T(512)} %param.21) | copy-start | bytes 6148
  3.3 16.7 %copy-start.3 = (bf16[512,512]{1,0:T(8,128)(2,1)S(1)}, bf16[512,512]{1,0:T(8,128)(2,1)}, u32[]{:S(2)}) copy-start(bf16[512,512]{1,0:T(8,128)(2,1)} %w_in_ref.1) | copy-start | bytes 1572868
  3.3 34.0 %all-to-all-start = ((bf16[128,2,1152]{2,1,0:T(2,128)(2,1)}), bf16[128,2,1152]{2,1,0:T(2,128)(2,1)S(1)}, u32[]{:S(2)}, u32[]{:S(2)}) async-start(bf16[128,2,1152]{2,1,0:T(2,128)(2,1)} %shard_map.130), calls=%async_computation | async-start | bytes 1179648 | tf_op jit(solution)/shard_map/all_to_all | solution.py:65
  19.8 0.7 copy-start.4
  19.8 0.7 copy-start.5
  21.4 21.3 %copy-start = (bf16[512,512]{1,0:T(8,128)(2,1)S(1)}, bf16[512,512]{1,0:T(8,128)(2,1)}, u32[]{:S(2)}) copy-start(bf16[512,512]{1,0:T(8,128)(2,1)} %w_out_ref.5) | copy-start | bytes 1572868
  37.5 7.0 %collective-permute-start = (bf16[256,1152]{1,0:T(8,128)(2,1)S(1)}, bf16[256,1152]{1,0:T(8,128)(2,1)S(1)}, u32[]{:S(2)}, u32[]{:S(2)}) collective-permute-start(bf16[256,1152]{1,0:T(8,128)(2,1)S(1)} %reshape.31.own_ref), channel_id=1, source_target_pairs={{0,1},{1,0},{2,3},{3,2},{4,5},{5,4},{6,7},{7,6},{8,9},{9,8},{10,11... | collective-permute-start | bytes 1769480 | tf_op jit(solution)/shard_map/ppermute | solution.py:420
  47.6 1.9 %collective-permute-start.1 = (bf16[256,256]{1,0:T(8,128)(2,1)S(1)}, bf16[256,256]{1,0:T(8,128)(2,1)S(1)}, u32[]{:S(2)}, u32[]{:S(2)}) collective-permute-start(bf16[256,256]{1,0:T(8,128)(2,1)S(1)} %get-tuple-element.34.msg_oth_ref), channel_id=1, source_target_pairs={{0,1},{1,0},{2,3},{3,2},{4,5},{5,4},{6,7},{7,6},{8,9},{9,8},{10,11... | collective-permute-start | bytes 393224 | tf_op jit(solution)/shard_map/ppermute | solution.py:441
  79.4 17.4 %copy-start.1 = (bf16[128,512]{1,0:T(8,128)(2,1)S(1)}, bf16[128,512]{1,0:T(8,128)(2,1)}, u32[]{:S(2)}) copy-start(bf16[128,512]{1,0:T(8,128)(2,1)} %feat_ref.1) | copy-start | bytes 393220
  79.4 17.4 %copy-start.2 = (s32[128,1]{0,1:T(1,128)S(1)}, s32[128,1]{0,1:T(1,128)}, u32[]{:S(2)}) copy-start(s32[128,1]{0,1:T(1,128)} %param.18) | copy-start | bytes 1540
  94.3 4.5 %collective-permute-start.2 = (bf16[16,32,512]{2,1,0:T(8,128)(2,1)S(1)}, bf16[16,32,512]{2,1,0:T(8,128)(2,1)S(1)}, u32[]{:S(2)}, u32[]{:S(2)}) collective-permute-start(bf16[16,32,512]{2,1,0:T(8,128)(2,1)S(1)} %all_to_all.22.refs_1_), channel_id=1, source_target_pairs={{0,1},{1,0},{2,3},{3,2},{4,5},{5,4},{6,7},{7,6},{8,9},{9,8},{10,11... | collective-permute-start | bytes 1572872 | tf_op jit(solution)/shard_map/ppermute | solution.py:476

commit v5 on v4

--- a/solution.py
+++ b/solution.py
@@ -16,20 +16,18 @@
 META = 128
 
 COS_POLY = (
-    0.9999992251396179,
-    -19.738981246948242,
-    64.92865753173828,
-    -85.27162170410156,
-    58.79049301147461,
-    -21.07110595703125,
+    1.4142135381698608,
+    -6.978850841522217,
+    5.739460468292236,
+    -1.883557915687561,
+    0.3106880187988281,
 )
 SIN_POLY = (
-    6.283185005187988,
-    -41.341590881347656,
-    81.59994506835938,
-    -76.61447143554688,
-    41.3428840637207,
-    -12.471243858337402,
+    4.442883014678955,
+    -7.308245658874512,
+    3.606354236602783,
+    -0.8461116552352905,
+    0.1098245158791542,
 )
 
 VM = pl.BlockSpec(memory_space=pltpu.VMEM)
@@ -98,37 +96,21 @@
     return jnp.sum(jnp.where(diagonal, row, 0.0), axis=1, keepdims=True)
 
 
-def fetch(pairs, sems):
-    copies = [pltpu.make_async_copy(src, dst, sems.at[i]) for i, (src, dst) in enumerate(pairs)]
-    for copy in copies:
-        copy.start()
-    for copy in copies:
-        copy.wait()
-
-
 def prep_kernel(
-    shard_ref, feat_hbm, gain_hbm, cot_hbm, pos_hbm, cry_hbm, own_hbm, out_ref,
-    feat_ref, gain_ref, cot_ref, pos_ref, cry_ref, own_ref, sems,
-):
-    fetch(
-        (
-            (own_hbm, own_ref),
-            (feat_hbm, feat_ref),
-            (cot_hbm, cot_ref),
-            (gain_hbm, gain_ref),
-            (pos_hbm, pos_ref),
-            (cry_hbm, cry_ref),
-        ),
-        sems,
-    )
+    shard_ref, feat_hbm, gain_hbm, cot_hbm, pos_hbm, cry_hbm, own_hbm, out_hbm,
+    feat_ref, gain_ref, cot_ref, pos_ref, cry_ref, own_ref, sems, stage_ref, out_sems,
+):
+    sources = (feat_hbm, gain_hbm, cot_hbm, pos_hbm, cry_hbm, own_hbm)
+    targets = (feat_ref, gain_ref, cot_ref, pos_ref, cry_ref, own_ref)
+    feat_in, gain_in, cot_in, pos_in, cry_in, own_in = copies = [
+        pltpu.make_async_copy(src, dst, sems.at[i])
+        for i, (src, dst) in enumerate(zip(sources, targets))
+    ]
+    for i in (5, 2, 0, 1, 3, 4):
+        copies[i].start()
     rows, width = feat_ref.shape
-    slots = out_ref.shape[0] * out_ref.shape[1]
-    hidden = feat_ref[...].astype(F32)
-    normed = (
-        hidden
-        * lax.rsqrt(jnp.mean(hidden * hidden, axis=-1, keepdims=True) + 1e-06)
-        * gain_ref[...]
-    ).astype(BF)
+    slots = out_hbm.shape[0] * out_hbm.shape[1]
+    own_in.wait()
     owner = own_ref[...].astype(F32)
     first = lax.broadcasted_iota(jnp.int32, (rows, rows), 0)
     second = lax.broadcasted_iota(jnp.int32, (rows, rows), 1)
@@ -139,6 +121,30 @@
     place = jnp.where(
         slot == lax.broadcasted_iota(jnp.int32, (slots, rows), 0), 1.0, 0.0
     ).astype(BF)
+    sent = []
+
+    def send(first, part):
+        span = slice(first, first + part.shape[1])
+        stage_ref[:, :, span] = part.reshape(slots // 2, 2, part.shape[1]).astype(BF)
+        copy = pltpu.make_async_copy(
+            stage_ref.at[:, :, span], out_hbm.at[:, :, span], out_sems.at[len(sent)]
+        )
+        copy.start()
+        sent.append(copy)
+
+    cot_in.wait()
+    send(width, dot(place, cot_ref[...], 1, 0))
+    feat_in.wait()
+    gain_in.wait()
+    hidden = feat_ref[...].astype(F32)
+    normed = (
+        hidden
+        * lax.rsqrt(jnp.mean(hidden * hidden, axis=-1, keepdims=True) + 1e-06)
+        * gain_ref[...]
+    ).astype(BF)
+    send(0, dot(place, normed, 1, 0))
+    pos_in.wait()
+    cry_in.wait()
     meta = jnp.concatenate(
         [
             pos_ref[...].astype(F32),
@@ -147,22 +153,21 @@
         ],
         axis=0,
     ).astype(BF)
-    first = 0
-    for part in (dot(place, normed, 1, 0), dot(place, cot_ref[...], 1, 0), dot(place, meta, 1, 1)):
-        last = first + part.shape[1]
-        out_ref[:, :, first:last] = part.reshape(slots // 2, 2, part.shape[1]).astype(BF)
-        first = last
+    send(2 * width, dot(place, meta, 1, 1))
+    for copy in sent:
+        copy.wait()
 
 
 def static_kernel(
-    shard_ref, k_ref, kc_ref, damp_ref, w_in_ref, kmat_ref, kcf_ref, filt_ref, w_in_t_ref, scale_s
+    shard_ref, k_ref, kc_ref, damp_ref, w_in_ref, kmat_ref, kone_ref, filt_ref, w_in_t_ref, scale_s
 ):
     half = filt_ref.shape[0]
     start = pl.multiple_of(shard_ref[0] * half, half)
     kf = k_ref[...].astype(F32)
     kmat_ref[...] = jnp.zeros(kmat_ref.shape, BF)
     kmat_ref[0:16, :] = jnp.concatenate([kf, jnp.zeros((13, kf.shape[1]), F32)], axis=0).astype(BF)
-    kcf_ref[...] = kc_ref[...].astype(F32)
+    crystal = lax.broadcasted_iota(jnp.int32, kone_ref.shape, 0)
+    kone_ref[...] = jnp.where(kc_ref[...] == crystal, 1.0, 0.0).astype(BF)
     ksq = kf[0:1] * kf[0:1] + kf[1:2] * kf[1:2] + kf[2:3] * kf[2:3]
     scale = scale_s / (1.0 + ksq)
     step = 32
@@ -177,35 +182,32 @@
     w_in_t_ref[...] = w_in_ref[:, pl.ds(start, half)].T
 
 
-def fill_phase(rows_ref, kmat_ref, kc_ref, turn_ref, phase_ref):
-    slots = rows_ref.shape[0]
-    kcount = kc_ref.shape[1]
+def start_phase(rows_ref, kmat_ref, kone_ref, turn_ref, same_ref):
     first = rows_ref.shape[1] - META
-    turn_ref[...] = dot(rows_ref[:, first:], kmat_ref[...], 1, 0)
-    tile_rows, tile_cols = 16, 512
-
-    def tile(i, carry):
-        at = pl.ds(pl.multiple_of(i * tile_rows, tile_rows), tile_rows)
-        crystal = rows_ref[at, first:].astype(F32)[:, 3:4]
-        for j in range(kcount // tile_cols):
-            span = slice(j * tile_cols, (j + 1) * tile_cols)
-            turn = turn_ref[at, span]
-            rest = turn - jnp.floor(turn + 0.5)
-            square = rest * rest
-            cosine = jnp.full(square.shape, COS_POLY[-1], F32)
-            for c in COS_POLY[-2::-1]:
-                cosine = cosine * square + c
-            sine = jnp.full(square.shape, SIN_POLY[-1], F32)
-            for c in SIN_POLY[-2::-1]:
-                sine = sine * square + c
-            matched = crystal == kc_ref[:, span]
-            phase_ref[at, span] = jnp.where(matched, cosine, 0.0).astype(BF)
-            phase_ref[at, kcount + j * tile_cols : kcount + (j + 1) * tile_cols] = jnp.where(
-                matched, sine * rest, 0.0
-            ).astype(BF)
-        return carry
-
-    lax.fori_loop(0, slots // tile_rows, tile, 0)
+    meta = rows_ref[:, first:]
+    turn_ref[...] = dot(meta, kmat_ref[...], 1, 0)
+    lane = lax.broadcasted_iota(jnp.int32, meta.shape, 1).astype(F32)
+    one = jnp.where(meta.astype(F32)[:, 3:4] == lane, 1.0, 0.0).astype(BF)
+    same_ref[...] = dot(one, kone_ref[...], 1, 0)
+
+
+def phase_tile(turn_ref, same_ref, phase_ref, at, first, count):
+    span = slice(first, first + count)
+    kcount = turn_ref.shape[1]
+    turn = turn_ref[at, span]
+    same = same_ref[at, span]
+    rest = turn - jnp.floor(turn + 0.5)
+    square = rest * rest
+    cosine = square * COS_POLY[-1] + COS_POLY[-2]
+    for c in COS_POLY[-3::-1]:
+        cosine = cosine * square + c
+    sine = square * SIN_POLY[-1] + SIN_POLY[-2]
+    for c in SIN_POLY[-3::-1]:
+        sine = sine * square + c
+    sine = sine * rest
+    held = sine * same
+    phase_ref[at, span] = (same - held * sine).astype(BF)
+    phase_ref[at, kcount + first : kcount + first + count] = (held * cosine).astype(BF)
 
 
 def fill_stack(rows_ref, w_in_t_ref, w_out_half, stack_ref):
@@ -220,54 +222,74 @@
 
 
 def own_kernel(
-    shard_ref, own_ref, kmat_ref, kc_ref, w_in_t_ref, w_out_ref, phase_ref, stack_ref, turn_ref
-):
+    shard_ref, own_ref, kmat_ref, kone_ref, w_in_t_ref, w_out_ref, phase_ref, stack_ref, part_ref,
+    turn_ref, same_ref,
+):
+    start_phase(own_ref, kmat_ref, kone_ref, turn_ref, same_ref)
     fill_stack(own_ref, w_in_t_ref, half_of(w_out_ref, shard_ref, w_in_t_ref.shape[0]), stack_ref)
-    fill_phase(own_ref, kmat_ref, kc_ref, turn_ref, phase_ref)
-
-
-def there_and_back(stacks, phases, rows, filt_ref, scaled_ref, scale_m):
-    kcount = filt_ref.shape[1]
-    block = 512
-    for j in range(2 * kcount // block):
-        span = slice(j * block, (j + 1) * block)
-        lo = (j * block) % kcount
-        structure = dot(stacks[0][rows, :], phases[0][:, span], 1, 0)
-        structure += dot(stacks[1][rows, :], phases[1][:, span], 1, 0)
-        scaled_ref[:, span] = (structure * filt_ref[:, lo : lo + block]).astype(BF)
-    return [
-        (scale_m * dot(scaled_ref[...], phase[...], 1, 1)).astype(BF) for phase in phases
-    ]
+    slots, kcount = turn_ref.shape
+    chunk = 256
+
+    def structure(first):
+        for at in (first, kcount + first):
+            span = slice(at, at + chunk)
+            part_ref[:, span] = dot(stack_ref[...], phase_ref[:, span], 1, 0)
+
+    for first in range(0, kcount, chunk):
+        if first:
+            structure(first - chunk)
+        for row in range(0, slots, 16):
+            phase_tile(turn_ref, same_ref, phase_ref, slice(row, row + 16), first, chunk)
+    structure(kcount - chunk)
 
 
 def forward_kernel(
-    shard_ref, oth_ref, phase_own_ref, stack_own_ref, kmat_ref, kc_ref, filt_ref, w_in_t_ref,
+    shard_ref, oth_ref, part_ref, phase_own_ref, kmat_ref, kone_ref, filt_ref, w_in_t_ref,
     w_out_ref,
     phase_ref, stack_ref, msg_own_ref, msg_oth_ref,
-    turn_ref, scaled_ref, scale_m,
+    turn_ref, same_ref, scaled_ref, scale_m,
 ):
     half = w_in_t_ref.shape[0]
     fill_stack(oth_ref, w_in_t_ref, half_of(w_out_ref, shard_ref, half), stack_ref)
-    fill_phase(oth_ref, kmat_ref, kc_ref, turn_ref, phase_ref)
-    msg_own_ref[...], msg_oth_ref[...] = there_and_back(
-        (stack_own_ref, stack_ref), (phase_own_ref, phase_ref), slice(0, half), filt_ref,
-        scaled_ref, scale_m,
-    )
+    start_phase(oth_ref, kmat_ref, kone_ref, turn_ref, same_ref)
+    slots, kcount = turn_ref.shape
+    chunk = 512
+
+    def structure(first):
+        filt = filt_ref[:, first : first + chunk]
+        for at in (first, kcount + first):
+            span = slice(at, at + chunk)
+            total = part_ref[0:half, span] + dot(stack_ref[0:half, :], phase_ref[:, span], 1, 0)
+            scaled_ref[:, span] = (total * filt).astype(BF)
+
+    for first in range(0, kcount, chunk):
+        if first:
+            structure(first - chunk)
+        for row in range(0, slots, 16):
+            phase_tile(turn_ref, same_ref, phase_ref, slice(row, row + 16), first, chunk)
+    structure(kcount - chunk)
+    for phase, out in ((phase_own_ref, msg_own_ref), (phase_ref, msg_oth_ref)):
+        out[...] = (scale_m * dot(scaled_ref[...], phase[...], 1, 1)).astype(BF)
 
 
 def backward_kernel(
-    own_ref, oth_ref, phase_own_ref, phase_oth_ref, stack_own_ref, stack_oth_ref, msg_own_ref,
-    msg_oth_ref, filt_ref, grad_ref, scaled_ref, scale_m,
+    own_ref, oth_ref, part_ref, phase_own_ref, phase_oth_ref, stack_ref, msg_own_ref, msg_oth_ref,
+    filt_ref, grad_ref, scaled_ref, scale_m,
 ):
     half = msg_own_ref.shape[0]
     width = grad_ref.shape[1]
+    kcount = filt_ref.shape[1]
+    chunk = 512
+    for at in range(0, 2 * kcount, chunk):
+        span = slice(at, at + chunk)
+        filt = filt_ref[:, at % kcount : at % kcount + chunk]
+        total = part_ref[half:, span] + dot(stack_ref[half:, :], phase_oth_ref[:, span], 1, 0)
+        scaled_ref[:, span] = (total * filt).astype(BF)
     total = dot(msg_own_ref[...], own_ref[:, width : 2 * width], 1, 0)
     total += dot(msg_oth_ref[...], oth_ref[:, width : 2 * width], 1, 0)
     grad_ref[0:half, :] = total.astype(BF)
-    back_own, back_oth = there_and_back(
-        (stack_own_ref, stack_oth_ref), (phase_own_ref, phase_oth_ref), slice(half, 2 * half),
-        filt_ref, scaled_ref, scale_m,
-    )
+    back_own = (scale_m * dot(scaled_ref[...], phase_own_ref[...], 1, 1)).astype(BF)
+    back_oth = (scale_m * dot(scaled_ref[...], phase_oth_ref[...], 1, 1)).astype(BF)
     total = dot(back_own, own_ref[:, 0:width], 1, 0)
     total += dot(back_oth, oth_ref[:, 0:width], 1, 0)
     grad_ref[half:, :] = total.astype(BF)
@@ -316,7 +338,27 @@
         out_ref[q] = total
 
 
-def update_kernel(shard_ref, feat_ref, recv_ref, own_ref, out_ref):
+def place_half(ref, member, grad_in_hbm, grad_out_hbm, in_ref, out_ref, sems):
+    block = ref.shape[1] // 2
+    half = PLANE * block
+    start = pl.multiple_of(member * half, half)
+    into = jnp.concatenate([ref[q, block:] for q in range(PLANE)], axis=0).astype(F32)
+    in_ref[...] = into.T
+    cols = pltpu.make_async_copy(in_ref, grad_in_hbm.at[:, pl.ds(start, half)], sems.at[0])
+    cols.start()
+    for q in range(PLANE):
+        out_ref[q * block : (q + 1) * block, :] = ref[q, 0:block].astype(F32)
+    rows = pltpu.make_async_copy(out_ref, grad_out_hbm.at[pl.ds(start, half), :], sems.at[1])
+    rows.start()
+    return cols, rows
+
+
+def own_final_kernel(
+    shard_ref, feat_ref, recv_ref, own_ref, half_ref,
+    new_hbm, grad_in_hbm, grad_out_hbm,
+    in_ref, out_ref, sems, new_ref, new_sem,
+):
+    copies = place_half(half_ref, shard_ref[0], grad_in_hbm, grad_out_hbm, in_ref, out_ref, sems)
     rows = feat_ref.shape[0]
     planes = recv_ref.shape[0]
     width = 2 * PLANE
@@ -332,26 +374,20 @@
         slot == lax.broadcasted_iota(jnp.int32, (rows, planes * width), 1), 1.0, 0.0
     ).astype(BF)
     change = jnp.concatenate([recv_ref[z, 0:width] for z in range(planes)], axis=0)
-    out_ref[...] = (feat_ref[...].astype(F32) + dot(pick, change, 1, 0)).astype(BF)
-
-
-def final_kernel(*refs, member):
-    shard_ref, ref = refs[:2]
-    grad_in_hbm, grad_out_hbm, in_ref, out_ref, sems = refs[-5:]
-    block = ref.shape[1] // 2
-    half = PLANE * block
-    which = shard_ref[0] if member == 0 else 1 - shard_ref[0]
-    start = pl.multiple_of(which * half, half)
-    for q in range(PLANE):
-        out_ref[q * block : (q + 1) * block, :] = ref[q, 0:block].astype(F32)
-    rows = pltpu.make_async_copy(out_ref, grad_out_hbm.at[pl.ds(start, half), :], sems.at[0])
-    rows.start()
-    into = jnp.concatenate([ref[q, block:] for q in range(PLANE)], axis=0).astype(F32)
-    in_ref[...] = into.T
-    cols = pltpu.make_async_copy(in_ref, grad_in_hbm.at[:, pl.ds(start, half)], sems.at[1])
-    cols.start()
-    rows.wait()
-    cols.wait()
+    new_ref[...] = (feat_ref[...].astype(F32) + dot(pick, change, 1, 0)).astype(BF)
+    new = pltpu.make_async_copy(new_ref, new_hbm, new_sem)
+    new.start()
+    for copy in (*copies, new):
+        copy.wait()
+
+
+def other_final_kernel(
+    shard_ref, half_ref, _grad_in, _grad_out, grad_in_hbm, grad_out_hbm, in_ref, out_ref, sems
+):
+    for copy in place_half(
+        half_ref, 1 - shard_ref[0], grad_in_hbm, grad_out_hbm, in_ref, out_ref, sems
+    ):
+        copy.wait()
 
 
 def local(
@@ -398,17 +434,22 @@
         jax.ShapeDtypeStruct((groups, capacity, packed), BF),
         operands,
         scratch=[pltpu.VMEM(a.shape, a.dtype) for a in operands[1:]]
-        + [pltpu.SemaphoreType.DMA((len(operands) - 1,))],
+        + [
+            pltpu.SemaphoreType.DMA((len(operands) - 1,)),
+            pltpu.VMEM((groups, capacity, packed), BF),
+            pltpu.SemaphoreType.DMA((3,)),
+        ],
         specs=[SM] + [HB] * (len(operands) - 1),
+        outs=HB,
         limit=FULL_VMEM,
     )
     recv = exchange(send, around)
     own = recv.reshape(slots, packed)
-    kmat, kc, filt, w_in_t = call(
+    kmat, kone, filt, w_in_t = call(
         functools.partial(static_kernel, scale_s=scale_s),
         (
             jax.ShapeDtypeStruct((META, kcount), BF),
-            jax.ShapeDtypeStruct((1, kcount), F32),
+            jax.ShapeDtypeStruct((META, kcount), BF),
             jax.ShapeDtypeStruct((half, kcount), F32),
             jax.ShapeDtypeStruct((half, width), BF),
         ),
@@ -416,33 +457,33 @@
         specs=[SM, VM, VM, VM, VM],
         flops=4_000_000_000,
     )
-    own, kmat, kc, filt, w_in_t = lax.optimization_barrier((own, kmat, kc, filt, w_in_t))
+    own, kmat, kone, filt, w_in_t = lax.optimization_barrier((own, kmat, kone, filt, w_in_t))
     other = lax.ppermute(own, "shard", swap)
     phase_shape = jax.ShapeDtypeStruct((slots, 2 * kcount), BF)
     stack_shape = jax.ShapeDtypeStruct((2 * half, slots), BF)
     message_shape = jax.ShapeDtypeStruct((half, slots), BF)
     turn = pltpu.VMEM((slots, kcount), F32)
     scaled = pltpu.VMEM((half, 2 * kcount), BF)
-    phase_own, stack_own = call(
+    phase_own, _, part = call(
         own_kernel,
-        (phase_shape, stack_shape),
-        [shard, own, kmat, kc, w_in_t, w_out],
-        scratch=[turn],
+        (phase_shape, stack_shape, jax.ShapeDtypeStruct((2 * half, 2 * kcount), F32)),
+        [shard, own, kmat, kone, w_in_t, w_out],
+        scratch=[turn, turn],
         specs=[SM] + [VM] * 5,
         flops=4_000_000_000,
     )
     phase_oth, stack_oth, message, message_oth = call(
         functools.partial(forward_kernel, scale_m=scale_m),
         (phase_shape, stack_shape, message_shape, message_shape),
-        [shard, other, phase_own, stack_own, kmat, kc, filt, w_in_t, w_out],
-        scratch=[turn, scaled],
+        [shard, other, part, phase_own, kmat, kone, filt, w_in_t, w_out],
+        scratch=[turn, turn, scaled],
         specs=[SM] + [VM] * 8,
     )
     got = lax.ppermute(message_oth, "shard", swap)
     grads = call(
         functools.partial(backward_kernel, scale_m=scale_m),
         jax.ShapeDtypeStruct((2 * half, width), BF),
-        [own, other, phase_own, phase_oth, stack_own, stack_oth, message, message_oth, filt],
+        [own, other, part, phase_own, phase_oth, stack_oth, message, message_oth, filt],
         scratch=[scaled],
         flops=4_000_000_000,
     )
@@ -466,38 +507,30 @@
         [recv_column],
     )
     mine = exchange(share, plane)
-    updated = call(
-        update_kernel,
-        jax.ShapeDtypeStruct((rows, width), BF),
-        [shard, features, recv_column, owner_row],
-        specs=[SM, VM, VM, VM],
-        flops=4_000_000_000,
-    )
     theirs = lax.ppermute(mine, "shard", swap)
     grads = (jax.ShapeDtypeStruct((width, width), F32),) * 2
-    placing = dict(
-        outs=(HB, HB),
-        scratch=[
-            pltpu.VMEM((width, half), F32),
-            pltpu.VMEM((half, width), F32),
-            pltpu.SemaphoreType.DMA((2,)),
-        ],
-    )
-    first = call(
-        functools.partial(final_kernel, member=0),
-        grads,
-        [shard, mine],
-        specs=[SM, VM],
+    placing = [
+        pltpu.VMEM((width, half), F32),
+        pltpu.VMEM((half, width), F32),
+        pltpu.SemaphoreType.DMA((2,)),
+    ]
+    updated, *first = call(
+        own_final_kernel,
+        (jax.ShapeDtypeStruct((rows, width), BF), *grads),
+        [shard, features, recv_column, owner_row, mine],
+        scratch=[*placing, pltpu.VMEM((rows, width), BF), pltpu.SemaphoreType.DMA],
+        specs=[SM, VM, VM, VM, VM],
+        outs=(HB, HB, HB),
         flops=4_000_000_000,
-        **placing,
     )
     grad_w_in, grad_w_out = call(
-        functools.partial(final_kernel, member=1),
+        other_final_kernel,
         grads,
         [shard, theirs, *first],
+        scratch=placing,
         specs=[SM, VM, HB, HB],
+        outs=(HB, HB),
         aliases={2: 0, 3: 1},
-        **placing,
     )
     return (updated, grad_w_in, grad_w_out)
 

time: 100 us -> 98.7 us (0.987)
  local copies, waits for them, and re-layouts: 0.94 us -> 3.5 us
  waiting for transfers between devices: 15.8 us -> 13.5 us
  Pallas kernels: 13.8 us -> 12.3 us
    all_to_all x1, waiting for transfers between devices: 15.8 us -> 13.3 us  [exchange(): lax.all_to_all(array, ('dp', 'shard'), split_axis=0, concat_axis=0, axis_...]
    unnamed x14 -> x12, local copies, waits for them, and re-layouts: 0.58 us -> 2.46 us
    pallas_call x11 -> x10, Pallas kernels: 13.8 us -> 12.3 us  [call(): pl.pallas_call(body, out_shape=out_shape, in_specs=specs if specs is not...]
  transfers between devices with their start and end apart: 4 -> 4, of which waited for: 1 -> 2; matrix products, arithmetic and copies ran while one was open for 0% -> 1% of each run, Pallas kernels for 6% -> 6%
where the time goes in v5:
time: 98.7 us; the launch traced here: 98.2 us
  blocking collectives  44 us (45%)
  starting transfers between devices  24.2 us (25%)
  waiting for transfers between devices  13.5 us (14%)
  Pallas kernels  12.3 us (12%)
  local copies, waits for them, and re-layouts  3.5 us (4%)
    all_to_all x3, blocking collectives, exchange(): lax.all_to_all(array, ('dp', 'shard'), split_axis=0, concat_axis=0, axis_...  44 us
    all_to_all x1, starting transfers between devices, exchange(): lax.all_to_all(array, ('dp', 'shard'), split_axis=0, concat_axis=0, axis_...  16.3 us
    all_to_all x1, waiting for transfers between devices, exchange(): lax.all_to_all(array, ('dp', 'shard'), split_axis=0, concat_axis=0, axis_...  13.3 us
    pallas_call x10, Pallas kernels, call(): pl.pallas_call(body, out_shape=out_shape, in_specs=specs if specs is not...  12.3 us
    ppermute x1, starting transfers between devices, local(): other = lax.ppermute(own, 'shard', swap)  5.21 us
    unnamed x12, local copies, waits for them, and re-layouts  2.46 us
    ppermute x1, starting transfers between devices, local(): theirs = lax.ppermute(mine, 'shard', swap)  2.45 us
  transfers between devices with their start and end apart: 4, of which 2 were waited for; matrix products, arithmetic and copies ran while one was open for 1% of the time, Pallas kernels for 6%

profile of v5, /device:TPU:1, one launch (start us, length us, event | category | flops | bytes accessed | tf_op | source)
XLA Modules:
  0.0 98.2 jit_solution(10788830471901807965)
XLA Ops:
  0.6 2.7 %shard_map.130 = bf16[128,2,1152]{2,1,0:T(2,128)(2,1)} custom-call(s32[1]{0:T(128)} %bitcast.shard_ref, bf16[128,512]{1,0:T(8,128)(2,1)} %feat_ref.1, f32[1,512]{1,0:T(1,128)} %bitcast.9, bf16[128,512]{1,0:T(8,128)(2,1)} %cot_hbm.1, bf16[3,128]{1,0:T(4,128)(2,1)} %pos_hbm.1, s32[1,128]{1,0:T(1,128)} %bitcast.11, s32[1,128]{1,0:T(1,128)} %bitcast.6), custom_call_target="tpu_custom_call" | custom-call | flops 1000000 | bytes 1000000 | tf_op jit(solution)/shard_map/pallas_call | solution.py:75
  3.3 16.3 %all-to-all-start = ((bf16[128,2,1152]{2,1,0:T(2,128)(2,1)}), bf16[128,2,1152]{2,1,0:T(2,128)(2,1)S(1)}, u32[]{:S(2)}, u32[]{:S(2)}) async-start(bf16[128,2,1152]{2,1,0:T(2,128)(2,1)} %shard_map.130), calls=%async_computation | async-start | bytes 1179648 | tf_op jit(solution)/shard_map/all_to_all | solution.py:63
  19.7 0.8 copy.16.damp_ref
  20.5 0.0 copy-start.3
  20.5 1.0 %copy-done.3 = bf16[512,512]{1,0:T(8,128)(2,1)S(1)} copy-done((bf16[512,512]{1,0:T(8,128)(2,1)S(1)}, bf16[512,512]{1,0:T(8,128)(2,1)}, u32[]{:S(2)}) %copy-start.3) | copy-done | bytes 524312
  21.5 0.0 copy-start.4
  21.5 0.7 copy-done.4
  22.2 0.0 copy-start.5
  22.3 0.7 copy-done.5
  22.9 0.0 copy-start
  22.9 1.0 shard_map.131
  23.9 13.3 %all-to-all-done = bf16[128,2,1152]{2,1,0:T(2,128)(2,1)S(1)} async-done(((bf16[128,2,1152]{2,1,0:T(2,128)(2,1)}), bf16[128,2,1152]{2,1,0:T(2,128)(2,1)S(1)}, u32[]{:S(2)}, u32[]{:S(2)}) %all-to-all-start) | async-done | bytes 589856 | tf_op jit(solution)/shard_map/all_to_all | solution.py:63
  37.1 0.2 reshape.31.own_ref
  37.4 5.2 %collective-permute-start = (bf16[256,1152]{1,0:T(8,128)(2,1)S(1)}, bf16[256,1152]{1,0:T(8,128)(2,1)S(1)}, u32[]{:S(2)}, u32[]{:S(2)}) collective-permute-start(bf16[256,1152]{1,0:T(8,128)(2,1)S(1)} %reshape.31.own_ref), channel_id=1, source_target_pairs={{0,1},{1,0},{2,3},{3,2},{4,5},{5,4},{6,7},{7,6},{8,9},{9,8},{10,11... | collective-permute-start | bytes 1769480 | tf_op jit(solution)/shard_map/ppermute | solution.py:461
  42.6 0.0 copy-done
  42.6 1.9 %shard_map.132 = (bf16[256,2048]{1,0:T(8,128)(2,1)S(1)}, bf16[512,256]{1,0:T(8,128)(2,1)}, f32[512,2048]{1,0:T(8,128)S(1)}) custom-call(s32[1]{0:T(128)} %bitcast.shard_ref, bf16[256,1152]{1,0:T(8,128)(2,1)S(1)} %reshape.31.own_ref, bf16[128,1024]{1,0:T(8,128)(2,1)S(1)} %get-tuple-element.28.kmat_ref, bf16[128,1024]{1,0:T(8,128)(2,1)S(1)} %get-tuple-element.29.kone_ref, ...), custom_call_target="tpu_custom_call" | custom-call | flops 4000000000 | bytes 1000000 | tf_op jit(solution)/shard_map/pallas_call | solution.py:75
  44.5 0.0 collective-permute-done.oth_ref
  44.5 2.3 %shard_map.133 = (bf16[256,2048]{1,0:T(8,128)(2,1)S(1)}, bf16[512,256]{1,0:T(8,128)(2,1)S(1)}, bf16[256,256]{1,0:T(8,128)(2,1)S(1)}, bf16[256,256]{1,0:T(8,128)(2,1)S(1)}) custom-call(s32[1]{0:T(128)} %bitcast.shard_ref, bf16[256,1152]{1,0:T(8,128)(2,1)S(1)} %collective-permute-done.oth_ref, f32[512,2048]{1,0:T(8,128)S(1)} %get-tuple-element.31.part_ref, ...), custom_call_target="tpu_custom_call" | custom-call | flops 1000000 | bytes 1000000 | tf_op jit(solution)/shard_map/pallas_call | solution.py:75
  46.8 0.2 collective-permute-start.1
  47.0 1.5 %shard_map.134.grad_ref = bf16[512,512]{1,0:T(8,128)(2,1)S(1)} custom-call(bf16[256,1152]{1,0:T(8,128)(2,1)S(1)} %reshape.31.own_ref, bf16[256,1152]{1,0:T(8,128)(2,1)S(1)} %collective-permute-done.oth_ref, f32[512,2048]{1,0:T(8,128)S(1)} %get-tuple-element.31.part_ref, bf16[256,2048]{1,0:T(8,128)(2,1)S(1)} %get-tuple-element.32.phase_own_ref, ...), custom_call_target="tpu_custom_call" | custom-call | flops 4000000000 | bytes 1000000 | tf_op jit(solution)/shard_map/pallas_call | solution.py:75
  48.5 0.0 copy-start.1
  48.5 0.0 copy-start.2
  48.5 0.0 collective-permute-done.1.got_ref
  48.5 0.3 shard_map.135
  48.8 17.8 %all_to_all.20.recv_ref = bf16[16,48,512]{2,1,0:T(8,128)(2,1)S(1)} all-to-all(bf16[16,48,512]{2,1,0:T(8,128)(2,1)S(1)} %shard_map.135), channel_id=1, replica_groups={{0,2,4,6,8,10,12,14,16,18,20,22,24,26,28,30},{32,34,36,38,40,42,44,46,4..., dimensions={0} | all-to-all | bytes 1572864 | tf_op jit(solution)/shard_map/all_to_all | solution.py:63
  66.6 0.2 shard_map.136
  66.9 11.4 %all_to_all.21.recv_ref = bf16[8,64,512]{2,1,0:T(8,128)(2,1)S(1)} all-to-all(bf16[8,64,512]{2,1,0:T(8,128)(2,1)S(1)} %shard_map.136), channel_id=1, replica_groups={{0,32,64,96,128,160,192,224},{2,34,66,98,130,162,194,226},{4,36,68,100,..., dimensions={0} | all-to-all | bytes 1048576 | tf_op jit(solution)/shard_map/all_to_all | solution.py:63
  78.3 0.1 shard_map.137
  78.4 14.8 %all_to_all.22.half_ref = bf16[16,32,512]{2,1,0:T(8,128)(2,1)S(1)} all-to-all(bf16[16,32,512]{2,1,0:T(8,128)(2,1)S(1)} %shard_map.137), channel_id=1, replica_groups={{0,2,4,6,8,10,12,14,16,18,20,22,24,26,28,30},{32,34,36,38,40,42,44,46,4..., dimensions={0} | all-to-all | bytes 1048576 | tf_op jit(solution)/shard_map/all_to_all | solution.py:63
  93.1 2.5 %collective-permute-start.2 = (bf16[16,32,512]{2,1,0:T(8,128)(2,1)S(1)}, bf16[16,32,512]{2,1,0:T(8,128)(2,1)S(1)}, u32[]{:S(2)}, u32[]{:S(2)}) collective-permute-start(bf16[16,32,512]{2,1,0:T(8,128)(2,1)S(1)} %all_to_all.22.half_ref), channel_id=1, source_target_pairs={{0,1},{1,0},{2,3},{3,2},{4,5},{5,4},{6,7},{7,6},{8,9},{9,8},{10,11... | collective-permute-start | bytes 1572872 | tf_op jit(solution)/shard_map/ppermute | solution.py:510
  95.6 0.0 copy-done.1
  95.6 0.0 copy-done.2
  95.6 1.3 %shard_map.138 = (bf16[128,512]{1,0:T(8,128)(2,1)}, f32[512,512]{1,0:T(8,128)}, f32[512,512]{1,0:T(8,128)}) custom-call(s32[1]{0:T(128)} %bitcast.shard_ref, bf16[128,512]{1,0:T(8,128)(2,1)S(1)} %copy-done.1, bf16[8,64,512]{2,1,0:T(8,128)(2,1)S(1)} %all_to_all.21.recv_ref, s32[1,128]{1,0:T(1,128)S(1)} %bitcast.7, bf16[16,32,512]{2,1,0:T(8,128)(2,1)S(1)} %all_to_all.22.half_ref), custom_call_target="tpu_custom_call" | custom-call | flops 4000000000 | bytes 1000000 | tf_op jit(solution)/shard_map/pallas_call | solution.py:75
  96.9 0.2 collective-permute-done.2.half_ref
  97.1 1.1 %shard_map.139 = (f32[512,512]{1,0:T(8,128)}, f32[512,512]{1,0:T(8,128)}) custom-call(s32[1]{0:T(128)} %bitcast.shard_ref, bf16[16,32,512]{2,1,0:T(8,128)(2,1)S(1)} %collective-permute-done.2.half_ref, f32[512,512]{1,0:T(8,128)} %get-tuple-element.39._grad_in, f32[512,512]{1,0:T(8,128)} %get-tuple-element.40._grad_out), custom_call_target="tpu_custom_call", output_to_operand_aliasing={{0}: (2, {}), {1}: (3, {})} | custom-call | flops 1000000 | bytes 1000000 | tf_op jit(solution)/shard_map/pallas_call | solution.py:75
Async XLA Ops:
  3.3 33.9 %all-to-all-start = ((bf16[128,2,1152]{2,1,0:T(2,128)(2,1)}), bf16[128,2,1152]{2,1,0:T(2,128)(2,1)S(1)}, u32[]{:S(2)}, u32[]{:S(2)}) async-start(bf16[128,2,1152]{2,1,0:T(2,128)(2,1)} %shard_map.130), calls=%async_computation | async-start | bytes 1179648 | tf_op jit(solution)/shard_map/all_to_all | solution.py:63
  20.5 1.0 %copy-start.3 = (bf16[512,512]{1,0:T(8,128)(2,1)S(1)}, bf16[512,512]{1,0:T(8,128)(2,1)}, u32[]{:S(2)}) copy-start(bf16[512,512]{1,0:T(8,128)(2,1)} %w_in_ref.1) | copy-start | bytes 1572868
  21.5 0.7 copy-start.4
  22.2 0.7 copy-start.5
  22.9 19.7 %copy-start = (bf16[512,512]{1,0:T(8,128)(2,1)S(1)}, bf16[512,512]{1,0:T(8,128)(2,1)}, u32[]{:S(2)}) copy-start(bf16[512,512]{1,0:T(8,128)(2,1)} %w_out_ref.5) | copy-start | bytes 1572868
  37.4 7.1 %collective-permute-start = (bf16[256,1152]{1,0:T(8,128)(2,1)S(1)}, bf16[256,1152]{1,0:T(8,128)(2,1)S(1)}, u32[]{:S(2)}, u32[]{:S(2)}) collective-permute-start(bf16[256,1152]{1,0:T(8,128)(2,1)S(1)} %reshape.31.own_ref), channel_id=1, source_target_pairs={{0,1},{1,0},{2,3},{3,2},{4,5},{5,4},{6,7},{7,6},{8,9},{9,8},{10,11... | collective-permute-start | bytes 1769480 | tf_op jit(solution)/shard_map/ppermute | solution.py:461
  46.8 1.7 %collective-permute-start.1 = (bf16[256,256]{1,0:T(8,128)(2,1)S(1)}, bf16[256,256]{1,0:T(8,128)(2,1)S(1)}, u32[]{:S(2)}, u32[]{:S(2)}) collective-permute-start(bf16[256,256]{1,0:T(8,128)(2,1)S(1)} %get-tuple-element.35.msg_oth_ref), channel_id=1, source_target_pairs={{0,1},{1,0},{2,3},{3,2},{4,5},{5,4},{6,7},{7,6},{8,9},{9,8},{10,11... | collective-permute-start | bytes 393224 | tf_op jit(solution)/shard_map/ppermute | solution.py:482
  48.5 47.1 %copy-start.1 = (bf16[128,512]{1,0:T(8,128)(2,1)S(1)}, bf16[128,512]{1,0:T(8,128)(2,1)}, u32[]{:S(2)}) copy-start(bf16[128,512]{1,0:T(8,128)(2,1)} %feat_ref.1) | copy-start | bytes 393220
  48.5 47.1 %copy-start.2 = (s32[128,1]{0,1:T(1,128)S(1)}, s32[128,1]{0,1:T(1,128)}, u32[]{:S(2)}) copy-start(s32[128,1]{0,1:T(1,128)} %param.18) | copy-start | bytes 1540
  93.1 4.0 %collective-permute-start.2 = (bf16[16,32,512]{2,1,0:T(8,128)(2,1)S(1)}, bf16[16,32,512]{2,1,0:T(8,128)(2,1)S(1)}, u32[]{:S(2)}, u32[]{:S(2)}) collective-permute-start(bf16[16,32,512]{2,1,0:T(8,128)(2,1)S(1)} %all_to_all.22.half_ref), channel_id=1, source_target_pairs={{0,1},{1,0},{2,3},{3,2},{4,5},{5,4},{6,7},{7,6},{8,9},{9,8},{10,11... | collective-permute-start | bytes 1572872 | tf_op jit(solution)/shard_map/ppermute | solution.py:510

commit v6 on v5

--- a/solution.py
+++ b/solution.py
@@ -125,7 +125,7 @@
 
     def send(first, part):
         span = slice(first, first + part.shape[1])
-        stage_ref[:, :, span] = part.reshape(slots // 2, 2, part.shape[1]).astype(BF)
+        stage_ref[:, :, span] = part.astype(BF).reshape(slots // 2, 2, part.shape[1])
         copy = pltpu.make_async_copy(
             stage_ref.at[:, :, span], out_hbm.at[:, :, span], out_sems.at[len(sent)]
         )
@@ -342,15 +342,23 @@
     block = ref.shape[1] // 2
     half = PLANE * block
     start = pl.multiple_of(member * half, half)
-    into = jnp.concatenate([ref[q, block:] for q in range(PLANE)], axis=0).astype(F32)
-    in_ref[...] = into.T
-    cols = pltpu.make_async_copy(in_ref, grad_in_hbm.at[:, pl.ds(start, half)], sems.at[0])
-    cols.start()
-    for q in range(PLANE):
-        out_ref[q * block : (q + 1) * block, :] = ref[q, 0:block].astype(F32)
-    rows = pltpu.make_async_copy(out_ref, grad_out_hbm.at[pl.ds(start, half), :], sems.at[1])
-    rows.start()
-    return cols, rows
+    copies = []
+
+    def send(src, dst):
+        copies.append(pltpu.make_async_copy(src, dst, sems.at[len(copies)]))
+        copies[-1].start()
+
+    for first in range(0, PLANE, 8):
+        for q in range(first, first + 8):
+            out_ref[q * block : (q + 1) * block, :] = ref[q, 0:block].astype(F32)
+        at = pl.ds(pl.multiple_of(start + first * block, 8 * block), 8 * block)
+        send(out_ref.at[first * block : (first + 8) * block, :], grad_out_hbm.at[at, :])
+    into = jnp.concatenate([ref[q, block:] for q in range(PLANE)], axis=0)
+    for first in range(0, into.shape[1], 128):
+        span = slice(first, first + 128)
+        in_ref[span, :] = into[:, span].astype(F32).T
+        send(in_ref.at[span, :], grad_in_hbm.at[span, pl.ds(start, half)])
+    return copies
 
 
 def own_final_kernel(
@@ -512,7 +520,7 @@
     placing = [
         pltpu.VMEM((width, half), F32),
         pltpu.VMEM((half, width), F32),
-        pltpu.SemaphoreType.DMA((2,)),
+        pltpu.SemaphoreType.DMA((6,)),
     ]
     updated, *first = call(
         own_final_kernel,

time: 98.7 us -> 98.3 us (level)
  no operation moved by 1% of the time
where the time goes in v6:
time: 98.3 us; the launch traced here: 97.9 us
  blocking collectives  44 us (45%)
  starting transfers between devices  24.2 us (25%)
  waiting for transfers between devices  13.5 us (14%)
  Pallas kernels  11.9 us (12%)
  local copies, waits for them, and re-layouts  3.5 us (4%)
    all_to_all x3, blocking collectives, exchange(): lax.all_to_all(array, ('dp', 'shard'), split_axis=0, concat_axis=0, axis_...  44 us
    all_to_all x1, starting transfers between devices, exchange(): lax.all_to_all(array, ('dp', 'shard'), split_axis=0, concat_axis=0, axis_...  16.3 us
    all_to_all x1, waiting for transfers between devices, exchange(): lax.all_to_all(array, ('dp', 'shard'), split_axis=0, concat_axis=0, axis_...  13.3 us
    pallas_call x10, Pallas kernels, call(): pl.pallas_call(body, out_shape=out_shape, in_specs=specs if specs is not...  11.9 us
    ppermute x1, starting transfers between devices, local(): other = lax.ppermute(own, 'shard', swap)  5.21 us
    unnamed x12, local copies, waits for them, and re-layouts  2.46 us
    ppermute x1, starting transfers between devices, local(): theirs = lax.ppermute(mine, 'shard', swap)  2.45 us
  transfers between devices with their start and end apart: 4, of which 2 were waited for; matrix products, arithmetic and copies ran while one was open for 1% of the time, Pallas kernels for 6%

profile of v6, /device:TPU:1, one launch (start us, length us, event | category | flops | bytes accessed | tf_op | source)
XLA Modules:
  0.0 97.9 jit_solution(530144634664108117)
XLA Ops:
  0.6 2.4 %shard_map.130 = bf16[128,2,1152]{2,1,0:T(2,128)(2,1)} custom-call(s32[1]{0:T(128)} %bitcast.shard_ref, bf16[128,512]{1,0:T(8,128)(2,1)} %feat_ref.1, f32[1,512]{1,0:T(1,128)} %bitcast.9, bf16[128,512]{1,0:T(8,128)(2,1)} %cot_hbm.1, bf16[3,128]{1,0:T(4,128)(2,1)} %pos_hbm.1, s32[1,128]{1,0:T(1,128)} %bitcast.11, s32[1,128]{1,0:T(1,128)} %bitcast.6), custom_call_target="tpu_custom_call" | custom-call | flops 1000000 | bytes 1000000 | tf_op jit(solution)/shard_map/pallas_call | solution.py:75
  3.0 16.3 %all-to-all-start = ((bf16[128,2,1152]{2,1,0:T(2,128)(2,1)}), bf16[128,2,1152]{2,1,0:T(2,128)(2,1)S(1)}, u32[]{:S(2)}, u32[]{:S(2)}) async-start(bf16[128,2,1152]{2,1,0:T(2,128)(2,1)} %shard_map.130), calls=%async_computation | async-start | bytes 1179648 | tf_op jit(solution)/shard_map/all_to_all | solution.py:63
  19.4 0.8 copy.16.damp_ref
  20.2 0.0 copy-start.3
  20.2 1.0 %copy-done.3 = bf16[512,512]{1,0:T(8,128)(2,1)S(1)} copy-done((bf16[512,512]{1,0:T(8,128)(2,1)S(1)}, bf16[512,512]{1,0:T(8,128)(2,1)}, u32[]{:S(2)}) %copy-start.3) | copy-done | bytes 524312
  21.2 0.0 copy-start.4
  21.2 0.7 copy-done.4
  21.9 0.0 copy-start.5
  21.9 0.7 copy-done.5
  22.6 0.0 copy-start
  22.6 1.0 shard_map.131
  23.6 13.3 %all-to-all-done = bf16[128,2,1152]{2,1,0:T(2,128)(2,1)S(1)} async-done(((bf16[128,2,1152]{2,1,0:T(2,128)(2,1)}), bf16[128,2,1152]{2,1,0:T(2,128)(2,1)S(1)}, u32[]{:S(2)}, u32[]{:S(2)}) %all-to-all-start) | async-done | bytes 589856 | tf_op jit(solution)/shard_map/all_to_all | solution.py:63
  36.8 0.2 reshape.31.own_ref
  37.1 5.2 %collective-permute-start = (bf16[256,1152]{1,0:T(8,128)(2,1)S(1)}, bf16[256,1152]{1,0:T(8,128)(2,1)S(1)}, u32[]{:S(2)}, u32[]{:S(2)}) collective-permute-start(bf16[256,1152]{1,0:T(8,128)(2,1)S(1)} %reshape.31.own_ref), channel_id=1, source_target_pairs={{0,1},{1,0},{2,3},{3,2},{4,5},{5,4},{6,7},{7,6},{8,9},{9,8},{10,11... | collective-permute-start | bytes 1769480 | tf_op jit(solution)/shard_map/ppermute | solution.py:469
  42.3 0.0 copy-done
  42.3 1.9 %shard_map.132 = (bf16[256,2048]{1,0:T(8,128)(2,1)S(1)}, bf16[512,256]{1,0:T(8,128)(2,1)}, f32[512,2048]{1,0:T(8,128)S(1)}) custom-call(s32[1]{0:T(128)} %bitcast.shard_ref, bf16[256,1152]{1,0:T(8,128)(2,1)S(1)} %reshape.31.own_ref, bf16[128,1024]{1,0:T(8,128)(2,1)S(1)} %get-tuple-element.28.kmat_ref, bf16[128,1024]{1,0:T(8,128)(2,1)S(1)} %get-tuple-element.29.kone_ref, ...), custom_call_target="tpu_custom_call" | custom-call | flops 4000000000 | bytes 1000000 | tf_op jit(solution)/shard_map/pallas_call | solution.py:75
  44.2 0.0 collective-permute-done.oth_ref
  44.2 2.3 %shard_map.133 = (bf16[256,2048]{1,0:T(8,128)(2,1)S(1)}, bf16[512,256]{1,0:T(8,128)(2,1)S(1)}, bf16[256,256]{1,0:T(8,128)(2,1)S(1)}, bf16[256,256]{1,0:T(8,128)(2,1)S(1)}) custom-call(s32[1]{0:T(128)} %bitcast.shard_ref, bf16[256,1152]{1,0:T(8,128)(2,1)S(1)} %collective-permute-done.oth_ref, f32[512,2048]{1,0:T(8,128)S(1)} %get-tuple-element.31.part_ref, ...), custom_call_target="tpu_custom_call" | custom-call | flops 1000000 | bytes 1000000 | tf_op jit(solution)/shard_map/pallas_call | solution.py:75
  46.5 0.2 collective-permute-start.1
  46.7 1.5 %shard_map.134.grad_ref = bf16[512,512]{1,0:T(8,128)(2,1)S(1)} custom-call(bf16[256,1152]{1,0:T(8,128)(2,1)S(1)} %reshape.31.own_ref, bf16[256,1152]{1,0:T(8,128)(2,1)S(1)} %collective-permute-done.oth_ref, f32[512,2048]{1,0:T(8,128)S(1)} %get-tuple-element.31.part_ref, bf16[256,2048]{1,0:T(8,128)(2,1)S(1)} %get-tuple-element.32.phase_own_ref, ...), custom_call_target="tpu_custom_call" | custom-call | flops 4000000000 | bytes 1000000 | tf_op jit(solution)/shard_map/pallas_call | solution.py:75
  48.1 0.0 copy-start.1
  48.2 0.0 copy-start.2
  48.2 0.0 collective-permute-done.1.got_ref
  48.2 0.3 shard_map.135
  48.5 17.8 %all_to_all.20.recv_ref = bf16[16,48,512]{2,1,0:T(8,128)(2,1)S(1)} all-to-all(bf16[16,48,512]{2,1,0:T(8,128)(2,1)S(1)} %shard_map.135), channel_id=1, replica_groups={{0,2,4,6,8,10,12,14,16,18,20,22,24,26,28,30},{32,34,36,38,40,42,44,46,4..., dimensions={0} | all-to-all | bytes 1572864 | tf_op jit(solution)/shard_map/all_to_all | solution.py:63
  66.3 0.2 shard_map.136
  66.6 11.4 %all_to_all.21.recv_ref = bf16[8,64,512]{2,1,0:T(8,128)(2,1)S(1)} all-to-all(bf16[8,64,512]{2,1,0:T(8,128)(2,1)S(1)} %shard_map.136), channel_id=1, replica_groups={{0,32,64,96,128,160,192,224},{2,34,66,98,130,162,194,226},{4,36,68,100,..., dimensions={0} | all-to-all | bytes 1048576 | tf_op jit(solution)/shard_map/all_to_all | solution.py:63
  78.0 0.1 shard_map.137
  78.1 14.8 %all_to_all.22.half_ref = bf16[16,32,512]{2,1,0:T(8,128)(2,1)S(1)} all-to-all(bf16[16,32,512]{2,1,0:T(8,128)(2,1)S(1)} %shard_map.137), channel_id=1, replica_groups={{0,2,4,6,8,10,12,14,16,18,20,22,24,26,28,30},{32,34,36,38,40,42,44,46,4..., dimensions={0} | all-to-all | bytes 1048576 | tf_op jit(solution)/shard_map/all_to_all | solution.py:63
  92.8 2.5 %collective-permute-start.2 = (bf16[16,32,512]{2,1,0:T(8,128)(2,1)S(1)}, bf16[16,32,512]{2,1,0:T(8,128)(2,1)S(1)}, u32[]{:S(2)}, u32[]{:S(2)}) collective-permute-start(bf16[16,32,512]{2,1,0:T(8,128)(2,1)S(1)} %all_to_all.22.half_ref), channel_id=1, source_target_pairs={{0,1},{1,0},{2,3},{3,2},{4,5},{5,4},{6,7},{7,6},{8,9},{9,8},{10,11... | collective-permute-start | bytes 1572872 | tf_op jit(solution)/shard_map/ppermute | solution.py:518
  95.3 0.0 copy-done.1
  95.3 0.0 copy-done.2
  95.3 1.2 %shard_map.138 = (bf16[128,512]{1,0:T(8,128)(2,1)}, f32[512,512]{1,0:T(8,128)}, f32[512,512]{1,0:T(8,128)}) custom-call(s32[1]{0:T(128)} %bitcast.shard_ref, bf16[128,512]{1,0:T(8,128)(2,1)S(1)} %copy-done.1, bf16[8,64,512]{2,1,0:T(8,128)(2,1)S(1)} %all_to_all.21.recv_ref, s32[1,128]{1,0:T(1,128)S(1)} %bitcast.7, bf16[16,32,512]{2,1,0:T(8,128)(2,1)S(1)} %all_to_all.22.half_ref), custom_call_target="tpu_custom_call" | custom-call | flops 4000000000 | bytes 1000000 | tf_op jit(solution)/shard_map/pallas_call | solution.py:75
  96.5 0.3 collective-permute-done.2.half_ref
  96.8 1.0 %shard_map.139 = (f32[512,512]{1,0:T(8,128)}, f32[512,512]{1,0:T(8,128)}) custom-call(s32[1]{0:T(128)} %bitcast.shard_ref, bf16[16,32,512]{2,1,0:T(8,128)(2,1)S(1)} %collective-permute-done.2.half_ref, f32[512,512]{1,0:T(8,128)} %get-tuple-element.39._grad_in, f32[512,512]{1,0:T(8,128)} %get-tuple-element.40._grad_out), custom_call_target="tpu_custom_call", output_to_operand_aliasing={{0}: (2, {}), {1}: (3, {})} | custom-call | flops 1000000 | bytes 1000000 | tf_op jit(solution)/shard_map/pallas_call | solution.py:75
Async XLA Ops:
  3.0 33.9 %all-to-all-start = ((bf16[128,2,1152]{2,1,0:T(2,128)(2,1)}), bf16[128,2,1152]{2,1,0:T(2,128)(2,1)S(1)}, u32[]{:S(2)}, u32[]{:S(2)}) async-start(bf16[128,2,1152]{2,1,0:T(2,128)(2,1)} %shard_map.130), calls=%async_computation | async-start | bytes 1179648 | tf_op jit(solution)/shard_map/all_to_all | solution.py:63
  20.2 1.0 %copy-start.3 = (bf16[512,512]{1,0:T(8,128)(2,1)S(1)}, bf16[512,512]{1,0:T(8,128)(2,1)}, u32[]{:S(2)}) copy-start(bf16[512,512]{1,0:T(8,128)(2,1)} %w_in_ref.1) | copy-start | bytes 1572868
  21.2 0.7 copy-start.4
  21.9 0.7 copy-start.5
  22.6 19.7 %copy-start = (bf16[512,512]{1,0:T(8,128)(2,1)S(1)}, bf16[512,512]{1,0:T(8,128)(2,1)}, u32[]{:S(2)}) copy-start(bf16[512,512]{1,0:T(8,128)(2,1)} %w_out_ref.5) | copy-start | bytes 1572868
  37.1 7.1 %collective-permute-start = (bf16[256,1152]{1,0:T(8,128)(2,1)S(1)}, bf16[256,1152]{1,0:T(8,128)(2,1)S(1)}, u32[]{:S(2)}, u32[]{:S(2)}) collective-permute-start(bf16[256,1152]{1,0:T(8,128)(2,1)S(1)} %reshape.31.own_ref), channel_id=1, source_target_pairs={{0,1},{1,0},{2,3},{3,2},{4,5},{5,4},{6,7},{7,6},{8,9},{9,8},{10,11... | collective-permute-start | bytes 1769480 | tf_op jit(solution)/shard_map/ppermute | solution.py:469
  46.5 1.7 %collective-permute-start.1 = (bf16[256,256]{1,0:T(8,128)(2,1)S(1)}, bf16[256,256]{1,0:T(8,128)(2,1)S(1)}, u32[]{:S(2)}, u32[]{:S(2)}) collective-permute-start(bf16[256,256]{1,0:T(8,128)(2,1)S(1)} %get-tuple-element.35.msg_oth_ref), channel_id=1, source_target_pairs={{0,1},{1,0},{2,3},{3,2},{4,5},{5,4},{6,7},{7,6},{8,9},{9,8},{10,11... | collective-permute-start | bytes 393224 | tf_op jit(solution)/shard_map/ppermute | solution.py:490
  48.1 47.1 %copy-start.1 = (bf16[128,512]{1,0:T(8,128)(2,1)S(1)}, bf16[128,512]{1,0:T(8,128)(2,1)}, u32[]{:S(2)}) copy-start(bf16[128,512]{1,0:T(8,128)(2,1)} %feat_ref.1) | copy-start | bytes 393220
  48.2 47.1 %copy-start.2 = (s32[128,1]{0,1:T(1,128)S(1)}, s32[128,1]{0,1:T(1,128)}, u32[]{:S(2)}) copy-start(s32[128,1]{0,1:T(1,128)} %param.18) | copy-start | bytes 1540
  92.8 4.0 %collective-permute-start.2 = (bf16[16,32,512]{2,1,0:T(8,128)(2,1)S(1)}, bf16[16,32,512]{2,1,0:T(8,128)(2,1)S(1)}, u32[]{:S(2)}, u32[]{:S(2)}) collective-permute-start(bf16[16,32,512]{2,1,0:T(8,128)(2,1)S(1)} %all_to_all.22.half_ref), channel_id=1, source_target_pairs={{0,1},{1,0},{2,3},{3,2},{4,5},{5,4},{6,7},{7,6},{8,9},{9,8},{10,11... | collective-permute-start | bytes 1572872 | tf_op jit(solution)/shard_map/ppermute | solution.py:518

commit v7 on v6

--- a/solution.py
+++ b/solution.py
@@ -37,8 +37,8 @@
 
 
 def place_of(owner, shard):
-    first = jnp.where(shard == 0, owner & 15, (owner >> 4) * 2 + (owner & 1))
-    second = jnp.where(shard == 0, owner >> 4, (owner >> 1) & 7)
+    first = 15 - jnp.where(shard == 0, owner & 15, (owner >> 4) * 2 + (owner & 1))
+    second = jnp.where(shard == 0, owner >> 4, 7 - ((owner >> 1) & 7))
     return first, second
 
 
@@ -47,8 +47,8 @@
 
     def split(shard):
         if shard == 0:
-            return {(x * 4 + y, z): (z, x, y) for z, x, y in every}
-        return {(z * 2 + y % 2, x * 2 + y // 2): (z, x, y) for z, x, y in every}
+            return {(15 - (x * 4 + y), z): (z, x, y) for z, x, y in every}
+        return {(15 - (z * 2 + y % 2), 7 - (x * 2 + y // 2)): (z, x, y) for z, x, y in every}
 
     around, first, second = [], [], []
     for shard in range(2):

time: 98.3 us -> 95.8 us (0.975)
  waiting for transfers between devices: 13.5 us -> 10.1 us
  starting transfers between devices: 24.2 us -> 25.6 us
    all_to_all x1, waiting for transfers between devices: 13.3 us -> 9.78 us  [exchange(): lax.all_to_all(array, ('dp', 'shard'), split_axis=0, concat_axis=0, axis_...]
    ppermute x1, starting transfers between devices: 2.45 us -> 5.38 us  [local(): theirs = lax.ppermute(mine, 'shard', swap)]
    ppermute x1, starting transfers between devices: 5.21 us -> 2.42 us  [local(): other = lax.ppermute(own, 'shard', swap)]
    all_to_all x1, starting transfers between devices: 16.3 us -> 17.6 us  [exchange(): lax.all_to_all(array, ('dp', 'shard'), split_axis=0, concat_axis=0, axis_...]
where the time goes in v7:
time: 95.8 us; the launch traced here: 95.4 us
  blocking collectives  43.7 us (46%)
  starting transfers between devices  25.6 us (27%)
  Pallas kernels  11.8 us (12%)
  waiting for transfers between devices  10.1 us (11%)
  local copies, waits for them, and re-layouts  3.5 us (4%)
    all_to_all x3, blocking collectives, exchange(): lax.all_to_all(array, ('dp', 'shard'), split_axis=0, concat_axis=0, axis_...  43.7 us
    all_to_all x1, starting transfers between devices, exchange(): lax.all_to_all(array, ('dp', 'shard'), split_axis=0, concat_axis=0, axis_...  17.6 us
    pallas_call x10, Pallas kernels, call(): pl.pallas_call(body, out_shape=out_shape, in_specs=specs if specs is not...  11.8 us
    all_to_all x1, waiting for transfers between devices, exchange(): lax.all_to_all(array, ('dp', 'shard'), split_axis=0, concat_axis=0, axis_...  9.78 us
    ppermute x1, starting transfers between devices, local(): theirs = lax.ppermute(mine, 'shard', swap)  5.38 us
    unnamed x12, local copies, waits for them, and re-layouts  2.46 us
    ppermute x1, starting transfers between devices, local(): other = lax.ppermute(own, 'shard', swap)  2.42 us
  transfers between devices with their start and end apart: 4, of which 2 were waited for; matrix products, arithmetic and copies ran while one was open for 1% of the time, Pallas kernels for 6%

profile of v7, /device:TPU:1, one launch (start us, length us, event | category | flops | bytes accessed | tf_op | source)
XLA Modules:
  0.0 95.4 jit_solution(1628938359886928273)
XLA Ops:
  0.6 2.4 %shard_map.130 = bf16[128,2,1152]{2,1,0:T(2,128)(2,1)} custom-call(s32[1]{0:T(128)} %bitcast.shard_ref, bf16[128,512]{1,0:T(8,128)(2,1)} %feat_ref.1, f32[1,512]{1,0:T(1,128)} %bitcast.9, bf16[128,512]{1,0:T(8,128)(2,1)} %cot_hbm.1, bf16[3,128]{1,0:T(4,128)(2,1)} %pos_hbm.1, s32[1,128]{1,0:T(1,128)} %bitcast.11, s32[1,128]{1,0:T(1,128)} %bitcast.6), custom_call_target="tpu_custom_call" | custom-call | flops 1000000 | bytes 1000000 | tf_op jit(solution)/shard_map/pallas_call | solution.py:75
  3.0 17.6 %all-to-all-start = ((bf16[128,2,1152]{2,1,0:T(2,128)(2,1)}), bf16[128,2,1152]{2,1,0:T(2,128)(2,1)S(1)}, u32[]{:S(2)}, u32[]{:S(2)}) async-start(bf16[128,2,1152]{2,1,0:T(2,128)(2,1)} %shard_map.130), calls=%async_computation | async-start | bytes 1179648 | tf_op jit(solution)/shard_map/all_to_all | solution.py:63
  20.6 0.8 copy.16.damp_ref
  21.4 0.0 copy-start.3
  21.4 1.0 %copy-done.3 = bf16[512,512]{1,0:T(8,128)(2,1)S(1)} copy-done((bf16[512,512]{1,0:T(8,128)(2,1)S(1)}, bf16[512,512]{1,0:T(8,128)(2,1)}, u32[]{:S(2)}) %copy-start.3) | copy-done | bytes 524312
  22.4 0.0 copy-start.4
  22.4 0.7 copy-done.4
  23.2 0.0 copy-start.5
  23.2 0.7 copy-done.5
  23.8 0.0 copy-start
  23.8 1.0 shard_map.131
  24.8 9.8 %all-to-all-done = bf16[128,2,1152]{2,1,0:T(2,128)(2,1)S(1)} async-done(((bf16[128,2,1152]{2,1,0:T(2,128)(2,1)}), bf16[128,2,1152]{2,1,0:T(2,128)(2,1)S(1)}, u32[]{:S(2)}, u32[]{:S(2)}) %all-to-all-start) | async-done | bytes 589856 | tf_op jit(solution)/shard_map/all_to_all | solution.py:63
  34.6 0.2 reshape.31.own_ref
  34.8 2.4 %collective-permute-start = (bf16[256,1152]{1,0:T(8,128)(2,1)S(1)}, bf16[256,1152]{1,0:T(8,128)(2,1)S(1)}, u32[]{:S(2)}, u32[]{:S(2)}) collective-permute-start(bf16[256,1152]{1,0:T(8,128)(2,1)S(1)} %reshape.31.own_ref), channel_id=1, source_target_pairs={{0,1},{1,0},{2,3},{3,2},{4,5},{5,4},{6,7},{7,6},{8,9},{9,8},{10,11... | collective-permute-start | bytes 1769480 | tf_op jit(solution)/shard_map/ppermute | solution.py:469
  37.2 0.0 copy-done
  37.2 1.9 %shard_map.132 = (bf16[256,2048]{1,0:T(8,128)(2,1)S(1)}, bf16[512,256]{1,0:T(8,128)(2,1)}, f32[512,2048]{1,0:T(8,128)S(1)}) custom-call(s32[1]{0:T(128)} %bitcast.shard_ref, bf16[256,1152]{1,0:T(8,128)(2,1)S(1)} %reshape.31.own_ref, bf16[128,1024]{1,0:T(8,128)(2,1)S(1)} %get-tuple-element.28.kmat_ref, bf16[128,1024]{1,0:T(8,128)(2,1)S(1)} %get-tuple-element.29.kone_ref, ...), custom_call_target="tpu_custom_call" | custom-call | flops 4000000000 | bytes 1000000 | tf_op jit(solution)/shard_map/pallas_call | solution.py:75
  39.1 0.0 collective-permute-done.oth_ref
  39.1 2.3 %shard_map.133 = (bf16[256,2048]{1,0:T(8,128)(2,1)S(1)}, bf16[512,256]{1,0:T(8,128)(2,1)S(1)}, bf16[256,256]{1,0:T(8,128)(2,1)S(1)}, bf16[256,256]{1,0:T(8,128)(2,1)S(1)}) custom-call(s32[1]{0:T(128)} %bitcast.shard_ref, bf16[256,1152]{1,0:T(8,128)(2,1)S(1)} %collective-permute-done.oth_ref, f32[512,2048]{1,0:T(8,128)S(1)} %get-tuple-element.31.part_ref, ...), custom_call_target="tpu_custom_call" | custom-call | flops 1000000 | bytes 1000000 | tf_op jit(solution)/shard_map/pallas_call | solution.py:75
  41.4 0.2 collective-permute-start.1
  41.6 1.5 %shard_map.134.grad_ref = bf16[512,512]{1,0:T(8,128)(2,1)S(1)} custom-call(bf16[256,1152]{1,0:T(8,128)(2,1)S(1)} %reshape.31.own_ref, bf16[256,1152]{1,0:T(8,128)(2,1)S(1)} %collective-permute-done.oth_ref, f32[512,2048]{1,0:T(8,128)S(1)} %get-tuple-element.31.part_ref, bf16[256,2048]{1,0:T(8,128)(2,1)S(1)} %get-tuple-element.32.phase_own_ref, ...), custom_call_target="tpu_custom_call" | custom-call | flops 4000000000 | bytes 1000000 | tf_op jit(solution)/shard_map/pallas_call | solution.py:75
  43.1 0.0 copy-start.1
  43.1 0.0 copy-start.2
  43.1 0.0 collective-permute-done.1.got_ref
  43.1 0.3 shard_map.135
  43.5 17.3 %all_to_all.20.recv_ref = bf16[16,48,512]{2,1,0:T(8,128)(2,1)S(1)} all-to-all(bf16[16,48,512]{2,1,0:T(8,128)(2,1)S(1)} %shard_map.135), channel_id=1, replica_groups={{30,28,26,24,22,20,18,16,14,12,10,8,6,4,2,0},{62,60,58,56,54,52,50,48,4..., dimensions={0} | all-to-all | bytes 1572864 | tf_op jit(solution)/shard_map/all_to_all | solution.py:63
  60.8 0.2 shard_map.136
  61.0 11.7 %all_to_all.21.recv_ref = bf16[8,64,512]{2,1,0:T(8,128)(2,1)S(1)} all-to-all(bf16[8,64,512]{2,1,0:T(8,128)(2,1)S(1)} %shard_map.136), channel_id=1, replica_groups={{30,62,94,126,158,190,222,254},{28,60,92,124,156,188,220,252},{26,58,90..., dimensions={0} | all-to-all | bytes 1048576 | tf_op jit(solution)/shard_map/all_to_all | solution.py:63
  72.8 0.1 shard_map.137
  72.8 14.6 %all_to_all.22.half_ref = bf16[16,32,512]{2,1,0:T(8,128)(2,1)S(1)} all-to-all(bf16[16,32,512]{2,1,0:T(8,128)(2,1)S(1)} %shard_map.137), channel_id=1, replica_groups={{30,28,26,24,22,20,18,16,14,12,10,8,6,4,2,0},{62,60,58,56,54,52,50,48,4..., dimensions={0} | all-to-all | bytes 1048576 | tf_op jit(solution)/shard_map/all_to_all | solution.py:63
  87.4 5.4 %collective-permute-start.2 = (bf16[16,32,512]{2,1,0:T(8,128)(2,1)S(1)}, bf16[16,32,512]{2,1,0:T(8,128)(2,1)S(1)}, u32[]{:S(2)}, u32[]{:S(2)}) collective-permute-start(bf16[16,32,512]{2,1,0:T(8,128)(2,1)S(1)} %all_to_all.22.half_ref), channel_id=1, source_target_pairs={{0,1},{1,0},{2,3},{3,2},{4,5},{5,4},{6,7},{7,6},{8,9},{9,8},{10,11... | collective-permute-start | bytes 1572872 | tf_op jit(solution)/shard_map/ppermute | solution.py:518
  92.8 0.0 copy-done.1
  92.8 0.0 copy-done.2
  92.8 1.2 %shard_map.138 = (bf16[128,512]{1,0:T(8,128)(2,1)}, f32[512,512]{1,0:T(8,128)}, f32[512,512]{1,0:T(8,128)}) custom-call(s32[1]{0:T(128)} %bitcast.shard_ref, bf16[128,512]{1,0:T(8,128)(2,1)S(1)} %copy-done.1, bf16[8,64,512]{2,1,0:T(8,128)(2,1)S(1)} %all_to_all.21.recv_ref, s32[1,128]{1,0:T(1,128)S(1)} %bitcast.7, bf16[16,32,512]{2,1,0:T(8,128)(2,1)S(1)} %all_to_all.22.half_ref), custom_call_target="tpu_custom_call" | custom-call | flops 4000000000 | bytes 1000000 | tf_op jit(solution)/shard_map/pallas_call | solution.py:75
  94.1 0.3 collective-permute-done.2.half_ref
  94.4 1.0 %shard_map.139 = (f32[512,512]{1,0:T(8,128)}, f32[512,512]{1,0:T(8,128)}) custom-call(s32[1]{0:T(128)} %bitcast.shard_ref, bf16[16,32,512]{2,1,0:T(8,128)(2,1)S(1)} %collective-permute-done.2.half_ref, f32[512,512]{1,0:T(8,128)} %get-tuple-element.39._grad_in, f32[512,512]{1,0:T(8,128)} %get-tuple-element.40._grad_out), custom_call_target="tpu_custom_call", output_to_operand_aliasing={{0}: (2, {}), {1}: (3, {})} | custom-call | flops 1000000 | bytes 1000000 | tf_op jit(solution)/shard_map/pallas_call | solution.py:75
Async XLA Ops:
  3.0 31.6 %all-to-all-start = ((bf16[128,2,1152]{2,1,0:T(2,128)(2,1)}), bf16[128,2,1152]{2,1,0:T(2,128)(2,1)S(1)}, u32[]{:S(2)}, u32[]{:S(2)}) async-start(bf16[128,2,1152]{2,1,0:T(2,128)(2,1)} %shard_map.130), calls=%async_computation | async-start | bytes 1179648 | tf_op jit(solution)/shard_map/all_to_all | solution.py:63
  21.4 1.0 %copy-start.3 = (bf16[512,512]{1,0:T(8,128)(2,1)S(1)}, bf16[512,512]{1,0:T(8,128)(2,1)}, u32[]{:S(2)}) copy-start(bf16[512,512]{1,0:T(8,128)(2,1)} %w_in_ref.1) | copy-start | bytes 1572868
  22.4 0.7 copy-start.4
  23.2 0.7 copy-start.5
  23.8 13.4 %copy-start = (bf16[512,512]{1,0:T(8,128)(2,1)S(1)}, bf16[512,512]{1,0:T(8,128)(2,1)}, u32[]{:S(2)}) copy-start(bf16[512,512]{1,0:T(8,128)(2,1)} %w_out_ref.5) | copy-start | bytes 1572868
  34.8 4.3 %collective-permute-start = (bf16[256,1152]{1,0:T(8,128)(2,1)S(1)}, bf16[256,1152]{1,0:T(8,128)(2,1)S(1)}, u32[]{:S(2)}, u32[]{:S(2)}) collective-permute-start(bf16[256,1152]{1,0:T(8,128)(2,1)S(1)} %reshape.31.own_ref), channel_id=1, source_target_pairs={{0,1},{1,0},{2,3},{3,2},{4,5},{5,4},{6,7},{7,6},{8,9},{9,8},{10,11... | collective-permute-start | bytes 1769480 | tf_op jit(solution)/shard_map/ppermute | solution.py:469
  41.4 1.7 %collective-permute-start.1 = (bf16[256,256]{1,0:T(8,128)(2,1)S(1)}, bf16[256,256]{1,0:T(8,128)(2,1)S(1)}, u32[]{:S(2)}, u32[]{:S(2)}) collective-permute-start(bf16[256,256]{1,0:T(8,128)(2,1)S(1)} %get-tuple-element.35.msg_oth_ref), channel_id=1, source_target_pairs={{0,1},{1,0},{2,3},{3,2},{4,5},{5,4},{6,7},{7,6},{8,9},{9,8},{10,11... | collective-permute-start | bytes 393224 | tf_op jit(solution)/shard_map/ppermute | solution.py:490
  43.1 49.7 %copy-start.1 = (bf16[128,512]{1,0:T(8,128)(2,1)S(1)}, bf16[128,512]{1,0:T(8,128)(2,1)}, u32[]{:S(2)}) copy-start(bf16[128,512]{1,0:T(8,128)(2,1)} %feat_ref.1) | copy-start | bytes 393220
  43.1 49.7 %copy-start.2 = (s32[128,1]{0,1:T(1,128)S(1)}, s32[128,1]{0,1:T(1,128)}, u32[]{:S(2)}) copy-start(s32[128,1]{0,1:T(1,128)} %param.18) | copy-start | bytes 1540
  87.4 6.9 %collective-permute-start.2 = (bf16[16,32,512]{2,1,0:T(8,128)(2,1)S(1)}, bf16[16,32,512]{2,1,0:T(8,128)(2,1)S(1)}, u32[]{:S(2)}, u32[]{:S(2)}) collective-permute-start(bf16[16,32,512]{2,1,0:T(8,128)(2,1)S(1)} %all_to_all.22.half_ref), channel_id=1, source_target_pairs={{0,1},{1,0},{2,3},{3,2},{4,5},{5,4},{6,7},{7,6},{8,9},{9,8},{10,11... | collective-permute-start | bytes 1572872 | tf_op jit(solution)/shard_map/ppermute | solution.py:518

commit v8 on v7

--- a/solution.py
+++ b/solution.py
@@ -37,8 +37,8 @@
 
 
 def place_of(owner, shard):
-    first = 15 - jnp.where(shard == 0, owner & 15, (owner >> 4) * 2 + (owner & 1))
-    second = jnp.where(shard == 0, owner >> 4, 7 - ((owner >> 1) & 7))
+    first = jnp.where(shard == 0, 15 - (owner & 15), 15 - ((owner >> 4) * 2 + (owner & 1)))
+    second = jnp.where(shard == 0, 7 - (owner >> 4), 7 - ((owner >> 1) & 7))
     return first, second
 
 
@@ -47,7 +47,7 @@
 
     def split(shard):
         if shard == 0:
-            return {(15 - (x * 4 + y), z): (z, x, y) for z, x, y in every}
+            return {(15 - (x * 4 + y), 7 - (z)): (z, x, y) for z, x, y in every}
         return {(15 - (z * 2 + y % 2), 7 - (x * 2 + y // 2)): (z, x, y) for z, x, y in every}
 
     around, first, second = [], [], []

time: 95.8 us -> 93.8 us (0.979)
  starting transfers between devices: 25.6 us -> 23.5 us
    ppermute x1, starting transfers between devices: 5.38 us -> 2.67 us  [local(): theirs = lax.ppermute(mine, 'shard', swap)]
where the time goes in v8:
time: 93.8 us; the launch traced here: 93.4 us
  blocking collectives  43.7 us (47%)
  starting transfers between devices  23.5 us (25%)
  Pallas kernels  11.9 us (13%)
  waiting for transfers between devices  10 us (11%)
  local copies, waits for them, and re-layouts  3.5 us (4%)
    all_to_all x3, blocking collectives, exchange(): lax.all_to_all(array, ('dp', 'shard'), split_axis=0, concat_axis=0, axis_...  43.7 us
    all_to_all x1, starting transfers between devices, exchange(): lax.all_to_all(array, ('dp', 'shard'), split_axis=0, concat_axis=0, axis_...  17.6 us
    pallas_call x10, Pallas kernels, call(): pl.pallas_call(body, out_shape=out_shape, in_specs=specs if specs is not...  11.9 us
    all_to_all x1, waiting for transfers between devices, exchange(): lax.all_to_all(array, ('dp', 'shard'), split_axis=0, concat_axis=0, axis_...  9.72 us
    ppermute x1, starting transfers between devices, local(): other = lax.ppermute(own, 'shard', swap)  3.11 us
    ppermute x1, starting transfers between devices, local(): theirs = lax.ppermute(mine, 'shard', swap)  2.67 us
    unnamed x12, local copies, waits for them, and re-layouts  2.46 us
  transfers between devices with their start and end apart: 4, of which 2 were waited for; matrix products, arithmetic and copies ran while one was open for 1% of the time, Pallas kernels for 6%

profile of v8, /device:TPU:1, one launch (start us, length us, event | category | flops | bytes accessed | tf_op | source)
XLA Modules:
  0.0 93.4 jit_solution(6281225219181365653)
XLA Ops:
  0.6 2.4 %shard_map.130 = bf16[128,2,1152]{2,1,0:T(2,128)(2,1)} custom-call(s32[1]{0:T(128)} %bitcast.shard_ref, bf16[128,512]{1,0:T(8,128)(2,1)} %feat_ref.1, f32[1,512]{1,0:T(1,128)} %bitcast.9, bf16[128,512]{1,0:T(8,128)(2,1)} %cot_hbm.1, bf16[3,128]{1,0:T(4,128)(2,1)} %pos_hbm.1, s32[1,128]{1,0:T(1,128)} %bitcast.11, s32[1,128]{1,0:T(1,128)} %bitcast.6), custom_call_target="tpu_custom_call" | custom-call | flops 1000000 | bytes 1000000 | tf_op jit(solution)/shard_map/pallas_call | solution.py:75
  3.0 17.6 %all-to-all-start = ((bf16[128,2,1152]{2,1,0:T(2,128)(2,1)}), bf16[128,2,1152]{2,1,0:T(2,128)(2,1)S(1)}, u32[]{:S(2)}, u32[]{:S(2)}) async-start(bf16[128,2,1152]{2,1,0:T(2,128)(2,1)} %shard_map.130), calls=%async_computation | async-start | bytes 1179648 | tf_op jit(solution)/shard_map/all_to_all | solution.py:63
  20.6 0.8 copy.16.damp_ref
  21.4 0.0 copy-start.3
  21.4 1.0 %copy-done.3 = bf16[512,512]{1,0:T(8,128)(2,1)S(1)} copy-done((bf16[512,512]{1,0:T(8,128)(2,1)S(1)}, bf16[512,512]{1,0:T(8,128)(2,1)}, u32[]{:S(2)}) %copy-start.3) | copy-done | bytes 524312
  22.4 0.0 copy-start.4
  22.4 0.7 copy-done.4
  23.2 0.0 copy-start.5
  23.2 0.7 copy-done.5
  23.8 0.0 copy-start
  23.8 1.0 %shard_map.131 = (bf16[128,1024]{1,0:T(8,128)(2,1)S(1)}, bf16[128,1024]{1,0:T(8,128)(2,1)S(1)}, f32[256,1024]{1,0:T(8,128)S(1)}, bf16[256,512]{1,0:T(8,128)(2,1)S(1)}) custom-call(s32[1]{0:T(128)} %bitcast.shard_ref, s32[3,1024]{1,0:T(4,128)S(1)} %copy-done.4, s32[1,1024]{1,0:T(1,128)S(1)} %bitcast.8, f32[512,1]{1,0:T(8,128)S(1)} %copy.16.damp_ref, ...), custom_call_target="tpu_custom_call" | custom-call | flops 4000000000 | bytes 1000000 | tf_op jit(solution)/shard_map/pallas_call | solution.py:75
  24.8 9.7 %all-to-all-done = bf16[128,2,1152]{2,1,0:T(2,128)(2,1)S(1)} async-done(((bf16[128,2,1152]{2,1,0:T(2,128)(2,1)}), bf16[128,2,1152]{2,1,0:T(2,128)(2,1)S(1)}, u32[]{:S(2)}, u32[]{:S(2)}) %all-to-all-start) | async-done | bytes 589856 | tf_op jit(solution)/shard_map/all_to_all | solution.py:63
  34.5 0.2 reshape.31.own_ref
  34.7 3.1 %collective-permute-start = (bf16[256,1152]{1,0:T(8,128)(2,1)S(1)}, bf16[256,1152]{1,0:T(8,128)(2,1)S(1)}, u32[]{:S(2)}, u32[]{:S(2)}) collective-permute-start(bf16[256,1152]{1,0:T(8,128)(2,1)S(1)} %reshape.31.own_ref), channel_id=1, source_target_pairs={{0,1},{1,0},{2,3},{3,2},{4,5},{5,4},{6,7},{7,6},{8,9},{9,8},{10,11... | collective-permute-start | bytes 1769480 | tf_op jit(solution)/shard_map/ppermute | solution.py:469
  37.9 0.0 copy-done
  37.9 1.9 %shard_map.132 = (bf16[256,2048]{1,0:T(8,128)(2,1)S(1)}, bf16[512,256]{1,0:T(8,128)(2,1)}, f32[512,2048]{1,0:T(8,128)S(1)}) custom-call(s32[1]{0:T(128)} %bitcast.shard_ref, bf16[256,1152]{1,0:T(8,128)(2,1)S(1)} %reshape.31.own_ref, bf16[128,1024]{1,0:T(8,128)(2,1)S(1)} %get-tuple-element.28.kmat_ref, bf16[128,1024]{1,0:T(8,128)(2,1)S(1)} %get-tuple-element.29.kone_ref, ...), custom_call_target="tpu_custom_call" | custom-call | flops 4000000000 | bytes 1000000 | tf_op jit(solution)/shard_map/pallas_call | solution.py:75
  39.7 0.0 collective-permute-done.oth_ref
  39.7 2.3 %shard_map.133 = (bf16[256,2048]{1,0:T(8,128)(2,1)S(1)}, bf16[512,256]{1,0:T(8,128)(2,1)S(1)}, bf16[256,256]{1,0:T(8,128)(2,1)S(1)}, bf16[256,256]{1,0:T(8,128)(2,1)S(1)}) custom-call(s32[1]{0:T(128)} %bitcast.shard_ref, bf16[256,1152]{1,0:T(8,128)(2,1)S(1)} %collective-permute-done.oth_ref, f32[512,2048]{1,0:T(8,128)S(1)} %get-tuple-element.31.part_ref, ...), custom_call_target="tpu_custom_call" | custom-call | flops 1000000 | bytes 1000000 | tf_op jit(solution)/shard_map/pallas_call | solution.py:75
  42.0 0.2 collective-permute-start.1
  42.2 1.5 %shard_map.134.grad_ref = bf16[512,512]{1,0:T(8,128)(2,1)S(1)} custom-call(bf16[256,1152]{1,0:T(8,128)(2,1)S(1)} %reshape.31.own_ref, bf16[256,1152]{1,0:T(8,128)(2,1)S(1)} %collective-permute-done.oth_ref, f32[512,2048]{1,0:T(8,128)S(1)} %get-tuple-element.31.part_ref, bf16[256,2048]{1,0:T(8,128)(2,1)S(1)} %get-tuple-element.32.phase_own_ref, ...), custom_call_target="tpu_custom_call" | custom-call | flops 4000000000 | bytes 1000000 | tf_op jit(solution)/shard_map/pallas_call | solution.py:75
  43.7 0.0 copy-start.1
  43.7 0.0 copy-start.2
  43.7 0.0 collective-permute-done.1.got_ref
  43.8 0.3 shard_map.135
  44.1 16.8 %all_to_all.20.recv_ref = bf16[16,48,512]{2,1,0:T(8,128)(2,1)S(1)} all-to-all(bf16[16,48,512]{2,1,0:T(8,128)(2,1)S(1)} %shard_map.135), channel_id=1, replica_groups={{254,252,250,248,246,244,242,240,238,236,234,232,230,228,226,224},{222,..., dimensions={0} | all-to-all | bytes 1572864 | tf_op jit(solution)/shard_map/all_to_all | solution.py:63
  60.9 0.2 shard_map.136
  61.1 12.3 %all_to_all.21.recv_ref = bf16[8,64,512]{2,1,0:T(8,128)(2,1)S(1)} all-to-all(bf16[8,64,512]{2,1,0:T(8,128)(2,1)S(1)} %shard_map.136), channel_id=1, replica_groups={{254,222,190,158,126,94,62,30},{252,220,188,156,124,92,60,28},{250,218,..., dimensions={0} | all-to-all | bytes 1048576 | tf_op jit(solution)/shard_map/all_to_all | solution.py:63
  73.5 0.1 shard_map.137
  73.5 14.6 %all_to_all.22.half_ref = bf16[16,32,512]{2,1,0:T(8,128)(2,1)S(1)} all-to-all(bf16[16,32,512]{2,1,0:T(8,128)(2,1)S(1)} %shard_map.137), channel_id=1, replica_groups={{254,252,250,248,246,244,242,240,238,236,234,232,230,228,226,224},{222,..., dimensions={0} | all-to-all | bytes 1048576 | tf_op jit(solution)/shard_map/all_to_all | solution.py:63
  88.1 2.7 %collective-permute-start.2 = (bf16[16,32,512]{2,1,0:T(8,128)(2,1)S(1)}, bf16[16,32,512]{2,1,0:T(8,128)(2,1)S(1)}, u32[]{:S(2)}, u32[]{:S(2)}) collective-permute-start(bf16[16,32,512]{2,1,0:T(8,128)(2,1)S(1)} %all_to_all.22.half_ref), channel_id=1, source_target_pairs={{0,1},{1,0},{2,3},{3,2},{4,5},{5,4},{6,7},{7,6},{8,9},{9,8},{10,11... | collective-permute-start | bytes 1572872 | tf_op jit(solution)/shard_map/ppermute | solution.py:518
  90.8 0.0 copy-done.1
  90.8 0.0 copy-done.2
  90.8 1.2 %shard_map.138 = (bf16[128,512]{1,0:T(8,128)(2,1)}, f32[512,512]{1,0:T(8,128)}, f32[512,512]{1,0:T(8,128)}) custom-call(s32[1]{0:T(128)} %bitcast.shard_ref, bf16[128,512]{1,0:T(8,128)(2,1)S(1)} %copy-done.1, bf16[8,64,512]{2,1,0:T(8,128)(2,1)S(1)} %all_to_all.21.recv_ref, s32[1,128]{1,0:T(1,128)S(1)} %bitcast.7, bf16[16,32,512]{2,1,0:T(8,128)(2,1)S(1)} %all_to_all.22.half_ref), custom_call_target="tpu_custom_call" | custom-call | flops 4000000000 | bytes 1000000 | tf_op jit(solution)/shard_map/pallas_call | solution.py:75
  92.1 0.3 collective-permute-done.2.half_ref
  92.3 1.0 %shard_map.139 = (f32[512,512]{1,0:T(8,128)}, f32[512,512]{1,0:T(8,128)}) custom-call(s32[1]{0:T(128)} %bitcast.shard_ref, bf16[16,32,512]{2,1,0:T(8,128)(2,1)S(1)} %collective-permute-done.2.half_ref, f32[512,512]{1,0:T(8,128)} %get-tuple-element.39._grad_in, f32[512,512]{1,0:T(8,128)} %get-tuple-element.40._grad_out), custom_call_target="tpu_custom_call", output_to_operand_aliasing={{0}: (2, {}), {1}: (3, {})} | custom-call | flops 1000000 | bytes 1000000 | tf_op jit(solution)/shard_map/pallas_call | solution.py:75
Async XLA Ops:
  3.0 31.5 %all-to-all-start = ((bf16[128,2,1152]{2,1,0:T(2,128)(2,1)}), bf16[128,2,1152]{2,1,0:T(2,128)(2,1)S(1)}, u32[]{:S(2)}, u32[]{:S(2)}) async-start(bf16[128,2,1152]{2,1,0:T(2,128)(2,1)} %shard_map.130), calls=%async_computation | async-start | bytes 1179648 | tf_op jit(solution)/shard_map/all_to_all | solution.py:63
  21.4 1.0 %copy-start.3 = (bf16[512,512]{1,0:T(8,128)(2,1)S(1)}, bf16[512,512]{1,0:T(8,128)(2,1)}, u32[]{:S(2)}) copy-start(bf16[512,512]{1,0:T(8,128)(2,1)} %w_in_ref.1) | copy-start | bytes 1572868
  22.4 0.7 copy-start.4
  23.2 0.7 copy-start.5
  23.8 14.0 %copy-start = (bf16[512,512]{1,0:T(8,128)(2,1)S(1)}, bf16[512,512]{1,0:T(8,128)(2,1)}, u32[]{:S(2)}) copy-start(bf16[512,512]{1,0:T(8,128)(2,1)} %w_out_ref.5) | copy-start | bytes 1572868
  34.7 5.0 %collective-permute-start = (bf16[256,1152]{1,0:T(8,128)(2,1)S(1)}, bf16[256,1152]{1,0:T(8,128)(2,1)S(1)}, u32[]{:S(2)}, u32[]{:S(2)}) collective-permute-start(bf16[256,1152]{1,0:T(8,128)(2,1)S(1)} %reshape.31.own_ref), channel_id=1, source_target_pairs={{0,1},{1,0},{2,3},{3,2},{4,5},{5,4},{6,7},{7,6},{8,9},{9,8},{10,11... | collective-permute-start | bytes 1769480 | tf_op jit(solution)/shard_map/ppermute | solution.py:469
  42.0 1.7 %collective-permute-start.1 = (bf16[256,256]{1,0:T(8,128)(2,1)S(1)}, bf16[256,256]{1,0:T(8,128)(2,1)S(1)}, u32[]{:S(2)}, u32[]{:S(2)}) collective-permute-start(bf16[256,256]{1,0:T(8,128)(2,1)S(1)} %get-tuple-element.35.msg_oth_ref), channel_id=1, source_target_pairs={{0,1},{1,0},{2,3},{3,2},{4,5},{5,4},{6,7},{7,6},{8,9},{9,8},{10,11... | collective-permute-start | bytes 393224 | tf_op jit(solution)/shard_map/ppermute | solution.py:490
  43.7 47.1 %copy-start.1 = (bf16[128,512]{1,0:T(8,128)(2,1)S(1)}, bf16[128,512]{1,0:T(8,128)(2,1)}, u32[]{:S(2)}) copy-start(bf16[128,512]{1,0:T(8,128)(2,1)} %feat_ref.1) | copy-start | bytes 393220
  43.7 47.1 %copy-start.2 = (s32[128,1]{0,1:T(1,128)S(1)}, s32[128,1]{0,1:T(1,128)}, u32[]{:S(2)}) copy-start(s32[128,1]{0,1:T(1,128)} %param.18) | copy-start | bytes 1540
  88.1 4.2 %collective-permute-start.2 = (bf16[16,32,512]{2,1,0:T(8,128)(2,1)S(1)}, bf16[16,32,512]{2,1,0:T(8,128)(2,1)S(1)}, u32[]{:S(2)}, u32[]{:S(2)}) collective-permute-start(bf16[16,32,512]{2,1,0:T(8,128)(2,1)S(1)} %all_to_all.22.half_ref), channel_id=1, source_target_pairs={{0,1},{1,0},{2,3},{3,2},{4,5},{5,4},{6,7},{7,6},{8,9},{9,8},{10,11... | collective-permute-start | bytes 1572872 | tf_op jit(solution)/shard_map/ppermute | solution.py:518

commit v9 on v8

--- a/solution.py
+++ b/solution.py
@@ -37,7 +37,7 @@
 
 
 def place_of(owner, shard):
-    first = jnp.where(shard == 0, 15 - (owner & 15), 15 - ((owner >> 4) * 2 + (owner & 1)))
+    first = jnp.where(shard == 0, 15 - ((owner & 3) * 4 + ((owner >> 2) & 3)), 15 - ((owner >> 4) * 2 + (owner & 1)))
     second = jnp.where(shard == 0, 7 - (owner >> 4), 7 - ((owner >> 1) & 7))
     return first, second
 
@@ -47,7 +47,7 @@
 
     def split(shard):
         if shard == 0:
-            return {(15 - (x * 4 + y), 7 - (z)): (z, x, y) for z, x, y in every}
+            return {(15 - (y * 4 + x), 7 - (z)): (z, x, y) for z, x, y in every}
         return {(15 - (z * 2 + y % 2), 7 - (x * 2 + y // 2)): (z, x, y) for z, x, y in every}
 
     around, first, second = [], [], []

time: 93.8 us -> 92.5 us (0.986)
  starting transfers between devices: 23.5 us -> 22 us
    ppermute x1, starting transfers between devices: 2.67 us -> 1.18 us  [local(): theirs = lax.ppermute(mine, 'shard', swap)]
where the time goes in v9:
time: 92.5 us; the launch traced here: 92 us
  blocking collectives  43.9 us (47%)
  starting transfers between devices  22 us (24%)
  Pallas kernels  11.8 us (13%)
  waiting for transfers between devices  10.1 us (11%)
  local copies, waits for them, and re-layouts  3.5 us (4%)
    all_to_all x3, blocking collectives, exchange(): lax.all_to_all(array, ('dp', 'shard'), split_axis=0, concat_axis=0, axis_...  43.9 us
    all_to_all x1, starting transfers between devices, exchange(): lax.all_to_all(array, ('dp', 'shard'), split_axis=0, concat_axis=0, axis_...  17.6 us
    pallas_call x10, Pallas kernels, call(): pl.pallas_call(body, out_shape=out_shape, in_specs=specs if specs is not...  11.8 us
    all_to_all x1, waiting for transfers between devices, exchange(): lax.all_to_all(array, ('dp', 'shard'), split_axis=0, concat_axis=0, axis_...  9.78 us
    ppermute x1, starting transfers between devices, local(): other = lax.ppermute(own, 'shard', swap)  3.03 us
    unnamed x12, local copies, waits for them, and re-layouts  2.46 us
  transfers between devices with their start and end apart: 4, of which 2 were waited for; matrix products, arithmetic and copies ran while one was open for 1% of the time, Pallas kernels for 6%

profile of v9, /device:TPU:1, one launch (start us, length us, event | category | flops | bytes accessed | tf_op | source)
XLA Modules:
  0.0 92.0 jit_solution(9987615640740079635)
XLA Ops:
  0.6 2.4 %shard_map.130 = bf16[128,2,1152]{2,1,0:T(2,128)(2,1)} custom-call(s32[1]{0:T(128)} %bitcast.shard_ref, bf16[128,512]{1,0:T(8,128)(2,1)} %feat_ref.1, f32[1,512]{1,0:T(1,128)} %bitcast.9, bf16[128,512]{1,0:T(8,128)(2,1)} %cot_hbm.1, bf16[3,128]{1,0:T(4,128)(2,1)} %pos_hbm.1, s32[1,128]{1,0:T(1,128)} %bitcast.11, s32[1,128]{1,0:T(1,128)} %bitcast.6), custom_call_target="tpu_custom_call" | custom-call | flops 1000000 | bytes 1000000 | tf_op jit(solution)/shard_map/pallas_call | solution.py:75
  3.0 17.6 %all-to-all-start = ((bf16[128,2,1152]{2,1,0:T(2,128)(2,1)}), bf16[128,2,1152]{2,1,0:T(2,128)(2,1)S(1)}, u32[]{:S(2)}, u32[]{:S(2)}) async-start(bf16[128,2,1152]{2,1,0:T(2,128)(2,1)} %shard_map.130), calls=%async_computation | async-start | bytes 1179648 | tf_op jit(solution)/shard_map/all_to_all | solution.py:63
  20.6 0.8 copy.16.damp_ref
  21.4 0.0 copy-start.3
  21.4 1.0 %copy-done.3 = bf16[512,512]{1,0:T(8,128)(2,1)S(1)} copy-done((bf16[512,512]{1,0:T(8,128)(2,1)S(1)}, bf16[512,512]{1,0:T(8,128)(2,1)}, u32[]{:S(2)}) %copy-start.3) | copy-done | bytes 524312
  22.4 0.0 copy-start.4
  22.4 0.7 copy-done.4
  23.2 0.0 copy-start.5
  23.2 0.7 copy-done.5
  23.8 0.0 copy-start
  23.8 1.0 %shard_map.131 = (bf16[128,1024]{1,0:T(8,128)(2,1)S(1)}, bf16[128,1024]{1,0:T(8,128)(2,1)S(1)}, f32[256,1024]{1,0:T(8,128)S(1)}, bf16[256,512]{1,0:T(8,128)(2,1)S(1)}) custom-call(s32[1]{0:T(128)} %bitcast.shard_ref, s32[3,1024]{1,0:T(4,128)S(1)} %copy-done.4, s32[1,1024]{1,0:T(1,128)S(1)} %bitcast.8, f32[512,1]{1,0:T(8,128)S(1)} %copy.16.damp_ref, ...), custom_call_target="tpu_custom_call" | custom-call | flops 4000000000 | bytes 1000000 | tf_op jit(solution)/shard_map/pallas_call | solution.py:75
  24.8 9.8 %all-to-all-done = bf16[128,2,1152]{2,1,0:T(2,128)(2,1)S(1)} async-done(((bf16[128,2,1152]{2,1,0:T(2,128)(2,1)}), bf16[128,2,1152]{2,1,0:T(2,128)(2,1)S(1)}, u32[]{:S(2)}, u32[]{:S(2)}) %all-to-all-start) | async-done | bytes 589856 | tf_op jit(solution)/shard_map/all_to_all | solution.py:63
  34.6 0.2 reshape.31.own_ref
  34.8 3.0 %collective-permute-start = (bf16[256,1152]{1,0:T(8,128)(2,1)S(1)}, bf16[256,1152]{1,0:T(8,128)(2,1)S(1)}, u32[]{:S(2)}, u32[]{:S(2)}) collective-permute-start(bf16[256,1152]{1,0:T(8,128)(2,1)S(1)} %reshape.31.own_ref), channel_id=1, source_target_pairs={{0,1},{1,0},{2,3},{3,2},{4,5},{5,4},{6,7},{7,6},{8,9},{9,8},{10,11... | collective-permute-start | bytes 1769480 | tf_op jit(solution)/shard_map/ppermute | solution.py:469
  37.8 0.0 copy-done
  37.8 1.9 %shard_map.132 = (bf16[256,2048]{1,0:T(8,128)(2,1)S(1)}, bf16[512,256]{1,0:T(8,128)(2,1)}, f32[512,2048]{1,0:T(8,128)S(1)}) custom-call(s32[1]{0:T(128)} %bitcast.shard_ref, bf16[256,1152]{1,0:T(8,128)(2,1)S(1)} %reshape.31.own_ref, bf16[128,1024]{1,0:T(8,128)(2,1)S(1)} %get-tuple-element.28.kmat_ref, bf16[128,1024]{1,0:T(8,128)(2,1)S(1)} %get-tuple-element.29.kone_ref, ...), custom_call_target="tpu_custom_call" | custom-call | flops 4000000000 | bytes 1000000 | tf_op jit(solution)/shard_map/pallas_call | solution.py:75
  39.7 0.0 collective-permute-done.oth_ref
  39.7 2.3 %shard_map.133 = (bf16[256,2048]{1,0:T(8,128)(2,1)S(1)}, bf16[512,256]{1,0:T(8,128)(2,1)S(1)}, bf16[256,256]{1,0:T(8,128)(2,1)S(1)}, bf16[256,256]{1,0:T(8,128)(2,1)S(1)}) custom-call(s32[1]{0:T(128)} %bitcast.shard_ref, bf16[256,1152]{1,0:T(8,128)(2,1)S(1)} %collective-permute-done.oth_ref, f32[512,2048]{1,0:T(8,128)S(1)} %get-tuple-element.31.part_ref, ...), custom_call_target="tpu_custom_call" | custom-call | flops 1000000 | bytes 1000000 | tf_op jit(solution)/shard_map/pallas_call | solution.py:75
  42.0 0.2 collective-permute-start.1
  42.2 1.5 %shard_map.134.grad_ref = bf16[512,512]{1,0:T(8,128)(2,1)S(1)} custom-call(bf16[256,1152]{1,0:T(8,128)(2,1)S(1)} %reshape.31.own_ref, bf16[256,1152]{1,0:T(8,128)(2,1)S(1)} %collective-permute-done.oth_ref, f32[512,2048]{1,0:T(8,128)S(1)} %get-tuple-element.31.part_ref, bf16[256,2048]{1,0:T(8,128)(2,1)S(1)} %get-tuple-element.32.phase_own_ref, ...), custom_call_target="tpu_custom_call" | custom-call | flops 4000000000 | bytes 1000000 | tf_op jit(solution)/shard_map/pallas_call | solution.py:75
  43.7 0.0 copy-start.1
  43.7 0.0 copy-start.2
  43.7 0.0 collective-permute-done.1.got_ref
  43.7 0.3 shard_map.135
  44.1 16.9 %all_to_all.20.recv_ref = bf16[16,48,512]{2,1,0:T(8,128)(2,1)S(1)} all-to-all(bf16[16,48,512]{2,1,0:T(8,128)(2,1)S(1)} %shard_map.135), channel_id=1, replica_groups={{254,246,238,230,252,244,236,228,250,242,234,226,248,240,232,224},{222,..., dimensions={0} | all-to-all | bytes 1572864 | tf_op jit(solution)/shard_map/all_to_all | solution.py:63
  60.9 0.2 shard_map.136
  61.2 12.3 %all_to_all.21.recv_ref = bf16[8,64,512]{2,1,0:T(8,128)(2,1)S(1)} all-to-all(bf16[8,64,512]{2,1,0:T(8,128)(2,1)S(1)} %shard_map.136), channel_id=1, replica_groups={{254,222,190,158,126,94,62,30},{246,214,182,150,118,86,54,22},{238,206,..., dimensions={0} | all-to-all | bytes 1048576 | tf_op jit(solution)/shard_map/all_to_all | solution.py:63
  73.5 0.1 shard_map.137
  73.5 14.7 %all_to_all.22.half_ref = bf16[16,32,512]{2,1,0:T(8,128)(2,1)S(1)} all-to-all(bf16[16,32,512]{2,1,0:T(8,128)(2,1)S(1)} %shard_map.137), channel_id=1, replica_groups={{254,246,238,230,252,244,236,228,250,242,234,226,248,240,232,224},{222,..., dimensions={0} | all-to-all | bytes 1048576 | tf_op jit(solution)/shard_map/all_to_all | solution.py:63
  88.2 1.2 %collective-permute-start.2 = (bf16[16,32,512]{2,1,0:T(8,128)(2,1)S(1)}, bf16[16,32,512]{2,1,0:T(8,128)(2,1)S(1)}, u32[]{:S(2)}, u32[]{:S(2)}) collective-permute-start(bf16[16,32,512]{2,1,0:T(8,128)(2,1)S(1)} %all_to_all.22.half_ref), channel_id=1, source_target_pairs={{0,1},{1,0},{2,3},{3,2},{4,5},{5,4},{6,7},{7,6},{8,9},{9,8},{10,11... | collective-permute-start | bytes 1572872 | tf_op jit(solution)/shard_map/ppermute | solution.py:518
  89.4 0.0 copy-done.1
  89.4 0.0 copy-done.2
  89.4 1.2 %shard_map.138 = (bf16[128,512]{1,0:T(8,128)(2,1)}, f32[512,512]{1,0:T(8,128)}, f32[512,512]{1,0:T(8,128)}) custom-call(s32[1]{0:T(128)} %bitcast.shard_ref, bf16[128,512]{1,0:T(8,128)(2,1)S(1)} %copy-done.1, bf16[8,64,512]{2,1,0:T(8,128)(2,1)S(1)} %all_to_all.21.recv_ref, s32[1,128]{1,0:T(1,128)S(1)} %bitcast.7, bf16[16,32,512]{2,1,0:T(8,128)(2,1)S(1)} %all_to_all.22.half_ref), custom_call_target="tpu_custom_call" | custom-call | flops 4000000000 | bytes 1000000 | tf_op jit(solution)/shard_map/pallas_call | solution.py:75
  90.7 0.3 collective-permute-done.2.half_ref
  91.0 1.0 %shard_map.139 = (f32[512,512]{1,0:T(8,128)}, f32[512,512]{1,0:T(8,128)}) custom-call(s32[1]{0:T(128)} %bitcast.shard_ref, bf16[16,32,512]{2,1,0:T(8,128)(2,1)S(1)} %collective-permute-done.2.half_ref, f32[512,512]{1,0:T(8,128)} %get-tuple-element.39._grad_in, f32[512,512]{1,0:T(8,128)} %get-tuple-element.40._grad_out), custom_call_target="tpu_custom_call", output_to_operand_aliasing={{0}: (2, {}), {1}: (3, {})} | custom-call | flops 1000000 | bytes 1000000 | tf_op jit(solution)/shard_map/pallas_call | solution.py:75
Async XLA Ops:
  3.0 31.6 %all-to-all-start = ((bf16[128,2,1152]{2,1,0:T(2,128)(2,1)}), bf16[128,2,1152]{2,1,0:T(2,128)(2,1)S(1)}, u32[]{:S(2)}, u32[]{:S(2)}) async-start(bf16[128,2,1152]{2,1,0:T(2,128)(2,1)} %shard_map.130), calls=%async_computation | async-start | bytes 1179648 | tf_op jit(solution)/shard_map/all_to_all | solution.py:63
  21.4 1.0 %copy-start.3 = (bf16[512,512]{1,0:T(8,128)(2,1)S(1)}, bf16[512,512]{1,0:T(8,128)(2,1)}, u32[]{:S(2)}) copy-start(bf16[512,512]{1,0:T(8,128)(2,1)} %w_in_ref.1) | copy-start | bytes 1572868
  22.4 0.7 copy-start.4
  23.2 0.7 copy-start.5
  23.8 14.0 %copy-start = (bf16[512,512]{1,0:T(8,128)(2,1)S(1)}, bf16[512,512]{1,0:T(8,128)(2,1)}, u32[]{:S(2)}) copy-start(bf16[512,512]{1,0:T(8,128)(2,1)} %w_out_ref.5) | copy-start | bytes 1572868
  34.8 4.9 %collective-permute-start = (bf16[256,1152]{1,0:T(8,128)(2,1)S(1)}, bf16[256,1152]{1,0:T(8,128)(2,1)S(1)}, u32[]{:S(2)}, u32[]{:S(2)}) collective-permute-start(bf16[256,1152]{1,0:T(8,128)(2,1)S(1)} %reshape.31.own_ref), channel_id=1, source_target_pairs={{0,1},{1,0},{2,3},{3,2},{4,5},{5,4},{6,7},{7,6},{8,9},{9,8},{10,11... | collective-permute-start | bytes 1769480 | tf_op jit(solution)/shard_map/ppermute | solution.py:469
  42.0 1.7 %collective-permute-start.1 = (bf16[256,256]{1,0:T(8,128)(2,1)S(1)}, bf16[256,256]{1,0:T(8,128)(2,1)S(1)}, u32[]{:S(2)}, u32[]{:S(2)}) collective-permute-start(bf16[256,256]{1,0:T(8,128)(2,1)S(1)} %get-tuple-element.35.msg_oth_ref), channel_id=1, source_target_pairs={{0,1},{1,0},{2,3},{3,2},{4,5},{5,4},{6,7},{7,6},{8,9},{9,8},{10,11... | collective-permute-start | bytes 393224 | tf_op jit(solution)/shard_map/ppermute | solution.py:490
  43.7 45.7 %copy-start.1 = (bf16[128,512]{1,0:T(8,128)(2,1)S(1)}, bf16[128,512]{1,0:T(8,128)(2,1)}, u32[]{:S(2)}) copy-start(bf16[128,512]{1,0:T(8,128)(2,1)} %feat_ref.1) | copy-start | bytes 393220
  43.7 45.7 %copy-start.2 = (s32[128,1]{0,1:T(1,128)S(1)}, s32[128,1]{0,1:T(1,128)}, u32[]{:S(2)}) copy-start(s32[128,1]{0,1:T(1,128)} %param.18) | copy-start | bytes 1540
  88.2 2.7 %collective-permute-start.2 = (bf16[16,32,512]{2,1,0:T(8,128)(2,1)S(1)}, bf16[16,32,512]{2,1,0:T(8,128)(2,1)S(1)}, u32[]{:S(2)}, u32[]{:S(2)}) collective-permute-start(bf16[16,32,512]{2,1,0:T(8,128)(2,1)S(1)} %all_to_all.22.half_ref), channel_id=1, source_target_pairs={{0,1},{1,0},{2,3},{3,2},{4,5},{5,4},{6,7},{7,6},{8,9},{9,8},{10,11... | collective-permute-start | bytes 1572872 | tf_op jit(solution)/shard_map/ppermute | solution.py:518

commit v10 on v9

--- a/solution.py
+++ b/solution.py
@@ -37,7 +37,7 @@
 
 
 def place_of(owner, shard):
-    first = jnp.where(shard == 0, 15 - ((owner & 3) * 4 + ((owner >> 2) & 3)), 15 - ((owner >> 4) * 2 + (owner & 1)))
+    first = jnp.where(shard == 0, 15 - ((owner & 3) * 4 + 3 - ((owner >> 2) & 3)), 15 - ((owner >> 4) * 2 + (owner & 1)))
     second = jnp.where(shard == 0, 7 - (owner >> 4), 7 - ((owner >> 1) & 7))
     return first, second
 
@@ -47,7 +47,7 @@
 
     def split(shard):
         if shard == 0:
-            return {(15 - (y * 4 + x), 7 - (z)): (z, x, y) for z, x, y in every}
+            return {(15 - (y * 4 + 3 - x), 7 - (z)): (z, x, y) for z, x, y in every}
         return {(15 - (z * 2 + y % 2), 7 - (x * 2 + y // 2)): (z, x, y) for z, x, y in every}
 
     around, first, second = [], [], []

time: 92.5 us -> 93.2 us (level)
  starting transfers between devices: 22 us -> 23.8 us
    ppermute x1, starting transfers between devices: 1.18 us -> 2.13 us  [local(): theirs = lax.ppermute(mine, 'shard', swap)]
where the time goes in v10:
time: 93.2 us; the launch traced here: 92.7 us
  blocking collectives  43.6 us (47%)
  starting transfers between devices  23.8 us (26%)
  Pallas kernels  11.8 us (13%)
  waiting for transfers between devices  9.18 us (10%)
  local copies, waits for them, and re-layouts  3.5 us (4%)
    all_to_all x3, blocking collectives, exchange(): lax.all_to_all(array, ('dp', 'shard'), split_axis=0, concat_axis=0, axis_...  43.6 us
    all_to_all x1, starting transfers between devices, exchange(): lax.all_to_all(array, ('dp', 'shard'), split_axis=0, concat_axis=0, axis_...  17.6 us
    pallas_call x10, Pallas kernels, call(): pl.pallas_call(body, out_shape=out_shape, in_specs=specs if specs is not...  11.8 us
    all_to_all x1, waiting for transfers between devices, exchange(): lax.all_to_all(array, ('dp', 'shard'), split_axis=0, concat_axis=0, axis_...  8.9 us
    ppermute x1, starting transfers between devices, local(): other = lax.ppermute(own, 'shard', swap)  3.91 us
    unnamed x12, local copies, waits for them, and re-layouts  2.46 us
    ppermute x1, starting transfers between devices, local(): theirs = lax.ppermute(mine, 'shard', swap)  2.13 us
  transfers between devices with their start and end apart: 4, of which 2 were waited for; matrix products, arithmetic and copies ran while one was open for 1% of the time, Pallas kernels for 6%

profile of v10, /device:TPU:1, one launch (start us, length us, event | category | flops | bytes accessed | tf_op | source)
XLA Modules:
  0.0 92.7 jit_solution(15083054526236660535)
XLA Ops:
  0.6 2.4 %shard_map.130 = bf16[128,2,1152]{2,1,0:T(2,128)(2,1)} custom-call(s32[1]{0:T(128)} %bitcast.shard_ref, bf16[128,512]{1,0:T(8,128)(2,1)} %feat_ref.1, f32[1,512]{1,0:T(1,128)} %bitcast.9, bf16[128,512]{1,0:T(8,128)(2,1)} %cot_hbm.1, bf16[3,128]{1,0:T(4,128)(2,1)} %pos_hbm.1, s32[1,128]{1,0:T(1,128)} %bitcast.11, s32[1,128]{1,0:T(1,128)} %bitcast.6), custom_call_target="tpu_custom_call" | custom-call | flops 1000000 | bytes 1000000 | tf_op jit(solution)/shard_map/pallas_call | solution.py:75
  3.0 17.6 %all-to-all-start = ((bf16[128,2,1152]{2,1,0:T(2,128)(2,1)}), bf16[128,2,1152]{2,1,0:T(2,128)(2,1)S(1)}, u32[]{:S(2)}, u32[]{:S(2)}) async-start(bf16[128,2,1152]{2,1,0:T(2,128)(2,1)} %shard_map.130), calls=%async_computation | async-start | bytes 1179648 | tf_op jit(solution)/shard_map/all_to_all | solution.py:63
  20.6 0.8 copy.16.damp_ref
  21.4 0.0 copy-start.3
  21.4 1.0 %copy-done.3 = bf16[512,512]{1,0:T(8,128)(2,1)S(1)} copy-done((bf16[512,512]{1,0:T(8,128)(2,1)S(1)}, bf16[512,512]{1,0:T(8,128)(2,1)}, u32[]{:S(2)}) %copy-start.3) | copy-done | bytes 524312
  22.4 0.0 copy-start.4
  22.4 0.7 copy-done.4
  23.2 0.0 copy-start.5
  23.2 0.7 copy-done.5
  23.8 0.0 copy-start
  23.8 1.0 %shard_map.131 = (bf16[128,1024]{1,0:T(8,128)(2,1)S(1)}, bf16[128,1024]{1,0:T(8,128)(2,1)S(1)}, f32[256,1024]{1,0:T(8,128)S(1)}, bf16[256,512]{1,0:T(8,128)(2,1)S(1)}) custom-call(s32[1]{0:T(128)} %bitcast.shard_ref, s32[3,1024]{1,0:T(4,128)S(1)} %copy-done.4, s32[1,1024]{1,0:T(1,128)S(1)} %bitcast.8, f32[512,1]{1,0:T(8,128)S(1)} %copy.16.damp_ref, ...), custom_call_target="tpu_custom_call" | custom-call | flops 4000000000 | bytes 1000000 | tf_op jit(solution)/shard_map/pallas_call | solution.py:75
  24.8 8.9 %all-to-all-done = bf16[128,2,1152]{2,1,0:T(2,128)(2,1)S(1)} async-done(((bf16[128,2,1152]{2,1,0:T(2,128)(2,1)}), bf16[128,2,1152]{2,1,0:T(2,128)(2,1)S(1)}, u32[]{:S(2)}, u32[]{:S(2)}) %all-to-all-start) | async-done | bytes 589856 | tf_op jit(solution)/shard_map/all_to_all | solution.py:63
  33.7 0.2 reshape.31.own_ref
  33.9 3.9 %collective-permute-start = (bf16[256,1152]{1,0:T(8,128)(2,1)S(1)}, bf16[256,1152]{1,0:T(8,128)(2,1)S(1)}, u32[]{:S(2)}, u32[]{:S(2)}) collective-permute-start(bf16[256,1152]{1,0:T(8,128)(2,1)S(1)} %reshape.31.own_ref), channel_id=1, source_target_pairs={{0,1},{1,0},{2,3},{3,2},{4,5},{5,4},{6,7},{7,6},{8,9},{9,8},{10,11... | collective-permute-start | bytes 1769480 | tf_op jit(solution)/shard_map/ppermute | solution.py:469
  37.8 0.0 copy-done
  37.8 1.9 %shard_map.132 = (bf16[256,2048]{1,0:T(8,128)(2,1)S(1)}, bf16[512,256]{1,0:T(8,128)(2,1)}, f32[512,2048]{1,0:T(8,128)S(1)}) custom-call(s32[1]{0:T(128)} %bitcast.shard_ref, bf16[256,1152]{1,0:T(8,128)(2,1)S(1)} %reshape.31.own_ref, bf16[128,1024]{1,0:T(8,128)(2,1)S(1)} %get-tuple-element.28.kmat_ref, bf16[128,1024]{1,0:T(8,128)(2,1)S(1)} %get-tuple-element.29.kone_ref, ...), custom_call_target="tpu_custom_call" | custom-call | flops 4000000000 | bytes 1000000 | tf_op jit(solution)/shard_map/pallas_call | solution.py:75
  39.7 0.0 collective-permute-done.oth_ref
  39.7 2.3 %shard_map.133 = (bf16[256,2048]{1,0:T(8,128)(2,1)S(1)}, bf16[512,256]{1,0:T(8,128)(2,1)S(1)}, bf16[256,256]{1,0:T(8,128)(2,1)S(1)}, bf16[256,256]{1,0:T(8,128)(2,1)S(1)}) custom-call(s32[1]{0:T(128)} %bitcast.shard_ref, bf16[256,1152]{1,0:T(8,128)(2,1)S(1)} %collective-permute-done.oth_ref, f32[512,2048]{1,0:T(8,128)S(1)} %get-tuple-element.31.part_ref, ...), custom_call_target="tpu_custom_call" | custom-call | flops 1000000 | bytes 1000000 | tf_op jit(solution)/shard_map/pallas_call | solution.py:75
  42.0 0.2 collective-permute-start.1
  42.2 1.5 %shard_map.134.grad_ref = bf16[512,512]{1,0:T(8,128)(2,1)S(1)} custom-call(bf16[256,1152]{1,0:T(8,128)(2,1)S(1)} %reshape.31.own_ref, bf16[256,1152]{1,0:T(8,128)(2,1)S(1)} %collective-permute-done.oth_ref, f32[512,2048]{1,0:T(8,128)S(1)} %get-tuple-element.31.part_ref, bf16[256,2048]{1,0:T(8,128)(2,1)S(1)} %get-tuple-element.32.phase_own_ref, ...), custom_call_target="tpu_custom_call" | custom-call | flops 4000000000 | bytes 1000000 | tf_op jit(solution)/shard_map/pallas_call | solution.py:75
  43.7 0.0 copy-start.1
  43.7 0.0 copy-start.2
  43.7 0.0 collective-permute-done.1.got_ref
  43.7 0.3 shard_map.135
  44.1 16.4 %all_to_all.20.recv_ref = bf16[16,48,512]{2,1,0:T(8,128)(2,1)S(1)} all-to-all(bf16[16,48,512]{2,1,0:T(8,128)(2,1)S(1)} %shard_map.135), channel_id=1, replica_groups={{230,238,246,254,228,236,244,252,226,234,242,250,224,232,240,248},{198,..., dimensions={0} | all-to-all | bytes 1572864 | tf_op jit(solution)/shard_map/all_to_all | solution.py:63
  60.5 0.2 shard_map.136
  60.7 12.2 %all_to_all.21.recv_ref = bf16[8,64,512]{2,1,0:T(8,128)(2,1)S(1)} all-to-all(bf16[8,64,512]{2,1,0:T(8,128)(2,1)S(1)} %shard_map.136), channel_id=1, replica_groups={{230,198,166,134,102,70,38,6},{238,206,174,142,110,78,46,14},{246,214,1..., dimensions={0} | all-to-all | bytes 1048576 | tf_op jit(solution)/shard_map/all_to_all | solution.py:63
  72.9 0.1 shard_map.137
  73.0 15.0 %all_to_all.22.half_ref = bf16[16,32,512]{2,1,0:T(8,128)(2,1)S(1)} all-to-all(bf16[16,32,512]{2,1,0:T(8,128)(2,1)S(1)} %shard_map.137), channel_id=1, replica_groups={{230,238,246,254,228,236,244,252,226,234,242,250,224,232,240,248},{198,..., dimensions={0} | all-to-all | bytes 1048576 | tf_op jit(solution)/shard_map/all_to_all | solution.py:63
  88.0 2.1 %collective-permute-start.2 = (bf16[16,32,512]{2,1,0:T(8,128)(2,1)S(1)}, bf16[16,32,512]{2,1,0:T(8,128)(2,1)S(1)}, u32[]{:S(2)}, u32[]{:S(2)}) collective-permute-start(bf16[16,32,512]{2,1,0:T(8,128)(2,1)S(1)} %all_to_all.22.half_ref), channel_id=1, source_target_pairs={{0,1},{1,0},{2,3},{3,2},{4,5},{5,4},{6,7},{7,6},{8,9},{9,8},{10,11... | collective-permute-start | bytes 1572872 | tf_op jit(solution)/shard_map/ppermute | solution.py:518
  90.1 0.0 copy-done.1
  90.1 0.0 copy-done.2
  90.1 1.2 %shard_map.138 = (bf16[128,512]{1,0:T(8,128)(2,1)}, f32[512,512]{1,0:T(8,128)}, f32[512,512]{1,0:T(8,128)}) custom-call(s32[1]{0:T(128)} %bitcast.shard_ref, bf16[128,512]{1,0:T(8,128)(2,1)S(1)} %copy-done.1, bf16[8,64,512]{2,1,0:T(8,128)(2,1)S(1)} %all_to_all.21.recv_ref, s32[1,128]{1,0:T(1,128)S(1)} %bitcast.7, bf16[16,32,512]{2,1,0:T(8,128)(2,1)S(1)} %all_to_all.22.half_ref), custom_call_target="tpu_custom_call" | custom-call | flops 4000000000 | bytes 1000000 | tf_op jit(solution)/shard_map/pallas_call | solution.py:75
  91.4 0.3 collective-permute-done.2.half_ref
  91.7 1.0 %shard_map.139 = (f32[512,512]{1,0:T(8,128)}, f32[512,512]{1,0:T(8,128)}) custom-call(s32[1]{0:T(128)} %bitcast.shard_ref, bf16[16,32,512]{2,1,0:T(8,128)(2,1)S(1)} %collective-permute-done.2.half_ref, f32[512,512]{1,0:T(8,128)} %get-tuple-element.39._grad_in, f32[512,512]{1,0:T(8,128)} %get-tuple-element.40._grad_out), custom_call_target="tpu_custom_call", output_to_operand_aliasing={{0}: (2, {}), {1}: (3, {})} | custom-call | flops 1000000 | bytes 1000000 | tf_op jit(solution)/shard_map/pallas_call | solution.py:75
Async XLA Ops:
  3.0 30.7 %all-to-all-start = ((bf16[128,2,1152]{2,1,0:T(2,128)(2,1)}), bf16[128,2,1152]{2,1,0:T(2,128)(2,1)S(1)}, u32[]{:S(2)}, u32[]{:S(2)}) async-start(bf16[128,2,1152]{2,1,0:T(2,128)(2,1)} %shard_map.130), calls=%async_computation | async-start | bytes 1179648 | tf_op jit(solution)/shard_map/all_to_all | solution.py:63
  21.4 1.0 %copy-start.3 = (bf16[512,512]{1,0:T(8,128)(2,1)S(1)}, bf16[512,512]{1,0:T(8,128)(2,1)}, u32[]{:S(2)}) copy-start(bf16[512,512]{1,0:T(8,128)(2,1)} %w_in_ref.1) | copy-start | bytes 1572868
  22.4 0.7 copy-start.4
  23.2 0.7 copy-start.5
  23.8 14.0 %copy-start = (bf16[512,512]{1,0:T(8,128)(2,1)S(1)}, bf16[512,512]{1,0:T(8,128)(2,1)}, u32[]{:S(2)}) copy-start(bf16[512,512]{1,0:T(8,128)(2,1)} %w_out_ref.5) | copy-start | bytes 1572868
  33.9 5.8 %collective-permute-start = (bf16[256,1152]{1,0:T(8,128)(2,1)S(1)}, bf16[256,1152]{1,0:T(8,128)(2,1)S(1)}, u32[]{:S(2)}, u32[]{:S(2)}) collective-permute-start(bf16[256,1152]{1,0:T(8,128)(2,1)S(1)} %reshape.31.own_ref), channel_id=1, source_target_pairs={{0,1},{1,0},{2,3},{3,2},{4,5},{5,4},{6,7},{7,6},{8,9},{9,8},{10,11... | collective-permute-start | bytes 1769480 | tf_op jit(solution)/shard_map/ppermute | solution.py:469
  42.0 1.7 %collective-permute-start.1 = (bf16[256,256]{1,0:T(8,128)(2,1)S(1)}, bf16[256,256]{1,0:T(8,128)(2,1)S(1)}, u32[]{:S(2)}, u32[]{:S(2)}) collective-permute-start(bf16[256,256]{1,0:T(8,128)(2,1)S(1)} %get-tuple-element.35.msg_oth_ref), channel_id=1, source_target_pairs={{0,1},{1,0},{2,3},{3,2},{4,5},{5,4},{6,7},{7,6},{8,9},{9,8},{10,11... | collective-permute-start | bytes 393224 | tf_op jit(solution)/shard_map/ppermute | solution.py:490
  43.7 46.4 %copy-start.1 = (bf16[128,512]{1,0:T(8,128)(2,1)S(1)}, bf16[128,512]{1,0:T(8,128)(2,1)}, u32[]{:S(2)}) copy-start(bf16[128,512]{1,0:T(8,128)(2,1)} %feat_ref.1) | copy-start | bytes 393220
  43.7 46.4 %copy-start.2 = (s32[128,1]{0,1:T(1,128)S(1)}, s32[128,1]{0,1:T(1,128)}, u32[]{:S(2)}) copy-start(s32[128,1]{0,1:T(1,128)} %param.18) | copy-start | bytes 1540
  88.0 3.7 %collective-permute-start.2 = (bf16[16,32,512]{2,1,0:T(8,128)(2,1)S(1)}, bf16[16,32,512]{2,1,0:T(8,128)(2,1)S(1)}, u32[]{:S(2)}, u32[]{:S(2)}) collective-permute-start(bf16[16,32,512]{2,1,0:T(8,128)(2,1)S(1)} %all_to_all.22.half_ref), channel_id=1, source_target_pairs={{0,1},{1,0},{2,3},{3,2},{4,5},{5,4},{6,7},{7,6},{8,9},{9,8},{10,11... | collective-permute-start | bytes 1572872 | tf_op jit(solution)/shard_map/ppermute | solution.py:518
